TPU v7x, 128 devices: a whole 4x4x4 slice. The times are simulated.
128 devices in a mesh: inner: 8 (over y_lo, x), outer: 16 (over y_hi, z, core).
Axes of the slice: x: 4, y: 4 (y_hi: 2, y_lo: 2; y = y_hi * 2 + y_lo), z: 4, core: 2. Of those that a mesh axis runs over, the one named last changes fastest.
Arguments:
- queries: bfloat16 [16384, 8192], P(('inner', 'outer')), may hold values from -6 to 6
- keys: bfloat16 [16384, 1024], P(('inner', 'outer')), may hold values from -6 to 6
- values: bfloat16 [16384, 1024], P(('inner', 'outer')), may hold values from -6 to 6
- grad_out: bfloat16 [16384, 8192], P(('inner', 'outer')), may hold values from -6 to 6
- doc_ids: int32 [16384], replicated, may hold values from 0 to 31, never falling along the last dimension, each value on 1 to 1024 neighbouring positions
Outputs:
- grad_queries: bfloat16 [16384, 8192], P(('inner', 'outer'))
- grad_keys: bfloat16 [16384, 1024], P(('inner', 'outer'))
- grad_values: bfloat16 [16384, 1024], P(('inner', 'outer'))
Inputs may be any that keep to these rules, and one draw needn't show every extreme that they name: `doc_ids`: document numbers never fall along the sequence; each document has 1 to 1024 tokens and one has exactly 1024.
All inputs are finite; a program needn't handle non-finite values.
Results may differ from a plain program's by a relative error of at most 0.011.
The roundings to bfloat16 on the way count: a program that leaves them out, or rounds other values in their place, can miss the bound.
Values may be sent and summed in bfloat16 or wider, within the bound.
No kernel may reach another device: no remote copies, remote signals or barrier semaphores. Data moves between devices by JAX's collectives and lax.ppermute only.
A program may use at most 64 MiB of HBM per device.

v0:
```python
import jax
import jax.numpy as jnp
from jax import lax
from jax.sharding import PartitionSpec as P

KVH = 8
HD = 128
G = 8
WINDOW = 384


def from_behind(value, axis, steps):
    count = lax.axis_size(axis)
    first, last = (max(0, -steps), min(count, count - steps))
    return lax.ppermute(value, axis, [(source, source + steps) for source in range(first, last)])


def as_sent(value):

    def short(part):
        return part.astype(jnp.bfloat16) if part.dtype == jnp.float32 else part

    return jax.tree.map(short, value)


def block_grads(
    query_rows, dout_rows, key_rows, value_rows, query_pos, key_pos, query_doc, key_doc
):
    count = query_rows.shape[0]
    scale = 1.0 / HD**0.5
    gap = query_pos[:, None] - key_pos[None, :]
    visible = (
        (gap >= 0)
        & (gap < WINDOW)
        & (key_pos[None, :] >= 0)
        & (query_doc[:, None] == key_doc[None, :])
    )
    dq_parts = []
    dk_parts = []
    dv_parts = []
    for group in range(KVH):
        qh = query_rows[:, group * G * HD : (group + 1) * G * HD].reshape(count, G, HD)
        dh = dout_rows[:, group * G * HD : (group + 1) * G * HD].reshape(count, G, HD)
        kh = key_rows[:, group * HD : (group + 1) * HD]
        vh = value_rows[:, group * HD : (group + 1) * HD]
        scores = jnp.einsum("rgd,kd->grk", qh, kh, preferred_element_type=jnp.float32) * scale
        masked = jnp.where(visible[None], scores, -jnp.inf)
        top = jnp.max(masked, axis=-1, keepdims=True)
        total = jnp.sum(
            jnp.where(visible[None], jnp.exp(scores - top), 0.0), axis=-1, keepdims=True
        )
        lse = top + jnp.log(total)
        probs = jnp.where(visible[None], jnp.exp(scores - lse), 0.0)
        probs_b = probs.astype(jnp.bfloat16)
        attn_out = jnp.einsum(
            "grk,kd->rgd", probs_b, vh, preferred_element_type=jnp.float32
        ).astype(jnp.bfloat16)
        attn_out = lax.optimization_barrier(attn_out)
        delta = jnp.sum(dh.astype(jnp.float32) * attn_out.astype(jnp.float32), axis=-1)
        dprobs = jnp.einsum("rgd,kd->grk", dh, vh, preferred_element_type=jnp.float32)
        dscores = (probs * (dprobs - jnp.transpose(delta)[:, :, None])).astype(jnp.bfloat16)
        dq_parts.append(
            (
                jnp.einsum("grk,kd->rgd", dscores, kh, preferred_element_type=jnp.float32) * scale
            ).reshape(count, G * HD)
        )
        dk_parts.append(
            jnp.einsum("grk,rgd->kd", dscores, qh, preferred_element_type=jnp.float32) * scale
        )
        dv_parts.append(jnp.einsum("grk,rgd->kd", probs_b, dh, preferred_element_type=jnp.float32))
    return (
        jnp.concatenate(dq_parts, axis=1).astype(jnp.bfloat16),
        jnp.concatenate(dk_parts, axis=1),
        jnp.concatenate(dv_parts, axis=1),
    )


def per_device(queries, keys, values, grad_out, doc_ids):
    rows = queries.shape[0]
    margin = 3 * rows
    index = lax.axis_index(("inner", "outer"))
    start = index * rows
    received = []
    current = (keys, values)
    for step in range(3):
        current = from_behind((current[0], current[1]), ("inner", "outer"), 1)
        received.append(current)
    earlier = received[::-1]
    key_rows = jnp.concatenate([piece[0] for piece in earlier] + [keys], axis=0)
    value_rows = jnp.concatenate([piece[1] for piece in earlier] + [values], axis=0)
    query_pos = start + jnp.arange(rows, dtype=jnp.int32)
    key_pos = start - margin + jnp.arange(4 * rows, dtype=jnp.int32)
    doc_pad = jnp.concatenate([jnp.full((margin,), -1, jnp.int32), doc_ids], axis=0)
    query_doc = lax.dynamic_slice_in_dim(doc_ids, start, rows, 0)
    key_doc = lax.dynamic_slice_in_dim(doc_pad, start, 4 * rows, 0)
    grad_queries, dk_part, dv_part = block_grads(
        queries, grad_out, key_rows, value_rows, query_pos, key_pos, query_doc, key_doc
    )
    running = (dk_part[0:rows], dv_part[0:rows])
    for step in range(1, 4):
        passed = from_behind((as_sent(running[0]), as_sent(running[1])), ("inner", "outer"), -1)
        running = (
            passed[0] + dk_part[step * rows : (step + 1) * rows],
            passed[1] + dv_part[step * rows : (step + 1) * rows],
        )
    key_total, value_total = running
    return (grad_queries, key_total.astype(jnp.bfloat16), value_total.astype(jnp.bfloat16))


def solution(mesh):
    return jax.shard_map(
        per_device,
        mesh=mesh,
        in_specs=(
            P(("inner", "outer"), None),
            P(("inner", "outer"), None),
            P(("inner", "outer"), None),
            P(("inner", "outer"), None),
            P(),
        ),
        out_specs=(
            P(("inner", "outer"), None),
            P(("inner", "outer"), None),
            P(("inner", "outer"), None),
        ),
        check_vma=False,
    )
```

profile of v0, /device:TPU:121, one launch (start us, length us, event | category | flops | bytes accessed | tf_op | source)
XLA Modules:
  0.0 124.9 jit_solution(676119034477917681)
XLA Ops:
  0.6 3.0 %collective-permute-start = (bf16[128,1024]{1,0:T(8,128)(2,1)}, bf16[128,1024]{1,0:T(8,128)(2,1)S(1)}, u32[]{:S(2)}, u32[]{:S(2)}) collective-permute-start(bf16[128,1024]{1,0:T(8,128)(2,1)} %param.6), channel_id=1, source_target_pairs={{0,1},{1,2},{2,3},{3,4},{4,5},{5,6},{6,7},{7,8},{8,9},{9,10},{10,1... | collective-permute-start | bytes 786440 | tf_op jit(solution)/shard_map/ppermute | solution.py:15
  3.6 1.9 %collective-permute-start.3 = (bf16[128,1024]{1,0:T(8,128)(2,1)}, bf16[128,1024]{1,0:T(8,128)(2,1)}, u32[]{:S(2)}, u32[]{:S(2)}) collective-permute-start(bf16[128,1024]{1,0:T(8,128)(2,1)} %param.7), channel_id=1, source_target_pairs={{0,1},{1,2},{2,3},{3,4},{4,5},{5,6},{6,7},{7,8},{8,9},{9,10},{10,1... | collective-permute-start | bytes 786440 | tf_op jit(solution)/shard_map/ppermute | solution.py:15
  6.4 1.9 %fusion.146 = (bf16[128,1024]{1,0:T(8,128)(2,1)S(1)}, bf16[128,1024]{1,0:T(8,128)(2,1)S(1)}, bf16[128,1024]{1,0:T(8,128)(2,1)S(1)}, bf16[128,1024]{1,0:T(8,128)(...) fusion(bf16[128,8192]{1,0:T(8,128)(2,1)} %param.5), kind=kLoop, calls=%fused_computation.256 | loop fusion | bytes 4194304 | tf_op jit(solution)/shard_map/slice | solution.py:42
  8.3 7.7 %collective-permute-start.1 = (bf16[128,1024]{1,0:T(8,128)(2,1)S(1)}, bf16[128,1024]{1,0:T(8,128)(2,1)}, u32[]{:S(2)}, u32[]{:S(2)}) collective-permute-start(bf16[128,1024]{1,0:T(8,128)(2,1)S(1)} %collective-permute-done), channel_id=1, source_target_pairs={{0,1},{1,2},{2,3},{3,4},{4,5},{5,6},{6,7},{7,8},{8,9},{9,10},{10,1... | collective-permute-start | bytes 786440 | tf_op jit(solution)/shard_map/ppermute | solution.py:15
  16.0 1.1 fusion.145
  17.1 1.9 %collective-permute-start.4 = (bf16[128,1024]{1,0:T(8,128)(2,1)}, bf16[128,1024]{1,0:T(8,128)(2,1)}, u32[]{:S(2)}, u32[]{:S(2)}) collective-permute-start(bf16[128,1024]{1,0:T(8,128)(2,1)} %collective-permute-done.3), channel_id=1, source_target_pairs={{0,1},{1,2},{2,3},{3,4},{4,5},{5,6},{6,7},{7,8},{8,9},{9,10},{10,1... | collective-permute-start | bytes 786440 | tf_op jit(solution)/shard_map/ppermute | solution.py:15
  19.3 9.0 %collective-permute-start.2 = (bf16[128,1024]{1,0:T(8,128)(2,1)}, bf16[128,1024]{1,0:T(8,128)(2,1)}, u32[]{:S(2)}, u32[]{:S(2)}) collective-permute-start(bf16[128,1024]{1,0:T(8,128)(2,1)} %collective-permute-done.1), channel_id=1, source_target_pairs={{0,1},{1,2},{2,3},{3,4},{4,5},{5,6},{6,7},{7,8},{8,9},{9,10},{10,1... | collective-permute-start | bytes 786440 | tf_op jit(solution)/shard_map/ppermute | solution.py:15
  31.2 1.8 %copy.261 = bf16[128,1024]{0,1:T(8,128)(2,1)} copy(bf16[128,1024]{1,0:T(8,128)(2,1)} %get-tuple-element.32) | data formatting | bytes 524288
  33.0 1.8 %copy.263 = bf16[128,1024]{0,1:T(8,128)(2,1)} copy(bf16[128,1024]{1,0:T(8,128)(2,1)} %get-tuple-element.31) | data formatting | bytes 524288
  34.8 1.8 %copy.265 = bf16[128,1024]{0,1:T(8,128)(2,1)} copy(bf16[128,1024]{1,0:T(8,128)(2,1)} %get-tuple-element.30) | data formatting | bytes 524288
  39.1 1.9 %collective-permute-start.5 = (bf16[128,1024]{1,0:T(8,128)(2,1)}, bf16[128,1024]{1,0:T(8,128)(2,1)S(1)}, u32[]{:S(2)}, u32[]{:S(2)}) collective-permute-start(bf16[128,1024]{1,0:T(8,128)(2,1)} %collective-permute-done.4), channel_id=1, source_target_pairs={{0,1},{1,2},{2,3},{3,4},{4,5},{5,6},{6,7},{7,8},{8,9},{9,10},{10,1... | collective-permute-start | bytes 786440 | tf_op jit(solution)/shard_map/ppermute | solution.py:15
  48.4 2.4 %fusion.5 = (f32[8,128]{1,0:T(8,128)S(1)}, f32[8,128]{1,0:T(8,128)S(1)}, f32[8,128]{1,0:T(8,128)S(1)}, f32[8,128]{1,0:T(8,128)S(1)}, f32[8,128]{1,0:T(8,128)S(1)...) fusion(f32[512,128,8]{1,0,2:T(8,128)S(1)} %get-tuple-element.41, ...), kind=kOutput, calls=%fused_computation.9 | convolution fusion | flops 147841024 | bytes 17276928 | tf_op jit(solution)/shard_map/rgd,kd->grk/dot_general | solution.py:46
  55.4 1.0 fusion.72
  56.4 2.8 %fusion.13 = (f32[8,128]{1,0:T(8,128)S(1)}, f32[8,128]{1,0:T(8,128)S(1)}, f32[8,128]{1,0:T(8,128)S(1)}, f32[8,128]{1,0:T(8,128)S(1)}, f32[8,128]{1,0:T(8,128)S(1)}, /*index=5*/f32[8,128]{1,0:T(8,128)S(1)}) fusion(f32[512,128,8]{1,0,2:T(8,128)S(1)} %fusion.127, f32[8,128]{1,0:T(8,128)S(1)} %get-tuple-element.16, pred[128,512]{0,1:T(8,128)(4,1)S(1)} %fusion.120, ...), kind=kLoop, calls=%fused_computation.21 | loop fusion | flops 12576768 | bytes 12697600 | tf_op jit(solution)/shard_map/reduce_sum | solution.py:49
  68.9 2.6 %collective-permute-start.9 = (bf16[128,1024]{0,1:T(8,128)(2,1)}, bf16[128,1024]{0,1:T(8,128)(2,1)}, u32[]{:S(2)}, u32[]{:S(2)}) collective-permute-start(bf16[128,1024]{0,1:T(8,128)(2,1)} %slice.254), channel_id=1, source_target_pairs={{1,0},{2,1},{3,2},{4,3},{5,4},{6,5},{7,6},{8,7},{9,8},{10,9},{11,1... | collective-permute-start | bytes 786440 | tf_op jit(solution)/shard_map/ppermute | solution.py:15
  82.9 1.3 %copy-done.1 = f32[512,1024]{0,1:T(8,128)} copy-done((f32[512,1024]{0,1:T(8,128)}, f32[512,1024]{0,1:T(8,128)S(1)}, u32[]{:S(2)}) %copy-start.1) | copy-done | bytes 2097176
  84.9 1.9 %collective-permute-start.6 = (bf16[128,1024]{0,1:T(8,128)(2,1)}, bf16[128,1024]{0,1:T(8,128)(2,1)}, u32[]{:S(2)}, u32[]{:S(2)}) collective-permute-start(bf16[128,1024]{0,1:T(8,128)(2,1)} %slice.255), channel_id=1, source_target_pairs={{1,0},{2,1},{3,2},{4,3},{5,4},{6,5},{7,6},{8,7},{9,8},{10,9},{11,1... | collective-permute-start | bytes 786440 | tf_op jit(solution)/shard_map/ppermute | solution.py:15
  87.6 1.3 %copy-done.14 = bf16[128,8192]{1,0:T(8,128)(2,1)} copy-done((bf16[128,8192]{1,0:T(8,128)(2,1)}, bf16[128,8192]{1,0:T(8,128)(2,1)S(1)}, u32[]{:S(2)}) %copy-start.14) | copy-done | bytes 2097176
  90.8 1.2 fusion.114
  92.0 1.9 %collective-permute-start.10 = (bf16[128,1024]{0,1:T(8,128)(2,1)S(1)}, bf16[128,1024]{0,1:T(8,128)(2,1)S(1)}, u32[]{:S(2)}, u32[]{:S(2)}) collective-permute-start(bf16[128,1024]{0,1:T(8,128)(2,1)S(1)} %fusion.114), channel_id=1, source_target_pairs={{1,0},{2,1},{3,2},{4,3},{5,4},{6,5},{7,6},{8,7},{9,8},{10,9},{11,1... | collective-permute-start | bytes 786440 | tf_op jit(solution)/shard_map/ppermute | solution.py:15
  93.9 3.5 %collective-permute-done.6 = bf16[128,1024]{0,1:T(8,128)(2,1)} collective-permute-done((bf16[128,1024]{0,1:T(8,128)(2,1)}, bf16[128,1024]{0,1:T(8,128)(2,1)}, u32[]{:S(2)}, u32[]{:S(2)}) %collective-permute-start.6) | collective-permute-done | bytes 262176 | tf_op jit(solution)/shard_map/ppermute | solution.py:15
  97.4 1.0 fusion.117
  98.5 1.9 %collective-permute-start.7 = (bf16[128,1024]{0,1:T(8,128)(2,1)S(1)}, bf16[128,1024]{0,1:T(8,128)(2,1)}, u32[]{:S(2)}, u32[]{:S(2)}) collective-permute-start(bf16[128,1024]{0,1:T(8,128)(2,1)S(1)} %fusion.117), channel_id=1, source_target_pairs={{1,0},{2,1},{3,2},{4,3},{5,4},{6,5},{7,6},{8,7},{9,8},{10,9},{11,1... | collective-permute-start | bytes 786440 | tf_op jit(solution)/shard_map/ppermute | solution.py:15
  101.3 2.9 %collective-permute-done.10 = bf16[128,1024]{0,1:T(8,128)(2,1)S(1)} collective-permute-done((bf16[128,1024]{0,1:T(8,128)(2,1)S(1)}, bf16[128,1024]{0,1:T(8,128)(2,1)S(1)}, u32[]{:S(2)}, u32[]{:S(2)}) %collective-permute-start.10) | collective-permute-done | bytes 262176 | tf_op jit(solution)/shard_map/ppermute | solution.py:15
  104.2 1.1 fusion.113
  105.3 1.9 %collective-permute-start.11 = (bf16[128,1024]{0,1:T(8,128)(2,1)S(1)}, bf16[128,1024]{0,1:T(8,128)(2,1)S(1)}, u32[]{:S(2)}, u32[]{:S(2)}) collective-permute-start(bf16[128,1024]{0,1:T(8,128)(2,1)S(1)} %fusion.113), channel_id=1, source_target_pairs={{1,0},{2,1},{3,2},{4,3},{5,4},{6,5},{7,6},{8,7},{9,8},{10,9},{11,1... | collective-permute-start | bytes 786440 | tf_op jit(solution)/shard_map/ppermute | solution.py:15
  107.2 3.6 %collective-permute-done.7 = bf16[128,1024]{0,1:T(8,128)(2,1)} collective-permute-done((bf16[128,1024]{0,1:T(8,128)(2,1)S(1)}, bf16[128,1024]{0,1:T(8,128)(2,1)}, u32[]{:S(2)}, u32[]{:S(2)}) %collective-permute-start.7) | collective-permute-done | bytes 262176 | tf_op jit(solution)/shard_map/ppermute | solution.py:15
  110.8 1.0 fusion.116
  111.8 1.9 %collective-permute-start.8 = (bf16[128,1024]{0,1:T(8,128)(2,1)S(1)}, bf16[128,1024]{0,1:T(8,128)(2,1)S(1)}, u32[]{:S(2)}, u32[]{:S(2)}) collective-permute-start(bf16[128,1024]{0,1:T(8,128)(2,1)S(1)} %fusion.116), channel_id=1, source_target_pairs={{1,0},{2,1},{3,2},{4,3},{5,4},{6,5},{7,6},{8,7},{9,8},{10,9},{11,1... | collective-permute-start | bytes 786440 | tf_op jit(solution)/shard_map/ppermute | solution.py:15
  114.4 3.0 %collective-permute-done.11 = bf16[128,1024]{0,1:T(8,128)(2,1)S(1)} collective-permute-done((bf16[128,1024]{0,1:T(8,128)(2,1)S(1)}, bf16[128,1024]{0,1:T(8,128)(2,1)S(1)}, u32[]{:S(2)}, u32[]{:S(2)}) %collective-permute-start.11) | collective-permute-done | bytes 262176 | tf_op jit(solution)/shard_map/ppermute | solution.py:15
  117.5 1.1 fusion.112
  119.4 4.6 %collective-permute-done.8 = bf16[128,1024]{0,1:T(8,128)(2,1)S(1)} collective-permute-done((bf16[128,1024]{0,1:T(8,128)(2,1)S(1)}, bf16[128,1024]{0,1:T(8,128)(2,1)S(1)}, u32[]{:S(2)}, u32[]{:S(2)}) %collective-permute-start.8) | collective-permute-done | bytes 262176 | tf_op jit(solution)/shard_map/ppermute | solution.py:15
  (144 shorter events, 45.4 us)
Async XLA Ops:
  0.6 7.7 %collective-permute-start = (bf16[128,1024]{1,0:T(8,128)(2,1)}, bf16[128,1024]{1,0:T(8,128)(2,1)S(1)}, u32[]{:S(2)}, u32[]{:S(2)}) collective-permute-start(bf16[128,1024]{1,0:T(8,128)(2,1)} %param.6), channel_id=1, source_target_pairs={{0,1},{1,2},{2,3},{3,4},{4,5},{5,6},{6,7},{7,8},{8,9},{9,10},{10,1... | collective-permute-start | bytes 786440 | tf_op jit(solution)/shard_map/ppermute | solution.py:15
  3.6 13.5 %collective-permute-start.3 = (bf16[128,1024]{1,0:T(8,128)(2,1)}, bf16[128,1024]{1,0:T(8,128)(2,1)}, u32[]{:S(2)}, u32[]{:S(2)}) collective-permute-start(bf16[128,1024]{1,0:T(8,128)(2,1)} %param.7), channel_id=1, source_target_pairs={{0,1},{1,2},{2,3},{3,4},{4,5},{5,6},{6,7},{7,8},{8,9},{9,10},{10,1... | collective-permute-start | bytes 786440 | tf_op jit(solution)/shard_map/ppermute | solution.py:15
  6.4 9.7 %copy-start = (bf16[128,8192]{1,0:T(8,128)(2,1)S(1)}, bf16[128,8192]{1,0:T(8,128)(2,1)}, u32[]{:S(2)}) copy-start(bf16[128,8192]{1,0:T(8,128)(2,1)} %param.8) | copy-start | bytes 6291460
  8.3 20.0 %copy-start.13 = (bf16[128,1024]{1,0:T(8,128)(2,1)}, bf16[128,1024]{1,0:T(8,128)(2,1)S(1)}, u32[]{:S(2)}) copy-start(bf16[128,1024]{1,0:T(8,128)(2,1)S(1)} %collective-permute-done) | copy-start | bytes 786436
  8.3 11.0 %collective-permute-start.1 = (bf16[128,1024]{1,0:T(8,128)(2,1)S(1)}, bf16[128,1024]{1,0:T(8,128)(2,1)}, u32[]{:S(2)}, u32[]{:S(2)}) collective-permute-start(bf16[128,1024]{1,0:T(8,128)(2,1)S(1)} %collective-permute-done), channel_id=1, source_target_pairs={{0,1},{1,2},{2,3},{3,4},{4,5},{5,6},{6,7},{7,8},{8,9},{9,10},{10,1... | collective-permute-start | bytes 786440 | tf_op jit(solution)/shard_map/ppermute | solution.py:15
  17.1 22.0 %collective-permute-start.4 = (bf16[128,1024]{1,0:T(8,128)(2,1)}, bf16[128,1024]{1,0:T(8,128)(2,1)}, u32[]{:S(2)}, u32[]{:S(2)}) collective-permute-start(bf16[128,1024]{1,0:T(8,128)(2,1)} %collective-permute-done.3), channel_id=1, source_target_pairs={{0,1},{1,2},{2,3},{3,4},{4,5},{5,6},{6,7},{7,8},{8,9},{9,10},{10,1... | collective-permute-start | bytes 786440 | tf_op jit(solution)/shard_map/ppermute | solution.py:15
  19.3 21.7 %collective-permute-start.2 = (bf16[128,1024]{1,0:T(8,128)(2,1)}, bf16[128,1024]{1,0:T(8,128)(2,1)}, u32[]{:S(2)}, u32[]{:S(2)}) collective-permute-start(bf16[128,1024]{1,0:T(8,128)(2,1)} %collective-permute-done.1), channel_id=1, source_target_pairs={{0,1},{1,2},{2,3},{3,4},{4,5},{5,6},{6,7},{7,8},{8,9},{9,10},{10,1... | collective-permute-start | bytes 786440 | tf_op jit(solution)/shard_map/ppermute | solution.py:15
  30.4 6.3 %copy-start.4 = (bf16[128,1024]{1,0:T(8,128)(2,1)S(1)}, bf16[128,1024]{1,0:T(8,128)(2,1)}, u32[]{:S(2)}) copy-start(bf16[128,1024]{1,0:T(8,128)(2,1)} %get-tuple-element.29) | copy-start | bytes 786436
  39.1 11.8 %collective-permute-start.5 = (bf16[128,1024]{1,0:T(8,128)(2,1)}, bf16[128,1024]{1,0:T(8,128)(2,1)S(1)}, u32[]{:S(2)}, u32[]{:S(2)}) collective-permute-start(bf16[128,1024]{1,0:T(8,128)(2,1)} %collective-permute-done.4), channel_id=1, source_target_pairs={{0,1},{1,2},{2,3},{3,4},{4,5},{5,6},{6,7},{7,8},{8,9},{9,10},{10,1... | collective-permute-start | bytes 786440 | tf_op jit(solution)/shard_map/ppermute | solution.py:15
  47.5 1.0 copy-start.10
  48.4 4.5 %copy-start.12 = (bf16[128,1024]{1,0:T(8,128)(2,1)S(1)}, bf16[128,1024]{1,0:T(8,128)(2,1)}, u32[]{:S(2)}) copy-start(bf16[128,1024]{1,0:T(8,128)(2,1)} %param.7) | copy-start | bytes 786436
  50.9 2.1 %copy-start.9 = (bf16[128,1024]{0,1:T(8,128)(2,1)S(1)}, bf16[128,1024]{0,1:T(8,128)(2,1)}, u32[]{:S(2)}) copy-start(bf16[128,1024]{0,1:T(8,128)(2,1)} %copy.261) | copy-start | bytes 786436
  62.7 1.0 copy-start.8
  63.3 1.0 copy-start.7
  64.2 1.0 copy-start.6
  64.8 1.0 copy-start.5
  68.1 5.9 %copy-start.3 = (f32[512,1024]{0,1:T(8,128)}, f32[512,1024]{0,1:T(8,128)S(1)}, u32[]{:S(2)}) copy-start(f32[512,1024]{0,1:T(8,128)S(1)} %fusion.88) | copy-start | bytes 6291460
  68.9 21.9 %collective-permute-start.9 = (bf16[128,1024]{0,1:T(8,128)(2,1)}, bf16[128,1024]{0,1:T(8,128)(2,1)}, u32[]{:S(2)}, u32[]{:S(2)}) collective-permute-start(bf16[128,1024]{0,1:T(8,128)(2,1)} %slice.254), channel_id=1, source_target_pairs={{1,0},{2,1},{3,2},{4,3},{5,4},{6,5},{7,6},{8,7},{9,8},{10,9},{11,1... | collective-permute-start | bytes 786440 | tf_op jit(solution)/shard_map/ppermute | solution.py:15
  82.3 4.9 %copy-start.11 = (bf16[128,8,128]{2,0,1:T(8,128)(2,1)S(1)}, bf16[128,8,128]{2,0,1:T(8,128)(2,1)}, u32[]{:S(2)}) copy-start(bf16[128,8,128]{2,0,1:T(8,128)(2,1)} %fusion.72) | copy-start | bytes 786436
  82.8 1.3 %copy-start.1 = (f32[512,1024]{0,1:T(8,128)}, f32[512,1024]{0,1:T(8,128)S(1)}, u32[]{:S(2)}) copy-start(f32[512,1024]{0,1:T(8,128)S(1)} %fusion.97) | copy-start | bytes 6291460
  84.9 12.5 %collective-permute-start.6 = (bf16[128,1024]{0,1:T(8,128)(2,1)}, bf16[128,1024]{0,1:T(8,128)(2,1)}, u32[]{:S(2)}, u32[]{:S(2)}) collective-permute-start(bf16[128,1024]{0,1:T(8,128)(2,1)} %slice.255), channel_id=1, source_target_pairs={{1,0},{2,1},{3,2},{4,3},{5,4},{6,5},{7,6},{8,7},{9,8},{10,9},{11,1... | collective-permute-start | bytes 786440 | tf_op jit(solution)/shard_map/ppermute | solution.py:15
  87.5 9.9 %copy-start.2 = (f32[512,1024]{0,1:T(8,128)S(1)}, f32[512,1024]{0,1:T(8,128)}, u32[]{:S(2)}) copy-start(f32[512,1024]{0,1:T(8,128)} %copy-done.1) | copy-start | bytes 6291460
  87.6 1.3 %copy-start.14 = (bf16[128,8192]{1,0:T(8,128)(2,1)}, bf16[128,8192]{1,0:T(8,128)(2,1)S(1)}, u32[]{:S(2)}) copy-start(bf16[128,8192]{1,0:T(8,128)(2,1)S(1)} %constant_dynamic-update-slice_fusion.12) | copy-start | bytes 6291460
  92.0 12.2 %collective-permute-start.10 = (bf16[128,1024]{0,1:T(8,128)(2,1)S(1)}, bf16[128,1024]{0,1:T(8,128)(2,1)S(1)}, u32[]{:S(2)}, u32[]{:S(2)}) collective-permute-start(bf16[128,1024]{0,1:T(8,128)(2,1)S(1)} %fusion.114), channel_id=1, source_target_pairs={{1,0},{2,1},{3,2},{4,3},{5,4},{6,5},{7,6},{8,7},{9,8},{10,9},{11,1... | collective-permute-start | bytes 786440 | tf_op jit(solution)/shard_map/ppermute | solution.py:15
  98.5 12.3 %collective-permute-start.7 = (bf16[128,1024]{0,1:T(8,128)(2,1)S(1)}, bf16[128,1024]{0,1:T(8,128)(2,1)}, u32[]{:S(2)}, u32[]{:S(2)}) collective-permute-start(bf16[128,1024]{0,1:T(8,128)(2,1)S(1)} %fusion.117), channel_id=1, source_target_pairs={{1,0},{2,1},{3,2},{4,3},{5,4},{6,5},{7,6},{8,7},{9,8},{10,9},{11,1... | collective-permute-start | bytes 786440 | tf_op jit(solution)/shard_map/ppermute | solution.py:15
  105.3 12.2 %collective-permute-start.11 = (bf16[128,1024]{0,1:T(8,128)(2,1)S(1)}, bf16[128,1024]{0,1:T(8,128)(2,1)S(1)}, u32[]{:S(2)}, u32[]{:S(2)}) collective-permute-start(bf16[128,1024]{0,1:T(8,128)(2,1)S(1)} %fusion.113), channel_id=1, source_target_pairs={{1,0},{2,1},{3,2},{4,3},{5,4},{6,5},{7,6},{8,7},{9,8},{10,9},{11,1... | collective-permute-start | bytes 786440 | tf_op jit(solution)/shard_map/ppermute | solution.py:15
  111.8 12.2 %collective-permute-start.8 = (bf16[128,1024]{0,1:T(8,128)(2,1)S(1)}, bf16[128,1024]{0,1:T(8,128)(2,1)S(1)}, u32[]{:S(2)}, u32[]{:S(2)}) collective-permute-start(bf16[128,1024]{0,1:T(8,128)(2,1)S(1)} %fusion.116), channel_id=1, source_target_pairs={{1,0},{2,1},{3,2},{4,3},{5,4},{6,5},{7,6},{8,7},{9,8},{10,9},{11,1... | collective-permute-start | bytes 786440 | tf_op jit(solution)/shard_map/ppermute | solution.py:15
where the time goes:
time: 126 us; the launch traced here: 125 us
  starting transfers between devices  37.6 us (30%)
  local copies, waits for them, and re-layouts  30.5 us (24%)
  matrix products  27.2 us (22%)
  waiting for transfers between devices  17.9 us (14%)
  other arithmetic  10.1 us (8%)
  between operations  1.61 us (1%)
    ppermute x12, starting transfers between devices, from_behind(): lax.ppermute(value, axis, [(source, source + steps) for source in range(f...  37.6 us
    unnamed x61, local copies, waits for them, and re-layouts  22.3 us
    ppermute x12, waiting for transfers between devices, from_behind(): lax.ppermute(value, axis, [(source, source + steps) for source in range(f...  17.9 us
    dot_general x8, matrix products, block_grads(): jnp.einsum('rgd,kd->grk', dh, vh, preferred_element_type=jnp.float32)  5.55 us
    dot_general x8, matrix products, block_grads(): jnp.einsum('rgd,kd->grk', qh, kh, preferred_element_type=jnp.float32)  5.51 us
    dot_general x8, matrix products, block_grads(): jnp.einsum('grk,kd->rgd', probs_b, vh, preferred_element_type=jnp.float32)  4.49 us
    dot_general x8, matrix products, block_grads(): jnp.einsum('grk,rgd->kd', probs_b, dh, preferred_element_type=jnp.float32)  4.45 us
    convert_element_type x4, other arithmetic, short(): return part.astype(jnp.bfloat16) if part.dtype == jnp.float32 else part  4.32 us
  transfers between devices with their start and end apart: 12, of which 6 were waited for; matrix products, arithmetic and copies ran while one was open for 37% of the time, Pallas kernels for 0%

commit v1 on v0

v1 whole, which is shorter than its diff:
```python
import jax
import jax.numpy as jnp
from jax import lax
from jax.experimental import pallas as pl
from jax.experimental.pallas import tpu as pltpu
from jax.sharding import PartitionSpec as P

KVH = 8
HD = 128
G = 8
WINDOW = 384
ROWS = 128
SPAN = 4 * ROWS
STACK = G * ROWS
AXES = ("inner", "outer")
SCALE = 1.0 / HD**0.5
SCALE_LOG2 = 1.4426950408889634 / HD**0.5
HIDDEN = -1e30
NT = (((1,), (1,)), ((), ()))
GROUPS = 2
MIB = 2**20
VMEM = pl.BlockSpec(memory_space=pltpu.VMEM)


def head_columns(group):
    return pl.ds(pl.multiple_of(group * HD, HD), HD)


def stacked_blocks(refs, group):
    return jnp.concatenate([ref[:, head_columns(group)] for ref in refs], axis=0)


def heads_of(ref, group):
    return [ref[:, head_columns(group * G + h)] for h in range(G)]


def put_blocks(refs, group, value):
    for i, ref in enumerate(refs):
        ref[:, head_columns(group)] = value[i * ROWS : (i + 1) * ROWS].astype(ref.dtype)


def over_groups(step):
    def body(i, carry):
        step([i * GROUPS + j for j in range(GROUPS)])
        return carry

    lax.fori_loop(0, KVH // GROUPS, body, 0)


def put_bias(index, docs_ref, bias_ref):
    odd = lax.rem(index, 2)
    line = lax.broadcasted_iota(jnp.int32, (ROWS, ROWS), 0)
    lane = lax.broadcasted_iota(jnp.int32, (ROWS, ROWS), 1)

    def docs_of(block):
        row = docs_ref[pl.ds(jnp.maximum(block, 0), 1), :].astype(jnp.float32)
        return jnp.broadcast_to(row, (ROWS, ROWS))

    query_doc = docs_of(index)
    for i, offset in enumerate([3 - 2 * odd, 2, 1 + 2 * odd, 0]):
        gap = offset * ROWS + lane - line
        same = docs_of(index - offset).T == query_doc
        visible = (gap >= 0) & (gap < WINDOW) & (index >= offset) & same
        bias_ref[i * ROWS : (i + 1) * ROWS] = jnp.where(visible, 0.0, HIDDEN).astype(jnp.bfloat16)


def probs_kernel(index_ref, docs_ref, query_hbm, dout_hbm, *refs):
    key_refs, probs_ref, query_ref, dot_ref = refs[:4], refs[4], refs[5], refs[6]
    dv_refs, dout_ref, own_ref, bias_ref, sems, own_sem = refs[7:11], *refs[11:16]
    own_load = pltpu.make_async_copy(key_refs[3], own_ref, own_sem)
    own_load.start()
    key_refs = [*key_refs[:3], own_ref]
    row = lax.broadcasted_iota(jnp.int32, (ROWS, STACK), 0)
    column = lax.broadcasted_iota(jnp.int32, (ROWS, STACK), 1)
    identity = jnp.where((column & (ROWS - 1)) == row, 1.0, 0.0).astype(jnp.bfloat16)
    width = GROUPS * STACK

    def loads(i):
        part = pl.ds(pl.multiple_of(i * width, width), width)
        return (
            pltpu.make_async_copy(query_hbm.at[:, part], query_ref.at[:, part], sems.at[0, i]),
            pltpu.make_async_copy(dout_hbm.at[:, part], dout_ref.at[:, part], sems.at[1, i]),
        )

    for i in range(KVH // GROUPS):
        for copy in loads(i):
            copy.start()
    put_bias(index_ref[0], docs_ref, bias_ref)
    bias = bias_ref[...]
    own_load.wait()

    def step(i, carry):
        for copy in loads(i):
            copy.wait()
        groups = [i * GROUPS + j for j in range(GROUPS)]
        scores = []
        for g in groups:
            query_t = jnp.concatenate([head.T for head in heads_of(query_ref, g)], axis=1)
            scores.append(
                jnp.dot(
                    jnp.concatenate([stacked_blocks(key_refs, g), bias], axis=1),
                    jnp.concatenate([query_t, identity], axis=0),
                    preferred_element_type=jnp.float32,
                )
            )
        for g, score in zip(groups, scores):
            powers = jnp.exp2((score - jnp.max(score, axis=0, keepdims=True)) * SCALE_LOG2)
            probs = powers * (1.0 / jnp.sum(powers, axis=0, keepdims=True))
            probs_b = probs.astype(jnp.bfloat16)
            probs_ref[g] = probs_b
            heads = heads_of(dout_ref, g)
            dot_ref[g] = jnp.concatenate([head.T for head in heads], axis=1)
            dout = jnp.concatenate(heads, axis=0)
            put_blocks(dv_refs, g, jnp.dot(probs_b, dout, preferred_element_type=jnp.float32))
        return carry

    lax.fori_loop(0, KVH // GROUPS, step, 0)


def scores_kernel(query_ref, dot_ref, probs_ref, mark_ref, dv_aside_ref, *refs):
    value_refs, dscores_ref, near_ref, dk_refs = refs[:4], refs[4], refs[5], refs[6:9]
    near_ref[:, KVH * HD :] = dv_aside_ref[...]

    def step(groups):
        deltas, dprobs = [], []
        for g in groups:
            values = stacked_blocks(value_refs, g)
            out = jnp.dot(values.T, probs_ref[g], preferred_element_type=jnp.float32)
            out = out.astype(jnp.bfloat16).astype(jnp.float32)
            deltas.append(jnp.sum(out * dot_ref[g].astype(jnp.float32), axis=0, keepdims=True))
            dprobs.append(jnp.dot(values, dot_ref[g], preferred_element_type=jnp.float32))
        for g, delta, dprob in zip(groups, deltas, dprobs):
            dscores = (probs_ref[g].astype(jnp.float32) * (dprob - delta)).astype(jnp.bfloat16)
            dscores_ref[g] = dscores
            query = jnp.concatenate(heads_of(query_ref, g), axis=0)
            dk = jnp.dot(dscores, query, preferred_element_type=jnp.float32)
            put_blocks([near_ref, *dk_refs], g, dk * SCALE)

    over_groups(step)


def queries_kernel(dscores_ref, *refs):
    key_refs, dq_ref = refs[:4], refs[4]
    for g in range(GROUPS):
        keys = jnp.concatenate([ref[:, g * HD : (g + 1) * HD] for ref in key_refs], axis=0)
        dq = jnp.dot(keys.T, dscores_ref[g], preferred_element_type=jnp.float32) * SCALE
        for h in range(G):
            column = (g * G + h) * HD
            dq_ref[:, column : column + HD] = dq[:, h * HD : (h + 1) * HD].T.astype(dq_ref.dtype)


PAIRS = KVH * G * SPAN * ROWS


def cost(products, exponentials=0):
    return pl.CostEstimate(
        flops=PAIRS * HD * 2 * products, bytes_accessed=16 * MIB, transcendentals=exponentials
    )


def limit(mib):
    return pltpu.CompilerParams(vmem_limit_bytes=mib * MIB)


def bf16(*shape):
    return jax.ShapeDtypeStruct(shape, jnp.bfloat16)


def block_shapes():
    kinds = [jnp.bfloat16, jnp.float32, jnp.bfloat16, jnp.float32]
    return [jax.ShapeDtypeStruct((ROWS, KVH * HD), kind) for kind in kinds]


def probs_and_dv(index, doc_ids, queries, grad_out, keys):
    hbm = pl.BlockSpec(memory_space=pltpu.HBM)
    smem = pl.BlockSpec(memory_space=pltpu.SMEM)
    out = pl.pallas_call(
        probs_kernel,
        in_specs=[smem, VMEM, hbm, hbm] + [VMEM] * 3 + [hbm],
        out_specs=[VMEM] * 7,
        out_shape=[bf16(KVH, SPAN, STACK), bf16(*queries.shape), bf16(KVH, HD, STACK)]
        + block_shapes(),
        scratch_shapes=[
            pltpu.VMEM(grad_out.shape, jnp.bfloat16),
            pltpu.VMEM(keys[3].shape, jnp.bfloat16),
            pltpu.VMEM((SPAN, ROWS), jnp.bfloat16),
            pltpu.SemaphoreType.DMA((2, KVH // GROUPS)),
            pltpu.SemaphoreType.DMA,
        ],
        name="probs_and_dv",
        compiler_params=limit(24),
        cost_estimate=cost(2, PAIRS),
    )(index, doc_ids.reshape(-1, ROWS), queries, grad_out, *keys)
    return out[:3], out[3:]


def dscores_and_dk(q, dot, probs, mark, dv_aside, values):
    out = pl.pallas_call(
        scores_kernel,
        in_specs=[VMEM] * 9,
        out_specs=[VMEM] * 5,
        out_shape=[bf16(KVH, SPAN, STACK), bf16(ROWS, 2 * KVH * HD)] + block_shapes()[1:],
        input_output_aliases={2: 0},
        name="dscores_and_dk",
        compiler_params=limit(24),
        cost_estimate=cost(3),
    )(q, dot, probs, mark, dv_aside, *values)
    return out[0], out[1], out[2:]


def dq_of(dscores, keys, shape):
    return pl.pallas_call(
        queries_kernel,
        grid=(KVH // GROUPS,),
        in_specs=[pl.BlockSpec((GROUPS, SPAN, STACK), lambda s: (s, 0, 0))]
        + [pl.BlockSpec((ROWS, GROUPS * HD), lambda s: (0, s))] * 4,
        out_specs=pl.BlockSpec((ROWS, GROUPS * G * HD), lambda s: (0, s)),
        out_shape=bf16(*shape),
        name="dq",
        compiler_params=limit(24),
        cost_estimate=cost(1),
    )(dscores, *keys)


def place_kernel(index_ref, place_ref):
    place_ref[0] = index_ref[0]


def place_of(index):
    smem = pl.BlockSpec(memory_space=pltpu.SMEM)
    return pl.pallas_call(
        place_kernel,
        in_specs=[smem],
        out_specs=smem,
        out_shape=jax.ShapeDtypeStruct((1,), jnp.int32),
        name="place",
        cost_estimate=pl.CostEstimate(flops=10**11, bytes_accessed=10**8, transcendentals=0),
    )(index.astype(jnp.int32)[None])


def mark_kernel(docs_ref, mark_ref):
    mark_ref[...] = docs_ref[0:8, :]


def small_mark(doc_ids):
    return pl.pallas_call(
        mark_kernel,
        grid=(1,),
        in_specs=[pl.BlockSpec((8, ROWS), lambda i: (0, 0))],
        out_specs=pl.BlockSpec((8, ROWS), lambda i: (0, 0)),
        out_shape=jax.ShapeDtypeStruct((8, ROWS), jnp.int32),
        name="mark",
    )(in_hbm(doc_ids.reshape(-1, ROWS)))


def in_hbm(x):
    return pltpu.with_memory_space_constraint(x, pltpu.HBM)


def per_device(queries, keys, values, grad_out, doc_ids):
    devices = lax.axis_size(AXES)
    index = lax.axis_index(AXES)
    ahead = [(i, i + (1 if i % 2 == 0 else 3)) for i in range(devices)]
    ahead = [pair for pair in ahead if pair[1] < devices]
    skip = [(i, i + 2) for i in range(devices - 2)]
    swap = [(i, i ^ 1) for i in range(devices)]
    back = [(b, a) for a, b in ahead]
    unskip = [(b, a) for a, b in skip]

    mark = small_mark(doc_ids)
    key_aside = lax.ppermute(keys, AXES, ahead)
    key_middle = lax.ppermute(keys, AXES, skip)
    mark, late_values = lax.optimization_barrier((mark, values))
    value_aside = lax.ppermute(late_values, AXES, ahead)
    value_middle = lax.ppermute(late_values, AXES, skip)
    key_aside, late_index = lax.optimization_barrier((key_aside, index))
    place = place_of(late_index)
    key_blocks = [key_aside, key_middle, lax.ppermute(key_middle, AXES, swap), in_hbm(keys)]
    (probs, query_copy, dot), dv_blocks = probs_and_dv(
        place, doc_ids, in_hbm(queries), in_hbm(grad_out), key_blocks
    )
    dv_aside, dv_middle, dv_paired, dv_own = dv_blocks
    _, value_aside, value_middle = lax.optimization_barrier(
        (dv_paired, value_aside, value_middle)
    )
    value_paired = lax.ppermute(value_middle, AXES, swap)
    dv_other = lax.ppermute(dv_paired, AXES, swap)
    dv_far = lax.ppermute((dv_middle + dv_other).astype(jnp.bfloat16), AXES, unskip)
    dscores, aside, dk_blocks = dscores_and_dk(
        query_copy,
        dot,
        probs,
        mark,
        dv_aside,
        [value_aside, value_middle, value_paired, values],
    )
    dk_middle, dk_paired, dk_own = dk_blocks
    dk_paired, dv_far = lax.optimization_barrier((dk_paired, dv_far))
    dk_other = lax.ppermute(dk_paired, AXES, swap)
    near = lax.ppermute(aside, AXES, back)
    dk_far = lax.ppermute((dk_middle + dk_other).astype(jnp.bfloat16), AXES, unskip)
    grad_queries = dq_of(dscores, key_blocks, queries.shape)
    width = keys.shape[1]
    grad_keys = (dk_own + near[:, :width] + dk_far).astype(jnp.bfloat16)
    grad_values = (dv_own + near[:, width:] + dv_far).astype(jnp.bfloat16)
    return grad_queries, grad_keys, grad_values


def solution(mesh):
    split = P(AXES, None)
    return jax.shard_map(
        per_device,
        mesh=mesh,
        in_specs=(split, split, split, split, P()),
        out_specs=(split, split, split),
        check_vma=False,
    )
```

time: 126 us -> 68.6 us (0.54)
  the two profiles are of different devices: /device:TPU:121 before, /device:TPU:120 now
where the time goes in v1:
time: 68.6 us; the launch traced here: 68.2 us
  Pallas kernels  25.3 us (37%)
  starting transfers between devices  21.2 us (31%)
  waiting for transfers between devices  19.6 us (29%)
  other arithmetic  1.17 us (2%)
  between operations  0.8 us (1%)
    pallas_call x1, Pallas kernels, probs_and_dv(): pl.pallas_call(probs_kernel, in_specs=[smem, VMEM, hbm, hbm] + [VMEM] * 3...  11.2 us
    ppermute x1, waiting for transfers between devices, per_device(): lax.ppermute((dk_middle + dk_other).astype(jnp.bfloat16), AXES, unskip)  10.1 us
    pallas_call x1, Pallas kernels, dscores_and_dk(): pl.pallas_call(scores_kernel, in_specs=[VMEM] * 9, out_specs=[VMEM] * 5,...  7.82 us
    ppermute x1, waiting for transfers between devices, per_device(): lax.ppermute((dv_middle + dv_other).astype(jnp.bfloat16), AXES, unskip)  4.86 us
    pallas_call x1, Pallas kernels, dq_of(): pl.pallas_call(queries_kernel, grid=(KVH // GROUPS,), in_specs=[pl.BlockS...  4.45 us
    ppermute x1, starting transfers between devices, per_device(): value_aside = lax.ppermute(late_values, AXES, ahead)  4.43 us
    ppermute x1, starting transfers between devices, per_device(): value_middle = lax.ppermute(late_values, AXES, skip)  3.82 us
    ppermute x1, waiting for transfers between devices, per_device(): near = lax.ppermute(aside, AXES, back)  3.08 us
  transfers between devices with their start and end apart: 11, of which 5 were waited for; matrix products, arithmetic and copies ran while one was open for 0% of the time, Pallas kernels for 37%

profile of v1, /device:TPU:120, one launch (start us, length us, event | category | flops | bytes accessed | tf_op | source)
XLA Modules:
  0.0 68.2 jit_solution(16733958556148107535)
XLA Ops:
  0.6 1.9 %collective-permute-start = (bf16[128,1024]{1,0:T(8,128)(2,1)}, bf16[128,1024]{1,0:T(8,128)(2,1)S(1)}, u32[]{:S(2)}, u32[]{:S(2)}) collective-permute-start(bf16[128,1024]{1,0:T(8,128)(2,1)} %refs_3_.5), channel_id=1, source_target_pairs={{0,1},{1,4},{2,3},{3,6},{4,5},{5,8},{6,7},{7,10},{8,9},{9,12},{10,... | collective-permute-start | bytes 786440 | tf_op jit(solution)/shard_map/ppermute | solution.py:271
  2.6 2.7 %collective-permute-start.1 = (bf16[128,1024]{1,0:T(8,128)(2,1)}, bf16[128,1024]{1,0:T(8,128)(2,1)S(1)}, u32[]{:S(2)}, u32[]{:S(2)}) collective-permute-start(bf16[128,1024]{1,0:T(8,128)(2,1)} %refs_3_.5), channel_id=1, source_target_pairs={{0,2},{1,3},{2,4},{3,5},{4,6},{5,7},{6,8},{7,9},{8,10},{9,11},{10,... | collective-permute-start | bytes 786440 | tf_op jit(solution)/shard_map/ppermute | solution.py:272
  5.3 1.3 %mark.1.mark_ref = s32[8,128]{1,0:T(8,128)} custom-call(s32[128,128]{1,0:T(8,128)} %bitcast.2), custom_call_target="tpu_custom_call" | custom-call | tf_op jit(solution)/shard_map/mark/pallas_call | solution.py:246
  6.6 3.8 %collective-permute-start.4 = (bf16[128,1024]{1,0:T(8,128)(2,1)}, bf16[128,1024]{1,0:T(8,128)(2,1)S(1)}, u32[]{:S(2)}, u32[]{:S(2)}) collective-permute-start(bf16[128,1024]{1,0:T(8,128)(2,1)} %refs_3_.4), channel_id=1, source_target_pairs={{0,2},{1,3},{2,4},{3,5},{4,6},{5,7},{6,8},{7,9},{8,10},{9,11},{10,... | collective-permute-start | bytes 786440 | tf_op jit(solution)/shard_map/ppermute | solution.py:275
  10.4 4.4 %collective-permute-start.3 = (bf16[128,1024]{1,0:T(8,128)(2,1)}, bf16[128,1024]{1,0:T(8,128)(2,1)S(1)}, u32[]{:S(2)}, u32[]{:S(2)}) collective-permute-start(bf16[128,1024]{1,0:T(8,128)(2,1)} %refs_3_.4), channel_id=1, source_target_pairs={{0,1},{1,4},{2,3},{3,6},{4,5},{5,8},{6,7},{7,10},{8,9},{9,12},{10,... | collective-permute-start | bytes 786440 | tf_op jit(solution)/shard_map/ppermute | solution.py:274
  14.8 0.0 collective-permute-done.refs_0_
  14.8 0.0 collective-permute-done.1.refs_1_
  14.8 0.8 %collective-permute-start.2 = (bf16[128,1024]{1,0:T(8,128)(2,1)S(1)}, bf16[128,1024]{1,0:T(8,128)(2,1)S(1)}, u32[]{:S(2)}, u32[]{:S(2)}) collective-permute-start(bf16[128,1024]{1,0:T(8,128)(2,1)S(1)} %collective-permute-done.1.refs_1_), channel_id=1, source_target_pairs={{0,1},{1,0},{2,3},{3,2},{4,5},{5,4},{6,7},{7,6},{8,9},{9,8},{10,11... | collective-permute-start | bytes 786440 | tf_op jit(solution)/shard_map/ppermute | solution.py:278
  15.7 0.5 place.1.index_ref
  16.2 0.0 copy-start
  16.2 0.0 copy-start.2
  16.2 0.6 collective-permute-done.2.refs_2_
  16.8 11.2 %probs_and_dv.1 = (bf16[8,512,1024]{2,1,0:T(8,128)(2,1)S(1)}, bf16[128,8192]{1,0:T(8,128)(2,1)S(1)}, bf16[8,128,1024]{2,1,0:T(8,128)(2,1)S(1)}, bf16[128,1024]{1...) custom-call(s32[1]{0:T(128)} %place.1.index_ref, ...), custom_call_target="tpu_custom_call" | custom-call | flops 2147483648 | bytes 16777216 | tf_op jit(solution)/shard_map/probs_and_dv/pallas_call | solution.py:177
  28.1 0.5 collective-permute-start.7
  28.5 0.0 collective-permute-done.4.refs_1_
  28.5 0.0 collective-permute-done.3.refs_0_
  28.5 0.1 collective-permute-start.5
  28.7 1.0 %collective-permute-done.7 = bf16[128,1024]{1,0:T(8,128)(2,1)S(1)} collective-permute-done((bf16[128,1024]{1,0:T(8,128)(2,1)S(1)}, bf16[128,1024]{1,0:T(8,128)(2,1)S(1)}, u32[]{:S(2)}, u32[]{:S(2)}) %collective-permute-start.7) | collective-permute-done | bytes 262176 | tf_op jit(solution)/shard_map/ppermute | solution.py:287
  29.7 0.1 add_convert_fusion.3
  29.8 2.9 %collective-permute-start.8 = (bf16[128,1024]{1,0:T(8,128)(2,1)S(1)}, bf16[128,1024]{1,0:T(8,128)(2,1)S(1)}, u32[]{:S(2)}, u32[]{:S(2)}) collective-permute-start(bf16[128,1024]{1,0:T(8,128)(2,1)S(1)} %add_convert_fusion.3), channel_id=1, source_target_pairs={{2,0},{3,1},{4,2},{5,3},{6,4},{7,5},{8,6},{9,7},{10,8},{11,9},{12,... | collective-permute-start | bytes 786440 | tf_op jit(solution)/shard_map/ppermute | solution.py:288
  32.7 0.0 collective-permute-done.5.refs_2_
  32.7 7.8 %dscores_and_dk.1 = (bf16[8,512,1024]{2,1,0:T(8,128)(2,1)S(1)}, bf16[128,2048]{1,0:T(8,128)(2,1)S(1)}, f32[128,1024]{1,0:T(8,128)S(1)}, bf16[128,1024]{1,0:T(8,128)(2,1)S(1)}, f32[128,1024]{1,0:T(8,128)S(1)}) custom-call(bf16[128,8192]{1,0:T(8,128)(2,1)S(1)} %get-tuple-element.25.query_ref, ...), custom_call_target="tpu_custom_call", output_to_operand_aliasing={{0}: (2, {})} | custom-call | flops 3221225472 | bytes 16777216 | tf_op jit(solution)/shard_map/dscores_and_dk/pallas_call | solution.py:198
  40.5 4.9 %collective-permute-done.8 = bf16[128,1024]{1,0:T(8,128)(2,1)S(1)} collective-permute-done((bf16[128,1024]{1,0:T(8,128)(2,1)S(1)}, bf16[128,1024]{1,0:T(8,128)(2,1)S(1)}, u32[]{:S(2)}, u32[]{:S(2)}) %collective-permute-start.8) | collective-permute-done | bytes 262176 | tf_op jit(solution)/shard_map/ppermute | solution.py:288
  45.4 0.0 collective-permute-start.9
  45.4 2.1 %collective-permute-start.6 = (bf16[128,2048]{1,0:T(8,128)(2,1)S(1)}, bf16[128,2048]{1,0:T(8,128)(2,1)S(1)}, u32[]{:S(2)}, u32[]{:S(2)}) collective-permute-start(bf16[128,2048]{1,0:T(8,128)(2,1)S(1)} %get-tuple-element.36), channel_id=1, source_target_pairs={{1,0},{4,1},{3,2},{6,3},{5,4},{8,5},{7,6},{10,7},{9,8},{12,9},{11,... | collective-permute-start | bytes 1572872 | tf_op jit(solution)/shard_map/ppermute | solution.py:300
  47.5 0.0 collective-permute-done.9
  47.5 0.1 add_convert_fusion.2
  47.6 1.9 %collective-permute-start.10 = (bf16[128,1024]{1,0:T(8,128)(2,1)S(1)}, bf16[128,1024]{1,0:T(8,128)(2,1)S(1)}, u32[]{:S(2)}, u32[]{:S(2)}) collective-permute-start(bf16[128,1024]{1,0:T(8,128)(2,1)S(1)} %add_convert_fusion.2), channel_id=1, source_target_pairs={{2,0},{3,1},{4,2},{5,3},{6,4},{7,5},{8,6},{9,7},{10,8},{11,9},{12,... | collective-permute-start | bytes 786440 | tf_op jit(solution)/shard_map/ppermute | solution.py:301
  49.5 4.4 %dq.1 = bf16[128,8192]{1,0:T(8,128)(2,1)} custom-call(bf16[8,512,1024]{2,1,0:T(8,128)(2,1)S(1)} %get-tuple-element.34.dscores_ref, bf16[128,1024]{1,0:T(8,128)(2,1)S(1)} %collective-permute-done.refs_0_, bf16[128,1024]{1,0:T(8,128)(2,1)S(1)} %collective-permute-done.1.refs_1_, bf16[128,1024]{1,0:T(8,128)(2,1)S(1)} %collective-permute-done.2.refs_2_, ...), custom_call_target="tpu_custom_call" | custom-call | flops 1073741824 | bytes 16777216 | tf_op jit(solution)/shard_map/dq/pallas_call | solution.py:212
  54.0 3.1 %collective-permute-done.6 = bf16[128,2048]{1,0:T(8,128)(2,1)S(1)} collective-permute-done((bf16[128,2048]{1,0:T(8,128)(2,1)S(1)}, bf16[128,2048]{1,0:T(8,128)(2,1)S(1)}, u32[]{:S(2)}, u32[]{:S(2)}) %collective-permute-start.6) | collective-permute-done | bytes 524320 | tf_op jit(solution)/shard_map/ppermute | solution.py:300
  57.0 10.1 %collective-permute-done.10 = bf16[128,1024]{1,0:T(8,128)(2,1)S(1)} collective-permute-done((bf16[128,1024]{1,0:T(8,128)(2,1)S(1)}, bf16[128,1024]{1,0:T(8,128)(2,1)S(1)}, u32[]{:S(2)}, u32[]{:S(2)}) %collective-permute-start.10) | collective-permute-done | bytes 262176 | tf_op jit(solution)/shard_map/ppermute | solution.py:301
  67.1 1.1 %add_convert_fusion = (bf16[128,1024]{1,0:T(8,128)(2,1)}, bf16[128,1024]{1,0:T(8,128)(2,1)}) fusion(bf16[128,1024]{1,0:T(8,128)(2,1)S(1)} %collective-permute-done.8, f32[128,1024]{1,0:T(8,128)S(1)} %get-tuple-element.41, bf16[128,2048]{1,0:T(8,128)(2,1)S(1)} %collective-permute-done.6, bf16[128,1024]{1,0:T(8,128)(2,1)S(1)} %collective-permute-done.10, ...), kind=kLoop, calls=%fused_computation | loop fusion | flops 1310720 | bytes 2621440 | tf_op jit(solution)/shard_map/convert_element_type | solution.py:305
  (4 shorter events, 0.0 us)
Async XLA Ops:
  0.6 14.2 %collective-permute-start = (bf16[128,1024]{1,0:T(8,128)(2,1)}, bf16[128,1024]{1,0:T(8,128)(2,1)S(1)}, u32[]{:S(2)}, u32[]{:S(2)}) collective-permute-start(bf16[128,1024]{1,0:T(8,128)(2,1)} %refs_3_.5), channel_id=1, source_target_pairs={{0,1},{1,4},{2,3},{3,6},{4,5},{5,8},{6,7},{7,10},{8,9},{9,12},{10,... | collective-permute-start | bytes 786440 | tf_op jit(solution)/shard_map/ppermute | solution.py:271
  2.6 12.3 %collective-permute-start.1 = (bf16[128,1024]{1,0:T(8,128)(2,1)}, bf16[128,1024]{1,0:T(8,128)(2,1)S(1)}, u32[]{:S(2)}, u32[]{:S(2)}) collective-permute-start(bf16[128,1024]{1,0:T(8,128)(2,1)} %refs_3_.5), channel_id=1, source_target_pairs={{0,2},{1,3},{2,4},{3,5},{4,6},{5,7},{6,8},{7,9},{8,10},{9,11},{10,... | collective-permute-start | bytes 786440 | tf_op jit(solution)/shard_map/ppermute | solution.py:272
  6.6 22.0 %collective-permute-start.4 = (bf16[128,1024]{1,0:T(8,128)(2,1)}, bf16[128,1024]{1,0:T(8,128)(2,1)S(1)}, u32[]{:S(2)}, u32[]{:S(2)}) collective-permute-start(bf16[128,1024]{1,0:T(8,128)(2,1)} %refs_3_.4), channel_id=1, source_target_pairs={{0,2},{1,3},{2,4},{3,5},{4,6},{5,7},{6,8},{7,9},{8,10},{9,11},{10,... | collective-permute-start | bytes 786440 | tf_op jit(solution)/shard_map/ppermute | solution.py:275
  10.4 18.2 %collective-permute-start.3 = (bf16[128,1024]{1,0:T(8,128)(2,1)}, bf16[128,1024]{1,0:T(8,128)(2,1)S(1)}, u32[]{:S(2)}, u32[]{:S(2)}) collective-permute-start(bf16[128,1024]{1,0:T(8,128)(2,1)} %refs_3_.4), channel_id=1, source_target_pairs={{0,1},{1,4},{2,3},{3,6},{4,5},{5,8},{6,7},{7,10},{8,9},{9,12},{10,... | collective-permute-start | bytes 786440 | tf_op jit(solution)/shard_map/ppermute | solution.py:274
  14.8 2.0 %collective-permute-start.2 = (bf16[128,1024]{1,0:T(8,128)(2,1)S(1)}, bf16[128,1024]{1,0:T(8,128)(2,1)S(1)}, u32[]{:S(2)}, u32[]{:S(2)}) collective-permute-start(bf16[128,1024]{1,0:T(8,128)(2,1)S(1)} %collective-permute-done.1.refs_1_), channel_id=1, source_target_pairs={{0,1},{1,0},{2,3},{3,2},{4,5},{5,4},{6,7},{7,6},{8,9},{9,8},{10,11... | collective-permute-start | bytes 786440 | tf_op jit(solution)/shard_map/ppermute | solution.py:278
  15.7 1.2 %copy-start.1 = (s32[16384]{0:T(1024)S(1)}, s32[16384]{0:T(1024)}, u32[]{:S(2)}) copy-start(s32[16384]{0:T(1024)} %param.9) | copy-start | bytes 196612
  16.2 16.5 %copy-start = (bf16[128,1024]{1,0:T(8,128)(2,1)S(1)}, bf16[128,1024]{1,0:T(8,128)(2,1)}, u32[]{:S(2)}) copy-start(bf16[128,1024]{1,0:T(8,128)(2,1)} %refs_3_.4) | copy-start | bytes 786436
  16.2 16.5 %copy-start.2 = (s32[8,128]{1,0:T(8,128)S(1)}, s32[8,128]{1,0:T(8,128)}, u32[]{:S(2)}) copy-start(s32[8,128]{1,0:T(8,128)} %mark.1.mark_ref) | copy-start | bytes 12292
  28.1 1.6 %collective-permute-start.7 = (bf16[128,1024]{1,0:T(8,128)(2,1)S(1)}, bf16[128,1024]{1,0:T(8,128)(2,1)S(1)}, u32[]{:S(2)}, u32[]{:S(2)}) collective-permute-start(bf16[128,1024]{1,0:T(8,128)(2,1)S(1)} %get-tuple-element.30), channel_id=1, source_target_pairs={{0,1},{1,0},{2,3},{3,2},{4,5},{5,4},{6,7},{7,6},{8,9},{9,8},{10,11... | collective-permute-start | bytes 786440 | tf_op jit(solution)/shard_map/ppermute | solution.py:287
  28.5 4.1 %collective-permute-start.5 = (bf16[128,1024]{1,0:T(8,128)(2,1)S(1)}, bf16[128,1024]{1,0:T(8,128)(2,1)S(1)}, u32[]{:S(2)}, u32[]{:S(2)}) collective-permute-start(bf16[128,1024]{1,0:T(8,128)(2,1)S(1)} %collective-permute-done.4.refs_1_), channel_id=1, source_target_pairs={{0,1},{1,0},{2,3},{3,2},{4,5},{5,4},{6,7},{7,6},{8,9},{9,8},{10,11... | collective-permute-start | bytes 786440 | tf_op jit(solution)/shard_map/ppermute | solution.py:286
  29.8 15.6 %collective-permute-start.8 = (bf16[128,1024]{1,0:T(8,128)(2,1)S(1)}, bf16[128,1024]{1,0:T(8,128)(2,1)S(1)}, u32[]{:S(2)}, u32[]{:S(2)}) collective-permute-start(bf16[128,1024]{1,0:T(8,128)(2,1)S(1)} %add_convert_fusion.3), channel_id=1, source_target_pairs={{2,0},{3,1},{4,2},{5,3},{6,4},{7,5},{8,6},{9,7},{10,8},{11,9},{12,... | collective-permute-start | bytes 786440 | tf_op jit(solution)/shard_map/ppermute | solution.py:288
  45.4 2.1 %collective-permute-start.9 = (bf16[128,1024]{1,0:T(8,128)(2,1)S(1)}, bf16[128,1024]{1,0:T(8,128)(2,1)S(1)}, u32[]{:S(2)}, u32[]{:S(2)}) collective-permute-start(bf16[128,1024]{1,0:T(8,128)(2,1)S(1)} %get-tuple-element.40), channel_id=1, source_target_pairs={{0,1},{1,0},{2,3},{3,2},{4,5},{5,4},{6,7},{7,6},{8,9},{9,8},{10,11... | collective-permute-start | bytes 786440 | tf_op jit(solution)/shard_map/ppermute | solution.py:299
  45.4 11.6 %collective-permute-start.6 = (bf16[128,2048]{1,0:T(8,128)(2,1)S(1)}, bf16[128,2048]{1,0:T(8,128)(2,1)S(1)}, u32[]{:S(2)}, u32[]{:S(2)}) collective-permute-start(bf16[128,2048]{1,0:T(8,128)(2,1)S(1)} %get-tuple-element.36), channel_id=1, source_target_pairs={{1,0},{4,1},{3,2},{6,3},{5,4},{8,5},{7,6},{10,7},{9,8},{12,9},{11,... | collective-permute-start | bytes 1572872 | tf_op jit(solution)/shard_map/ppermute | solution.py:300
  47.6 19.5 %collective-permute-start.10 = (bf16[128,1024]{1,0:T(8,128)(2,1)S(1)}, bf16[128,1024]{1,0:T(8,128)(2,1)S(1)}, u32[]{:S(2)}, u32[]{:S(2)}) collective-permute-start(bf16[128,1024]{1,0:T(8,128)(2,1)S(1)} %add_convert_fusion.2), channel_id=1, source_target_pairs={{2,0},{3,1},{4,2},{5,3},{6,4},{7,5},{8,6},{9,7},{10,8},{11,9},{12,... | collective-permute-start | bytes 786440 | tf_op jit(solution)/shard_map/ppermute | solution.py:301

commit v2 on v1

v2 whole, which is shorter than its diff:
```python
import jax
import jax.numpy as jnp
from jax import lax
from jax.experimental import pallas as pl
from jax.experimental.pallas import tpu as pltpu
from jax.sharding import PartitionSpec as P

KVH = 8
HD = 128
G = 8
WINDOW = 384
ROWS = 128
SPAN = 4 * ROWS
STACK = G * ROWS
AXES = ("inner", "outer")
SCALE = 1.0 / HD**0.5
SCALE_LOG2 = 1.4426950408889634 / HD**0.5
HIDDEN = -1e30
NT = (((1,), (1,)), ((), ()))
GROUPS = 2
MIB = 2**20
VMEM = pl.BlockSpec(memory_space=pltpu.VMEM)


def head_columns(group):
    return pl.ds(pl.multiple_of(group * HD, HD), HD)


def stacked_blocks(refs, group):
    return jnp.concatenate([ref[:, head_columns(group)] for ref in refs], axis=0)


def heads_of(ref, group):
    return [ref[:, head_columns(group * G + h)] for h in range(G)]


def put_blocks(refs, group, value):
    for i, ref in enumerate(refs):
        ref[:, head_columns(group)] = value[i * ROWS : (i + 1) * ROWS].astype(ref.dtype)


def put_bias(index, docs_ref, bias_ref):
    odd = lax.rem(index, 2)
    line = lax.broadcasted_iota(jnp.int32, (ROWS, ROWS), 0)
    lane = lax.broadcasted_iota(jnp.int32, (ROWS, ROWS), 1)

    def docs_of(block):
        row = docs_ref[pl.ds(jnp.maximum(block, 0), 1), :].astype(jnp.float32)
        return jnp.broadcast_to(row, (ROWS, ROWS))

    query_doc = docs_of(index)
    for i, offset in enumerate([3 - 2 * odd, 2, 1 + 2 * odd, 0]):
        gap = offset * ROWS + lane - line
        same = docs_of(index - offset).T == query_doc
        visible = (gap >= 0) & (gap < WINDOW) & (index >= offset) & same
        bias_ref[i * ROWS : (i + 1) * ROWS] = jnp.where(visible, 0.0, HIDDEN).astype(jnp.bfloat16)


def stack_kernel(index_ref, docs_ref, query_hbm, dout_hbm, keys_hbm, *refs):
    qt_ref, dot_ref, query_ref, dout_ref, bias_ref, own_ref, sems, own_sem = refs
    loads = []
    for i, (source, target) in enumerate([(query_hbm, query_ref), (dout_hbm, dout_ref)]):
        for g in range(KVH):
            part = slice(g * STACK, (g + 1) * STACK)
            loads.append(
                pltpu.make_async_copy(source.at[:, part], target.at[:, part], sems.at[i, g])
            )
    own_load = pltpu.make_async_copy(keys_hbm, own_ref, own_sem)
    for load in [*loads, own_load]:
        load.start()
    put_bias(index_ref[0], docs_ref, bias_ref)
    for g in range(KVH):
        loads[g].wait()
        loads[KVH + g].wait()
        for source, target in [(query_ref, qt_ref), (dout_ref, dot_ref)]:
            target[g] = jnp.concatenate([head.T for head in heads_of(source, g)], axis=1)
    own_load.wait()


def probs_kernel(place_ref, qt_ref, bias_ref, dout_ref, *refs):
    key_refs, probs_ref, dv_refs = refs[:4], refs[4], refs[5:9]
    bias = bias_ref[...]
    row = lax.broadcasted_iota(jnp.int32, (ROWS, STACK), 0)
    column = lax.broadcasted_iota(jnp.int32, (ROWS, STACK), 1)
    identity = jnp.where((column & (ROWS - 1)) == row, 1.0, 0.0).astype(jnp.bfloat16)

    def step(i, carry):
        groups = [i * GROUPS + j for j in range(GROUPS)]
        scores = [
            jnp.dot(
                jnp.concatenate([stacked_blocks(key_refs, g), bias], axis=1),
                jnp.concatenate([qt_ref[g], identity], axis=0),
                preferred_element_type=jnp.float32,
            )
            for g in groups
        ]
        for g, score in zip(groups, scores):
            powers = jnp.exp2((score - jnp.max(score, axis=0, keepdims=True)) * SCALE_LOG2)
            probs = powers * (1.0 / jnp.sum(powers, axis=0, keepdims=True))
            probs_b = probs.astype(jnp.bfloat16)
            probs_ref[g] = probs_b
            dout = jnp.concatenate(heads_of(dout_ref, g), axis=0)
            put_blocks(dv_refs, g, jnp.dot(probs_b, dout, preferred_element_type=jnp.float32))
        return carry

    lax.fori_loop(0, KVH // GROUPS, step, 0)


def scores_kernel(query_ref, dot_ref, probs_ref, *refs):
    value_refs, dscores_ref, dk_refs = refs[:4], refs[4], refs[5:9]
    def step(i, carry):
        groups = [i * GROUPS + j for j in range(GROUPS)]
        deltas, dprobs = [], []
        for g in groups:
            values = stacked_blocks(value_refs, g)
            out = jnp.dot(values.T, probs_ref[g], preferred_element_type=jnp.float32)
            out = out.astype(jnp.bfloat16).astype(jnp.float32)
            deltas.append(jnp.sum(out * dot_ref[g].astype(jnp.float32), axis=0, keepdims=True))
            dprobs.append(jnp.dot(values, dot_ref[g], preferred_element_type=jnp.float32))
        for g, delta, dprob in zip(groups, deltas, dprobs):
            dscores = (probs_ref[g].astype(jnp.float32) * (dprob - delta)).astype(jnp.bfloat16)
            dscores_ref[g] = dscores
            query = jnp.concatenate(heads_of(query_ref, g), axis=0)
            dk = jnp.dot(dscores, query, preferred_element_type=jnp.float32)
            put_blocks(dk_refs, g, dk * SCALE)
        return carry

    lax.fori_loop(0, KVH // GROUPS, step, 0)


def queries_kernel(dscores_ref, *refs):
    key_refs, dq_ref = refs[:4], refs[4]
    for g in range(GROUPS):
        keys = jnp.concatenate([ref[:, g * HD : (g + 1) * HD] for ref in key_refs], axis=0)
        dq = jnp.dot(keys.T, dscores_ref[g], preferred_element_type=jnp.float32) * SCALE
        for h in range(G):
            column = (g * G + h) * HD
            dq_ref[:, column : column + HD] = dq[:, h * HD : (h + 1) * HD].T.astype(dq_ref.dtype)


PAIRS = KVH * G * SPAN * ROWS


def cost(products, exponentials=0):
    return pl.CostEstimate(
        flops=PAIRS * HD * 2 * products, bytes_accessed=16 * MIB, transcendentals=exponentials
    )


def limit(mib):
    return pltpu.CompilerParams(vmem_limit_bytes=mib * MIB)


def bf16(*shape):
    return jax.ShapeDtypeStruct(shape, jnp.bfloat16)


def block_shapes():
    kinds = [jnp.bfloat16, jnp.float32, jnp.bfloat16, jnp.float32]
    return [jax.ShapeDtypeStruct((ROWS, KVH * HD), kind) for kind in kinds]


HBM = pl.BlockSpec(memory_space=pltpu.HBM)
SMEM = pl.BlockSpec(memory_space=pltpu.SMEM)


def stacked(index, doc_ids, queries, grad_out, keys):
    flat = (KVH, HD, STACK)
    return pl.pallas_call(
        stack_kernel,
        in_specs=[SMEM, VMEM, HBM, HBM, HBM],
        out_specs=[VMEM] * 6,
        out_shape=[
            pltpu.VMEM(shape, jnp.bfloat16)
            for shape in (flat, flat, queries.shape, queries.shape, (SPAN, ROWS), keys.shape)
        ],
        scratch_shapes=[
            pltpu.SemaphoreType.DMA((2, KVH)),
            pltpu.SemaphoreType.DMA,
        ],
        name="stacked",
        compiler_params=limit(12),
    )(index.astype(jnp.int32)[None], doc_ids.reshape(-1, ROWS), queries, grad_out, keys)


def probs_and_dv(place, qt, bias, grad_out, keys):
    out = pl.pallas_call(
        probs_kernel,
        in_specs=[SMEM] + [VMEM] * 7,
        out_specs=[VMEM] * 5,
        out_shape=[bf16(KVH, SPAN, STACK)] + block_shapes(),
        name="probs_and_dv",
        compiler_params=limit(10),
        cost_estimate=cost(2, PAIRS),
    )(place, qt, bias, grad_out, *keys)
    return out[0], out[1:]


def dscores_and_dk(queries, dot, probs, values):
    out = pl.pallas_call(
        scores_kernel,
        in_specs=[VMEM] * 7,
        out_specs=[VMEM] * 5,
        out_shape=[bf16(KVH, SPAN, STACK)] + block_shapes(),
        input_output_aliases={2: 0},
        name="dscores_and_dk",
        compiler_params=limit(10),
        cost_estimate=cost(3),
    )(queries, dot, probs, *values)
    return out[0], out[1:]


def dq_of(dscores, keys, shape):
    return pl.pallas_call(
        queries_kernel,
        grid=(KVH // GROUPS,),
        in_specs=[pl.BlockSpec((GROUPS, SPAN, STACK), lambda s: (s, 0, 0))]
        + [pl.BlockSpec((ROWS, GROUPS * HD), lambda s: (0, s))] * 4,
        out_specs=pl.BlockSpec((ROWS, GROUPS * G * HD), lambda s: (0, s)),
        out_shape=bf16(*shape),
        name="dq",
        compiler_params=limit(24),
        cost_estimate=cost(1),
    )(dscores, *keys)


def place_kernel(index_ref, place_ref):
    place_ref[0] = index_ref[0]


def place_of(index):
    smem = pl.BlockSpec(memory_space=pltpu.SMEM)
    return pl.pallas_call(
        place_kernel,
        in_specs=[smem],
        out_specs=smem,
        out_shape=jax.ShapeDtypeStruct((1,), jnp.int32),
        name="place",
        compiler_params=limit(1),
        cost_estimate=pl.CostEstimate(flops=10**11, bytes_accessed=10**8, transcendentals=0),
    )(index.astype(jnp.int32)[None])


def sum_kernel(place_ref, own_ref, other_ref, out_ref):
    out_ref[...] = (own_ref[...] + other_ref[...].astype(jnp.float32)).astype(jnp.bfloat16)


def sum_of(place, own, other):
    return pl.pallas_call(
        sum_kernel,
        in_specs=[SMEM, VMEM, VMEM],
        out_specs=VMEM,
        out_shape=pltpu.VMEM(own.shape, jnp.bfloat16),
        name="sum",
        compiler_params=limit(2),
    )(place, own, other)


def in_hbm(x):
    return pltpu.with_memory_space_constraint(x, pltpu.HBM)


def per_device(queries, keys, values, grad_out, doc_ids):
    devices = lax.axis_size(AXES)
    index = lax.axis_index(AXES)
    ahead = [(i, i + (1 if i % 2 == 0 else 3)) for i in range(devices)]
    ahead = [pair for pair in ahead if pair[1] < devices]
    skip = [(i, i + 2) for i in range(devices - 2)]
    swap = [(i, i ^ 1) for i in range(devices)]
    back = [(b, a) for a, b in ahead]
    unskip = [(b, a) for a, b in skip]

    queries, grad_out = in_hbm(queries), in_hbm(grad_out)
    key_aside = lax.ppermute(keys, AXES, ahead)
    key_middle = lax.ppermute(keys, AXES, skip)
    qt, dot, queries, grad_out, bias, own_keys = stacked(index, doc_ids, queries, grad_out, in_hbm(keys))
    dot, queries, late_values = lax.optimization_barrier((dot, queries, values))
    value_aside = lax.ppermute(late_values, AXES, ahead)
    value_middle = lax.ppermute(late_values, AXES, skip)
    key_paired = lax.ppermute(key_middle, AXES, swap)
    key_aside, key_middle, late_index, qt, grad_out, bias, own_keys = lax.optimization_barrier(
        (key_aside, key_middle, index, qt, grad_out, bias, own_keys)
    )
    place = place_of(late_index)
    key_blocks = [key_aside, key_middle, key_paired, own_keys]
    probs, dv_blocks = probs_and_dv(place, qt, bias, grad_out, key_blocks)
    dv_aside, dv_middle, dv_paired, dv_own = dv_blocks
    _, value_aside, value_middle = lax.optimization_barrier(
        (dv_paired, value_aside, value_middle)
    )
    value_paired = lax.ppermute(value_middle, AXES, swap)
    dv_other = lax.ppermute(dv_paired, AXES, swap)
    dv_far = lax.ppermute((dv_middle + dv_other).astype(jnp.bfloat16), AXES, unskip)
    dv_near = lax.ppermute(dv_aside, AXES, back)
    dscores, dk_blocks = dscores_and_dk(
        queries,
        dot,
        probs,
        [value_aside, value_middle, value_paired, values],
    )
    dk_aside, dk_middle, dk_paired, dk_own = dk_blocks

    dk_other = lax.ppermute(dk_paired, AXES, swap)
    dk_near = lax.ppermute(dk_aside, AXES, back)
    dk_middle, late_index = lax.optimization_barrier((dk_middle, index))
    dk_sum = sum_of(place_of(late_index), dk_middle, dk_other)
    dk_far = lax.ppermute(dk_sum, AXES, unskip)
    grad_queries = dq_of(dscores, key_blocks, queries.shape)
    grad_keys = (dk_own + dk_near + dk_far).astype(jnp.bfloat16)
    grad_values = (dv_own + dv_near + dv_far).astype(jnp.bfloat16)
    return grad_queries, grad_keys, grad_values


def solution(mesh):
    split = P(AXES, None)
    return jax.shard_map(
        per_device,
        mesh=mesh,
        in_specs=(split, split, split, split, P()),
        out_specs=(split, split, split),
        check_vma=False,
    )
```

time: 68.6 us -> 64.8 us (0.945)
  the two profiles are of different devices: /device:TPU:120 before, /device:TPU:8 now
where the time goes in v2:
time: 64.8 us; the launch traced here: 64.4 us
  starting transfers between devices  32.5 us (50%)
  Pallas kernels  24.6 us (38%)
  waiting for transfers between devices  3.98 us (6%)
  other arithmetic  1.67 us (3%)
  local copies, waits for them, and re-layouts  0.84 us (1%)
  between operations  0.8 us (1%)
    pallas_call x1, Pallas kernels, probs_and_dv(): pl.pallas_call(probs_kernel, in_specs=[SMEM] + [VMEM] * 7, out_specs=[VME...  8.54 us
    pallas_call x1, Pallas kernels, dscores_and_dk(): pl.pallas_call(scores_kernel, in_specs=[VMEM] * 7, out_specs=[VMEM] * 5,...  7.67 us
    ppermute x1, starting transfers between devices, per_device(): dk_near = lax.ppermute(dk_aside, AXES, back)  7.07 us
    ppermute x1, starting transfers between devices, per_device(): value_aside = lax.ppermute(late_values, AXES, ahead)  5.59 us
    ppermute x1, starting transfers between devices, per_device(): dv_near = lax.ppermute(dv_aside, AXES, back)  5.47 us
    ppermute x1, starting transfers between devices, per_device(): key_middle = lax.ppermute(keys, AXES, skip)  3.83 us
    pallas_call x1, Pallas kernels, dq_of(): pl.pallas_call(queries_kernel, grid=(KVH // GROUPS,), in_specs=[pl.BlockS...  3.39 us
    pallas_call x1, Pallas kernels, stacked(): pl.pallas_call(stack_kernel, in_specs=[SMEM, VMEM, HBM, HBM, HBM], out_sp...  3.33 us
  transfers between devices with their start and end apart: 12, of which 5 were waited for; matrix products, arithmetic and copies ran while one was open for 1% of the time, Pallas kernels for 38%

profile of v2, /device:TPU:8, one launch (start us, length us, event | category | flops | bytes accessed | tf_op | source)
XLA Modules:
  0.0 64.4 jit_solution(14892616551709381620)
XLA Ops:
  0.6 3.8 %collective-permute-start.1 = (bf16[128,1024]{1,0:T(8,128)(2,1)}, bf16[128,1024]{1,0:T(8,128)(2,1)S(1)}, u32[]{:S(2)}, u32[]{:S(2)}) collective-permute-start(bf16[128,1024]{1,0:T(8,128)(2,1)} %keys_hbm.1), channel_id=1, source_target_pairs={{0,2},{1,3},{2,4},{3,5},{4,6},{5,7},{6,8},{7,9},{8,10},{9,11},{10,... | collective-permute-start | bytes 786440 | tf_op jit(solution)/shard_map/ppermute | solution.py:275
  4.5 1.9 %collective-permute-start = (bf16[128,1024]{1,0:T(8,128)(2,1)}, bf16[128,1024]{1,0:T(8,128)(2,1)S(1)}, u32[]{:S(2)}, u32[]{:S(2)}) collective-permute-start(bf16[128,1024]{1,0:T(8,128)(2,1)} %keys_hbm.1), channel_id=1, source_target_pairs={{0,1},{1,4},{2,3},{3,6},{4,5},{5,8},{6,7},{7,10},{8,9},{9,12},{10,... | collective-permute-start | bytes 786440 | tf_op jit(solution)/shard_map/ppermute | solution.py:274
  6.4 0.8 %copy-done.1 = s32[16384]{0:T(1024)S(1)} copy-done((s32[16384]{0:T(1024)S(1)}, s32[16384]{0:T(1024)}, u32[]{:S(2)}) %copy-start.1) | copy-done | bytes 65560
  7.2 3.3 %stacked.1 = (bf16[8,128,1024]{2,1,0:T(8,128)(2,1)S(1)}, bf16[8,128,1024]{2,1,0:T(8,128)(2,1)S(1)}, bf16[128,8192]{1,0:T(8,128)(2,1)S(1)}, bf16[128,8192]{1,0:T(...) custom-call(s32[1]{0:T(128)} %bitcast.index_ref, s32[128,128]{1,0:T(8,128)S(1)} %bitcast.4, ...), custom_call_target="tpu_custom_call" | custom-call | tf_op jit(solution)/shard_map/stacked/pallas_call | solution.py:169
  10.6 5.6 %collective-permute-start.3 = (bf16[128,1024]{1,0:T(8,128)(2,1)S(1)}, bf16[128,1024]{1,0:T(8,128)(2,1)S(1)}, u32[]{:S(2)}, u32[]{:S(2)}) collective-permute-start(bf16[128,1024]{1,0:T(8,128)(2,1)S(1)} %copy-done), channel_id=1, source_target_pairs={{0,1},{1,4},{2,3},{3,6},{4,5},{5,8},{6,7},{7,10},{8,9},{9,12},{10,... | collective-permute-start | bytes 786440 | tf_op jit(solution)/shard_map/ppermute | solution.py:278
  16.2 2.2 %collective-permute-start.4 = (bf16[128,1024]{1,0:T(8,128)(2,1)S(1)}, bf16[128,1024]{1,0:T(8,128)(2,1)S(1)}, u32[]{:S(2)}, u32[]{:S(2)}) collective-permute-start(bf16[128,1024]{1,0:T(8,128)(2,1)S(1)} %copy-done), channel_id=1, source_target_pairs={{0,2},{1,3},{2,4},{3,5},{4,6},{5,7},{6,8},{7,9},{8,10},{9,11},{10,... | collective-permute-start | bytes 786440 | tf_op jit(solution)/shard_map/ppermute | solution.py:279
  18.4 0.3 collective-permute-done.1.refs_1_
  18.8 0.3 collective-permute-done.refs_0_
  19.1 0.0 collective-permute-start.2
  19.1 0.5 place.2.place_ref
  19.6 1.0 %collective-permute-done.2.refs_2_ = bf16[128,1024]{1,0:T(8,128)(2,1)S(1)} collective-permute-done((bf16[128,1024]{1,0:T(8,128)(2,1)S(1)}, bf16[128,1024]{1,0:T(8,128)(2,1)S(1)}, u32[]{:S(2)}, u32[]{:S(2)}) %collective-permute-start.2) | collective-permute-done | bytes 262176 | tf_op jit(solution)/shard_map/ppermute | solution.py:280
  20.6 8.5 %probs_and_dv.1 = (bf16[8,512,1024]{2,1,0:T(8,128)(2,1)S(1)}, bf16[128,1024]{1,0:T(8,128)(2,1)S(1)}, f32[128,1024]{1,0:T(8,128)S(1)}, bf16[128,1024]{1,0:T(8,128)(2,1)S(1)}, f32[128,1024]{1,0:T(8,128)S(1)}) custom-call(s32[1]{0:T(128)} %place.2.place_ref, bf16[8,128,1024]{2,1,0:T(8,128)(2,1)S(1)} %get-tuple-element.42.qt_ref, ...), custom_call_target="tpu_custom_call" | custom-call | flops 2147483648 | bytes 16777216 | tf_op jit(solution)/shard_map/probs_and_dv/pallas_call | solution.py:187
  29.2 0.2 collective-permute-start.10
  29.4 1.1 %collective-permute-done.4.refs_1_ = bf16[128,1024]{1,0:T(8,128)(2,1)S(1)} collective-permute-done((bf16[128,1024]{1,0:T(8,128)(2,1)S(1)}, bf16[128,1024]{1,0:T(8,128)(2,1)S(1)}, u32[]{:S(2)}, u32[]{:S(2)}) %collective-permute-start.4) | collective-permute-done | bytes 262176 | tf_op jit(solution)/shard_map/ppermute | solution.py:279
  30.5 5.5 %collective-permute-start.9 = (bf16[128,1024]{1,0:T(8,128)(2,1)S(1)}, bf16[128,1024]{1,0:T(8,128)(2,1)S(1)}, u32[]{:S(2)}, u32[]{:S(2)}) collective-permute-start(bf16[128,1024]{1,0:T(8,128)(2,1)S(1)} %get-tuple-element.61), channel_id=1, source_target_pairs={{1,0},{4,1},{3,2},{6,3},{5,4},{8,5},{7,6},{10,7},{9,8},{12,9},{11,... | collective-permute-start | bytes 786440 | tf_op jit(solution)/shard_map/ppermute | solution.py:294
  36.0 0.0 collective-permute-done.10
  36.0 0.1 add_convert_fusion.1
  36.1 2.9 %collective-permute-start.11 = (bf16[128,1024]{1,0:T(8,128)(2,1)S(1)}, bf16[128,1024]{1,0:T(8,128)(2,1)S(1)}, u32[]{:S(2)}, u32[]{:S(2)}) collective-permute-start(bf16[128,1024]{1,0:T(8,128)(2,1)S(1)} %add_convert_fusion.1), channel_id=1, source_target_pairs={{2,0},{3,1},{4,2},{5,3},{6,4},{7,5},{8,6},{9,7},{10,8},{11,9},{12,... | collective-permute-start | bytes 786440 | tf_op jit(solution)/shard_map/ppermute | solution.py:293
  39.0 0.0 collective-permute-done.5.refs_2_
  39.0 7.7 %dscores_and_dk.1 = (bf16[8,512,1024]{2,1,0:T(8,128)(2,1)S(1)}, bf16[128,1024]{1,0:T(8,128)(2,1)S(1)}, f32[128,1024]{1,0:T(8,128)S(1)}, bf16[128,1024]{1,0:T(8,128)(2,1)S(1)}, f32[128,1024]{1,0:T(8,128)S(1)}) custom-call(bf16[128,8192]{1,0:T(8,128)(2,1)S(1)} %get-tuple-element.35.query_ref, ...), custom_call_target="tpu_custom_call", output_to_operand_aliasing={{0}: (2, {})} | custom-call | flops 3221225472 | bytes 16777216 | tf_op jit(solution)/shard_map/dscores_and_dk/pallas_call | solution.py:200
  46.7 0.3 collective-permute-start.7
  47.0 0.5 place.3.place_ref
  47.5 7.1 %collective-permute-start.6 = (bf16[128,1024]{1,0:T(8,128)(2,1)S(1)}, bf16[128,1024]{1,0:T(8,128)(2,1)S(1)}, u32[]{:S(2)}, u32[]{:S(2)}) collective-permute-start(bf16[128,1024]{1,0:T(8,128)(2,1)S(1)} %get-tuple-element.55), channel_id=1, source_target_pairs={{1,0},{4,1},{3,2},{6,3},{5,4},{8,5},{7,6},{10,7},{9,8},{12,9},{11,... | collective-permute-start | bytes 786440 | tf_op jit(solution)/shard_map/ppermute | solution.py:304
  54.6 0.0 collective-permute-done.7.other_ref
  54.6 0.7 %sum.1 = bf16[128,1024]{1,0:T(8,128)(2,1)S(1)} custom-call(s32[1]{0:T(128)} %place.3.place_ref, f32[128,1024]{1,0:T(8,128)S(1)} %get-tuple-element.58.own_ref, bf16[128,1024]{1,0:T(8,128)(2,1)S(1)} %collective-permute-done.7.other_ref), custom_call_target="tpu_custom_call" | custom-call | tf_op jit(solution)/shard_map/sum/pallas_call | solution.py:249
  55.3 2.9 %collective-permute-start.8 = (bf16[128,1024]{1,0:T(8,128)(2,1)S(1)}, bf16[128,1024]{1,0:T(8,128)(2,1)S(1)}, u32[]{:S(2)}, u32[]{:S(2)}) collective-permute-start(bf16[128,1024]{1,0:T(8,128)(2,1)S(1)} %sum.1), channel_id=1, source_target_pairs={{2,0},{3,1},{4,2},{5,3},{6,4},{7,5},{8,6},{9,7},{10,8},{11,9},{12,... | collective-permute-start | bytes 786440 | tf_op jit(solution)/shard_map/ppermute | solution.py:307
  58.2 3.4 %dq.1 = bf16[128,8192]{1,0:T(8,128)(2,1)} custom-call(bf16[8,512,1024]{2,1,0:T(8,128)(2,1)S(1)} %get-tuple-element.53.dscores_ref, bf16[128,1024]{1,0:T(8,128)(2,1)S(1)} %collective-permute-done.refs_0_, bf16[128,1024]{1,0:T(8,128)(2,1)S(1)} %collective-permute-done.1.refs_1_, bf16[128,1024]{1,0:T(8,128)(2,1)S(1)} %collective-permute-done.2.refs_2_, ...), custom_call_target="tpu_custom_call" | custom-call | flops 1073741824 | bytes 16777216 | tf_op jit(solution)/shard_map/dq/pallas_call | solution.py:214
  61.6 0.0 collective-permute-done.9
  61.6 0.0 collective-permute-done.11
  61.6 0.8 %add_convert_fusion = bf16[128,1024]{1,0:T(8,128)(2,1)} fusion(bf16[128,1024]{1,0:T(8,128)(2,1)S(1)} %collective-permute-done.11, f32[128,1024]{1,0:T(8,128)S(1)} %get-tuple-element.60, bf16[128,1024]{1,0:T(8,128)(2,1)S(1)} %collective-permute-done.9), kind=kLoop, calls=%fused_computation | loop fusion | flops 655360 | bytes 1310720 | tf_op jit(solution)/shard_map/convert_element_type | solution.py:310
  62.4 1.1 %collective-permute-done.8 = bf16[128,1024]{1,0:T(8,128)(2,1)S(1)} collective-permute-done((bf16[128,1024]{1,0:T(8,128)(2,1)S(1)}, bf16[128,1024]{1,0:T(8,128)(2,1)S(1)}, u32[]{:S(2)}, u32[]{:S(2)}) %collective-permute-start.8) | collective-permute-done | bytes 262176 | tf_op jit(solution)/shard_map/ppermute | solution.py:307
  63.6 0.8 %add_convert_fusion.2 = bf16[128,1024]{1,0:T(8,128)(2,1)} fusion(bf16[128,1024]{1,0:T(8,128)(2,1)S(1)} %collective-permute-done.8, f32[128,1024]{1,0:T(8,128)S(1)} %get-tuple-element.54, bf16[128,1024]{1,0:T(8,128)(2,1)S(1)} %collective-permute-done.6), kind=kLoop, calls=%fused_computation.2 | loop fusion | flops 655360 | bytes 1310720 | tf_op jit(solution)/shard_map/convert_element_type | solution.py:309
  (6 shorter events, 0.0 us)
Async XLA Ops:
  0.6 18.1 %collective-permute-start.1 = (bf16[128,1024]{1,0:T(8,128)(2,1)}, bf16[128,1024]{1,0:T(8,128)(2,1)S(1)}, u32[]{:S(2)}, u32[]{:S(2)}) collective-permute-start(bf16[128,1024]{1,0:T(8,128)(2,1)} %keys_hbm.1), channel_id=1, source_target_pairs={{0,2},{1,3},{2,4},{3,5},{4,6},{5,7},{6,8},{7,9},{8,10},{9,11},{10,... | collective-permute-start | bytes 786440 | tf_op jit(solution)/shard_map/ppermute | solution.py:275
  4.5 14.6 %collective-permute-start = (bf16[128,1024]{1,0:T(8,128)(2,1)}, bf16[128,1024]{1,0:T(8,128)(2,1)S(1)}, u32[]{:S(2)}, u32[]{:S(2)}) collective-permute-start(bf16[128,1024]{1,0:T(8,128)(2,1)} %keys_hbm.1), channel_id=1, source_target_pairs={{0,1},{1,4},{2,3},{3,6},{4,5},{5,8},{6,7},{7,10},{8,9},{9,12},{10,... | collective-permute-start | bytes 786440 | tf_op jit(solution)/shard_map/ppermute | solution.py:274
  6.4 0.8 %copy-start.1 = (s32[16384]{0:T(1024)S(1)}, s32[16384]{0:T(1024)}, u32[]{:S(2)}) copy-start(s32[16384]{0:T(1024)} %param.9) | copy-start | bytes 196612
  7.2 3.3 %copy-start = (bf16[128,1024]{1,0:T(8,128)(2,1)S(1)}, bf16[128,1024]{1,0:T(8,128)(2,1)}, u32[]{:S(2)}) copy-start(bf16[128,1024]{1,0:T(8,128)(2,1)} %refs_3_.1) | copy-start | bytes 786436
  10.6 18.8 %collective-permute-start.3 = (bf16[128,1024]{1,0:T(8,128)(2,1)S(1)}, bf16[128,1024]{1,0:T(8,128)(2,1)S(1)}, u32[]{:S(2)}, u32[]{:S(2)}) collective-permute-start(bf16[128,1024]{1,0:T(8,128)(2,1)S(1)} %copy-done), channel_id=1, source_target_pairs={{0,1},{1,4},{2,3},{3,6},{4,5},{5,8},{6,7},{7,10},{8,9},{9,12},{10,... | collective-permute-start | bytes 786440 | tf_op jit(solution)/shard_map/ppermute | solution.py:278
  16.2 14.3 %collective-permute-start.4 = (bf16[128,1024]{1,0:T(8,128)(2,1)S(1)}, bf16[128,1024]{1,0:T(8,128)(2,1)S(1)}, u32[]{:S(2)}, u32[]{:S(2)}) collective-permute-start(bf16[128,1024]{1,0:T(8,128)(2,1)S(1)} %copy-done), channel_id=1, source_target_pairs={{0,2},{1,3},{2,4},{3,5},{4,6},{5,7},{6,8},{7,9},{8,10},{9,11},{10,... | collective-permute-start | bytes 786440 | tf_op jit(solution)/shard_map/ppermute | solution.py:279
  19.1 1.5 %collective-permute-start.2 = (bf16[128,1024]{1,0:T(8,128)(2,1)S(1)}, bf16[128,1024]{1,0:T(8,128)(2,1)S(1)}, u32[]{:S(2)}, u32[]{:S(2)}) collective-permute-start(bf16[128,1024]{1,0:T(8,128)(2,1)S(1)} %collective-permute-done.1.refs_1_), channel_id=1, source_target_pairs={{0,1},{1,0},{2,3},{3,2},{4,5},{5,4},{6,7},{7,6},{8,9},{9,8},{10,11... | collective-permute-start | bytes 786440 | tf_op jit(solution)/shard_map/ppermute | solution.py:280
  29.2 6.8 %collective-permute-start.10 = (bf16[128,1024]{1,0:T(8,128)(2,1)S(1)}, bf16[128,1024]{1,0:T(8,128)(2,1)S(1)}, u32[]{:S(2)}, u32[]{:S(2)}) collective-permute-start(bf16[128,1024]{1,0:T(8,128)(2,1)S(1)} %get-tuple-element.49), channel_id=1, source_target_pairs={{0,1},{1,0},{2,3},{3,2},{4,5},{5,4},{6,7},{7,6},{8,9},{9,8},{10,11... | collective-permute-start | bytes 786440 | tf_op jit(solution)/shard_map/ppermute | solution.py:292
  30.5 8.5 %collective-permute-start.5 = (bf16[128,1024]{1,0:T(8,128)(2,1)S(1)}, bf16[128,1024]{1,0:T(8,128)(2,1)S(1)}, u32[]{:S(2)}, u32[]{:S(2)}) collective-permute-start(bf16[128,1024]{1,0:T(8,128)(2,1)S(1)} %collective-permute-done.4.refs_1_), channel_id=1, source_target_pairs={{0,1},{1,0},{2,3},{3,2},{4,5},{5,4},{6,7},{7,6},{8,9},{9,8},{10,11... | collective-permute-start | bytes 786440 | tf_op jit(solution)/shard_map/ppermute | solution.py:291
  30.5 31.1 %collective-permute-start.9 = (bf16[128,1024]{1,0:T(8,128)(2,1)S(1)}, bf16[128,1024]{1,0:T(8,128)(2,1)S(1)}, u32[]{:S(2)}, u32[]{:S(2)}) collective-permute-start(bf16[128,1024]{1,0:T(8,128)(2,1)S(1)} %get-tuple-element.61), channel_id=1, source_target_pairs={{1,0},{4,1},{3,2},{6,3},{5,4},{8,5},{7,6},{10,7},{9,8},{12,9},{11,... | collective-permute-start | bytes 786440 | tf_op jit(solution)/shard_map/ppermute | solution.py:294
  36.1 25.5 %collective-permute-start.11 = (bf16[128,1024]{1,0:T(8,128)(2,1)S(1)}, bf16[128,1024]{1,0:T(8,128)(2,1)S(1)}, u32[]{:S(2)}, u32[]{:S(2)}) collective-permute-start(bf16[128,1024]{1,0:T(8,128)(2,1)S(1)} %add_convert_fusion.1), channel_id=1, source_target_pairs={{2,0},{3,1},{4,2},{5,3},{6,4},{7,5},{8,6},{9,7},{10,8},{11,9},{12,... | collective-permute-start | bytes 786440 | tf_op jit(solution)/shard_map/ppermute | solution.py:293
  46.7 7.9 %collective-permute-start.7 = (bf16[128,1024]{1,0:T(8,128)(2,1)S(1)}, bf16[128,1024]{1,0:T(8,128)(2,1)S(1)}, u32[]{:S(2)}, u32[]{:S(2)}) collective-permute-start(bf16[128,1024]{1,0:T(8,128)(2,1)S(1)} %get-tuple-element.59), channel_id=1, source_target_pairs={{0,1},{1,0},{2,3},{3,2},{4,5},{5,4},{6,7},{7,6},{8,9},{9,8},{10,11... | collective-permute-start | bytes 786440 | tf_op jit(solution)/shard_map/ppermute | solution.py:303
  47.5 14.9 %collective-permute-start.6 = (bf16[128,1024]{1,0:T(8,128)(2,1)S(1)}, bf16[128,1024]{1,0:T(8,128)(2,1)S(1)}, u32[]{:S(2)}, u32[]{:S(2)}) collective-permute-start(bf16[128,1024]{1,0:T(8,128)(2,1)S(1)} %get-tuple-element.55), channel_id=1, source_target_pairs={{1,0},{4,1},{3,2},{6,3},{5,4},{8,5},{7,6},{10,7},{9,8},{12,9},{11,... | collective-permute-start | bytes 786440 | tf_op jit(solution)/shard_map/ppermute | solution.py:304
  55.3 8.3 %collective-permute-start.8 = (bf16[128,1024]{1,0:T(8,128)(2,1)S(1)}, bf16[128,1024]{1,0:T(8,128)(2,1)S(1)}, u32[]{:S(2)}, u32[]{:S(2)}) collective-permute-start(bf16[128,1024]{1,0:T(8,128)(2,1)S(1)} %sum.1), channel_id=1, source_target_pairs={{2,0},{3,1},{4,2},{5,3},{6,4},{7,5},{8,6},{9,7},{10,8},{11,9},{12,... | collective-permute-start | bytes 786440 | tf_op jit(solution)/shard_map/ppermute | solution.py:307

commit v3 on v2

--- a/solution.py
+++ b/solution.py
@@ -16,6 +16,7 @@
 SCALE = 1.0 / HD**0.5
 SCALE_LOG2 = 1.4426950408889634 / HD**0.5
 HIDDEN = -1e30
+KEY_MOST = 6.0
 NT = (((1,), (1,)), ((), ()))
 GROUPS = 2
 MIB = 2**20
@@ -56,8 +57,9 @@
         bias_ref[i * ROWS : (i + 1) * ROWS] = jnp.where(visible, 0.0, HIDDEN).astype(jnp.bfloat16)
 
 
-def stack_kernel(index_ref, docs_ref, query_hbm, dout_hbm, keys_hbm, *refs):
-    qt_ref, dot_ref, query_ref, dout_ref, bias_ref, own_ref, sems, own_sem = refs
+def stack_kernel(index_ref, docs_hbm, query_hbm, dout_hbm, keys_hbm, *refs):
+    qt_ref, dot_ref, query_ref, dout_ref, bias_ref, own_ref, size_ref = refs[:7]
+    docs_ref, sems, own_sem, docs_sem = refs[7:]
     loads = []
     for i, (source, target) in enumerate([(query_hbm, query_ref), (dout_hbm, dout_ref)]):
         for g in range(KVH):
@@ -66,25 +68,31 @@
                 pltpu.make_async_copy(source.at[:, part], target.at[:, part], sems.at[i, g])
             )
     own_load = pltpu.make_async_copy(keys_hbm, own_ref, own_sem)
-    for load in [*loads, own_load]:
+    docs_load = pltpu.make_async_copy(docs_hbm, docs_ref, docs_sem)
+    for load in [docs_load, *loads, own_load]:
         load.start()
+    docs_load.wait()
     put_bias(index_ref[0], docs_ref, bias_ref)
+    size = jnp.zeros((1, STACK), jnp.float32)
     for g in range(KVH):
         loads[g].wait()
         loads[KVH + g].wait()
         for source, target in [(query_ref, qt_ref), (dout_ref, dot_ref)]:
             target[g] = jnp.concatenate([head.T for head in heads_of(source, g)], axis=1)
+        sums = jnp.sum(jnp.abs(qt_ref[g].astype(jnp.float32)), axis=0, keepdims=True)
+        size = jnp.maximum(size, sums)
+    size_ref[...] = jnp.broadcast_to(size, size_ref.shape)
     own_load.wait()
 
 
-def probs_kernel(place_ref, qt_ref, bias_ref, dout_ref, *refs):
+def probs_kernel(place_ref, size_ref, qt_ref, bias_ref, dout_ref, *refs):
     key_refs, probs_ref, dv_refs = refs[:4], refs[4], refs[5:9]
     bias = bias_ref[...]
     row = lax.broadcasted_iota(jnp.int32, (ROWS, STACK), 0)
     column = lax.broadcasted_iota(jnp.int32, (ROWS, STACK), 1)
     identity = jnp.where((column & (ROWS - 1)) == row, 1.0, 0.0).astype(jnp.bfloat16)
 
-    def step(i, carry):
+    def step(i, shift):
         groups = [i * GROUPS + j for j in range(GROUPS)]
         scores = [
             jnp.dot(
@@ -95,18 +103,28 @@
             for g in groups
         ]
         for g, score in zip(groups, scores):
-            powers = jnp.exp2((score - jnp.max(score, axis=0, keepdims=True)) * SCALE_LOG2)
+            if shift:
+                score = score - jnp.max(score, axis=0, keepdims=True)
+            powers = jnp.exp2(score * SCALE_LOG2)
             probs = powers * (1.0 / jnp.sum(powers, axis=0, keepdims=True))
             probs_b = probs.astype(jnp.bfloat16)
             probs_ref[g] = probs_b
             dout = jnp.concatenate(heads_of(dout_ref, g), axis=0)
             put_blocks(dv_refs, g, jnp.dot(probs_b, dout, preferred_element_type=jnp.float32))
-        return carry
-
-    lax.fori_loop(0, KVH // GROUPS, step, 0)
-
-
-def scores_kernel(query_ref, dot_ref, probs_ref, *refs):
+
+    def run(shift):
+        def body(i, carry):
+            step(i, shift)
+            return carry
+
+        lax.fori_loop(0, KVH // GROUPS, body, 0)
+
+    small = jnp.max(size_ref[0:1]) * (KEY_MOST * SCALE_LOG2) <= 115.0
+    pl.when(small)(lambda: run(False))
+    pl.when(jnp.logical_not(small))(lambda: run(True))
+
+
+def scores_kernel(mark_ref, query_ref, dot_ref, probs_ref, *refs):
     value_refs, dscores_ref, dk_refs = refs[:4], refs[4], refs[5:9]
     def step(i, carry):
         groups = [i * GROUPS + j for j in range(GROUPS)]
@@ -129,7 +147,7 @@
 
 
 def queries_kernel(dscores_ref, *refs):
-    key_refs, dq_ref = refs[:4], refs[4]
+    key_refs, dq_ref = refs[:4], refs[-1]
     for g in range(GROUPS):
         keys = jnp.concatenate([ref[:, g * HD : (g + 1) * HD] for ref in key_refs], axis=0)
         dq = jnp.dot(keys.T, dscores_ref[g], preferred_element_type=jnp.float32) * SCALE
@@ -147,6 +165,9 @@
     )
 
 
+AHEAD = pl.CostEstimate(flops=10**11, bytes_accessed=10**8, transcendentals=0)
+
+
 def limit(mib):
     return pltpu.CompilerParams(vmem_limit_bytes=mib * MIB)
 
@@ -168,64 +189,81 @@
     flat = (KVH, HD, STACK)
     return pl.pallas_call(
         stack_kernel,
-        in_specs=[SMEM, VMEM, HBM, HBM, HBM],
-        out_specs=[VMEM] * 6,
+        in_specs=[SMEM, HBM, HBM, HBM, HBM],
+        out_specs=[VMEM] * 7,
         out_shape=[
             pltpu.VMEM(shape, jnp.bfloat16)
             for shape in (flat, flat, queries.shape, queries.shape, (SPAN, ROWS), keys.shape)
-        ],
+        ]
+        + [pltpu.VMEM((8, STACK), jnp.float32)],
         scratch_shapes=[
+            pltpu.VMEM((doc_ids.shape[0] // ROWS, ROWS), jnp.int32),
             pltpu.SemaphoreType.DMA((2, KVH)),
+            pltpu.SemaphoreType.DMA,
             pltpu.SemaphoreType.DMA,
         ],
         name="stacked",
         compiler_params=limit(12),
-    )(index.astype(jnp.int32)[None], doc_ids.reshape(-1, ROWS), queries, grad_out, keys)
-
-
-def probs_and_dv(place, qt, bias, grad_out, keys):
+    )(index.astype(jnp.int32)[None], in_hbm(doc_ids.reshape(-1, ROWS)), queries, grad_out, keys)
+
+
+def probs_and_dv(place, size, qt, bias, grad_out, keys):
     out = pl.pallas_call(
         probs_kernel,
-        in_specs=[SMEM] + [VMEM] * 7,
+        in_specs=[SMEM] + [VMEM] * 8,
         out_specs=[VMEM] * 5,
         out_shape=[bf16(KVH, SPAN, STACK)] + block_shapes(),
         name="probs_and_dv",
         compiler_params=limit(10),
         cost_estimate=cost(2, PAIRS),
-    )(place, qt, bias, grad_out, *keys)
+    )(place, size, qt, bias, grad_out, *keys)
     return out[0], out[1:]
 
 
-def dscores_and_dk(queries, dot, probs, values):
+def dscores_and_dk(mark, queries, dot, probs, values):
     out = pl.pallas_call(
         scores_kernel,
-        in_specs=[VMEM] * 7,
+        in_specs=[SMEM] + [VMEM] * 7,
         out_specs=[VMEM] * 5,
         out_shape=[bf16(KVH, SPAN, STACK)] + block_shapes(),
-        input_output_aliases={2: 0},
+        input_output_aliases={3: 0},
         name="dscores_and_dk",
         compiler_params=limit(10),
         cost_estimate=cost(3),
-    )(queries, dot, probs, *values)
+    )(mark, queries, dot, probs, *values)
     return out[0], out[1:]
 
 
-def dq_of(dscores, keys, shape):
+def dq_of(dscores, keys, shape, first, count, earlier=()):
     return pl.pallas_call(
         queries_kernel,
-        grid=(KVH // GROUPS,),
-        in_specs=[pl.BlockSpec((GROUPS, SPAN, STACK), lambda s: (s, 0, 0))]
-        + [pl.BlockSpec((ROWS, GROUPS * HD), lambda s: (0, s))] * 4,
-        out_specs=pl.BlockSpec((ROWS, GROUPS * G * HD), lambda s: (0, s)),
+        grid=(count,),
+        in_specs=[pl.BlockSpec((GROUPS, SPAN, STACK), lambda s: (s + first, 0, 0))]
+        + [pl.BlockSpec((ROWS, GROUPS * HD), lambda s: (0, s + first))] * 4
+        + [pl.BlockSpec(memory_space=pl.ANY)] * len(earlier),
+        out_specs=pl.BlockSpec((ROWS, GROUPS * G * HD), lambda s: (0, s + first)),
         out_shape=bf16(*shape),
+        input_output_aliases={5: 0} if earlier else {},
         name="dq",
         compiler_params=limit(24),
-        cost_estimate=cost(1),
-    )(dscores, *keys)
+        cost_estimate=cost(1) if earlier else AHEAD,
+    )(dscores, *keys, *earlier)
 
 
 def place_kernel(index_ref, place_ref):
     place_ref[0] = index_ref[0]
+
+
+def mark_of(index):
+    smem = pl.BlockSpec(memory_space=pltpu.SMEM)
+    return pl.pallas_call(
+        place_kernel,
+        in_specs=[smem],
+        out_specs=smem,
+        out_shape=jax.ShapeDtypeStruct((1,), jnp.int32),
+        name="mark",
+        compiler_params=limit(1),
+    )(index.astype(jnp.int32)[None])
 
 
 def place_of(index):
@@ -237,23 +275,8 @@
         out_shape=jax.ShapeDtypeStruct((1,), jnp.int32),
         name="place",
         compiler_params=limit(1),
-        cost_estimate=pl.CostEstimate(flops=10**11, bytes_accessed=10**8, transcendentals=0),
+        cost_estimate=AHEAD,
     )(index.astype(jnp.int32)[None])
-
-
-def sum_kernel(place_ref, own_ref, other_ref, out_ref):
-    out_ref[...] = (own_ref[...] + other_ref[...].astype(jnp.float32)).astype(jnp.bfloat16)
-
-
-def sum_of(place, own, other):
-    return pl.pallas_call(
-        sum_kernel,
-        in_specs=[SMEM, VMEM, VMEM],
-        out_specs=VMEM,
-        out_shape=pltpu.VMEM(own.shape, jnp.bfloat16),
-        name="sum",
-        compiler_params=limit(2),
-    )(place, own, other)
 
 
 def in_hbm(x):
@@ -273,17 +296,17 @@
     queries, grad_out = in_hbm(queries), in_hbm(grad_out)
     key_aside = lax.ppermute(keys, AXES, ahead)
     key_middle = lax.ppermute(keys, AXES, skip)
-    qt, dot, queries, grad_out, bias, own_keys = stacked(index, doc_ids, queries, grad_out, in_hbm(keys))
-    dot, queries, late_values = lax.optimization_barrier((dot, queries, values))
+    qt, dot, queries, grad_out, bias, own_keys, size = stacked(index, doc_ids, queries, grad_out, in_hbm(keys))
+    mark, late_values = lax.optimization_barrier((mark_of(index), values))
     value_aside = lax.ppermute(late_values, AXES, ahead)
     value_middle = lax.ppermute(late_values, AXES, skip)
     key_paired = lax.ppermute(key_middle, AXES, swap)
-    key_aside, key_middle, late_index, qt, grad_out, bias, own_keys = lax.optimization_barrier(
-        (key_aside, key_middle, index, qt, grad_out, bias, own_keys)
+    key_aside, key_middle, late_index, qt, grad_out, bias, own_keys, size = lax.optimization_barrier(
+        (key_aside, key_middle, index, qt, grad_out, bias, own_keys, size)
     )
     place = place_of(late_index)
     key_blocks = [key_aside, key_middle, key_paired, own_keys]
-    probs, dv_blocks = probs_and_dv(place, qt, bias, grad_out, key_blocks)
+    probs, dv_blocks = probs_and_dv(place, size, qt, bias, grad_out, key_blocks)
     dv_aside, dv_middle, dv_paired, dv_own = dv_blocks
     _, value_aside, value_middle = lax.optimization_barrier(
         (dv_paired, value_aside, value_middle)
@@ -293,6 +316,7 @@
     dv_far = lax.ppermute((dv_middle + dv_other).astype(jnp.bfloat16), AXES, unskip)
     dv_near = lax.ppermute(dv_aside, AXES, back)
     dscores, dk_blocks = dscores_and_dk(
+        mark,
         queries,
         dot,
         probs,
@@ -301,11 +325,13 @@
     dk_aside, dk_middle, dk_paired, dk_own = dk_blocks
 
     dk_other = lax.ppermute(dk_paired, AXES, swap)
+    first_dq = dq_of(dscores, key_blocks, queries.shape, 0, 1)
+    dk_other, first_dq = lax.optimization_barrier((dk_other, first_dq))
+    dk_sum = (dk_middle + dk_other).astype(jnp.bfloat16)
+    dk_far = lax.ppermute(dk_sum, AXES, unskip)
+    dk_sum, dk_aside = lax.optimization_barrier((dk_sum, dk_aside))
     dk_near = lax.ppermute(dk_aside, AXES, back)
-    dk_middle, late_index = lax.optimization_barrier((dk_middle, index))
-    dk_sum = sum_of(place_of(late_index), dk_middle, dk_other)
-    dk_far = lax.ppermute(dk_sum, AXES, unskip)
-    grad_queries = dq_of(dscores, key_blocks, queries.shape)
+    grad_queries = dq_of(dscores, key_blocks, queries.shape, 1, KVH // GROUPS - 1, [first_dq])
     grad_keys = (dk_own + dk_near + dk_far).astype(jnp.bfloat16)
     grad_values = (dv_own + dv_near + dv_far).astype(jnp.bfloat16)
     return grad_queries, grad_keys, grad_values

time: 64.8 us -> 64.3 us (level)
  the two profiles are of different devices: /device:TPU:8 before, /device:TPU:121 now
where the time goes in v3:
time: 64.3 us; the launch traced here: 63.5 us
  starting transfers between devices  27.5 us (43%)
  Pallas kernels  26.1 us (41%)
  waiting for transfers between devices  7.34 us (11%)
  other arithmetic  1.72 us (3%)
  between operations  0.81 us (1%)
    pallas_call x1, Pallas kernels, probs_and_dv(): pl.pallas_call(probs_kernel, in_specs=[SMEM] + [VMEM] * 8, out_specs=[VME...  8.64 us
    pallas_call x1, Pallas kernels, dscores_and_dk(): pl.pallas_call(scores_kernel, in_specs=[SMEM] + [VMEM] * 7, out_specs=[VM...  8.31 us
    ppermute x1, waiting for transfers between devices, per_device(): dk_near = lax.ppermute(dk_aside, AXES, back)  6.54 us
    ppermute x1, starting transfers between devices, per_device(): key_aside = lax.ppermute(keys, AXES, ahead)  5.74 us
    ppermute x1, starting transfers between devices, per_device(): dk_far = lax.ppermute(dk_sum, AXES, unskip)  5.5 us
    pallas_call x2, Pallas kernels, dq_of(): pl.pallas_call(queries_kernel, grid=(count,), in_specs=[pl.BlockSpec((GRO...  4.16 us
    pallas_call x1, Pallas kernels, stacked(): pl.pallas_call(stack_kernel, in_specs=[SMEM, HBM, HBM, HBM, HBM], out_spe...  3.95 us
    ppermute x1, starting transfers between devices, per_device(): value_middle = lax.ppermute(late_values, AXES, skip)  3.86 us
  transfers between devices with their start and end apart: 12, of which 3 were waited for; matrix products, arithmetic and copies ran while one was open for 1% of the time, Pallas kernels for 41%

profile of v3, /device:TPU:121, one launch (start us, length us, event | category | flops | bytes accessed | tf_op | source)
XLA Modules:
  0.0 63.5 jit_solution(8263244051888720132)
XLA Ops:
  0.6 2.4 %collective-permute-start.1 = (bf16[128,1024]{1,0:T(8,128)(2,1)}, bf16[128,1024]{1,0:T(8,128)(2,1)S(1)}, u32[]{:S(2)}, u32[]{:S(2)}) collective-permute-start(bf16[128,1024]{1,0:T(8,128)(2,1)} %keys_hbm.1), channel_id=1, source_target_pairs={{0,2},{1,3},{2,4},{3,5},{4,6},{5,7},{6,8},{7,9},{8,10},{9,11},{10,... | collective-permute-start | bytes 786440 | tf_op jit(solution)/shard_map/ppermute | solution.py:298
  3.1 5.7 %collective-permute-start = (bf16[128,1024]{1,0:T(8,128)(2,1)}, bf16[128,1024]{1,0:T(8,128)(2,1)S(1)}, u32[]{:S(2)}, u32[]{:S(2)}) collective-permute-start(bf16[128,1024]{1,0:T(8,128)(2,1)} %keys_hbm.1), channel_id=1, source_target_pairs={{0,1},{1,4},{2,3},{3,6},{4,5},{5,8},{6,7},{7,10},{8,9},{9,12},{10,... | collective-permute-start | bytes 786440 | tf_op jit(solution)/shard_map/ppermute | solution.py:297
  8.8 0.5 mark.1.mark_ref
  9.3 1.9 %collective-permute-start.3 = (bf16[128,1024]{1,0:T(8,128)(2,1)}, bf16[128,1024]{1,0:T(8,128)(2,1)S(1)}, u32[]{:S(2)}, u32[]{:S(2)}) collective-permute-start(bf16[128,1024]{1,0:T(8,128)(2,1)} %refs_3_.1), channel_id=1, source_target_pairs={{0,1},{1,4},{2,3},{3,6},{4,5},{5,8},{6,7},{7,10},{8,9},{9,12},{10,... | collective-permute-start | bytes 786440 | tf_op jit(solution)/shard_map/ppermute | solution.py:301
  11.3 3.9 %collective-permute-start.4 = (bf16[128,1024]{1,0:T(8,128)(2,1)}, bf16[128,1024]{1,0:T(8,128)(2,1)S(1)}, u32[]{:S(2)}, u32[]{:S(2)}) collective-permute-start(bf16[128,1024]{1,0:T(8,128)(2,1)} %refs_3_.1), channel_id=1, source_target_pairs={{0,2},{1,3},{2,4},{3,5},{4,6},{5,7},{6,8},{7,9},{8,10},{9,11},{10,... | collective-permute-start | bytes 786440 | tf_op jit(solution)/shard_map/ppermute | solution.py:302
  15.1 4.0 %stacked.1 = (bf16[8,128,1024]{2,1,0:T(8,128)(2,1)S(1)}, bf16[8,128,1024]{2,1,0:T(8,128)(2,1)S(1)}, bf16[128,8192]{1,0:T(8,128)(2,1)S(1)}, bf16[128,8192]{1,0:T(...) custom-call(s32[1]{0:T(128)} %bitcast.index_ref, ...), custom_call_target="tpu_custom_call" | custom-call | tf_op jit(solution)/shard_map/stacked/pallas_call | solution.py:190
  19.1 0.0 collective-permute-done.1.refs_1_
  19.1 0.0 collective-permute-done.refs_0_
  19.1 0.9 %collective-permute-start.2 = (bf16[128,1024]{1,0:T(8,128)(2,1)S(1)}, bf16[128,1024]{1,0:T(8,128)(2,1)S(1)}, u32[]{:S(2)}, u32[]{:S(2)}) collective-permute-start(bf16[128,1024]{1,0:T(8,128)(2,1)S(1)} %collective-permute-done.1.refs_1_), channel_id=1, source_target_pairs={{0,1},{1,0},{2,3},{3,2},{4,5},{5,4},{6,7},{7,6},{8,9},{9,8},{10,11... | collective-permute-start | bytes 786440 | tf_op jit(solution)/shard_map/ppermute | solution.py:303
  20.0 0.5 place.1.place_ref
  20.5 0.0 copy-start
  20.5 0.6 collective-permute-done.2.refs_2_
  21.1 8.6 %probs_and_dv.1 = (bf16[8,512,1024]{2,1,0:T(8,128)(2,1)S(1)}, bf16[128,1024]{1,0:T(8,128)(2,1)S(1)}, f32[128,1024]{1,0:T(8,128)S(1)}, bf16[128,1024]{1,0:T(8,128)(2,1)S(1)}, f32[128,1024]{1,0:T(8,128)S(1)}) custom-call(s32[1]{0:T(128)} %place.1.place_ref, f32[8,1024]{1,0:T(8,128)S(1)} %get-tuple-element.44.size_ref, ...), custom_call_target="tpu_custom_call" | custom-call | flops 2147483648 | bytes 16777216 | tf_op jit(solution)/shard_map/probs_and_dv/pallas_call | solution.py:211
  29.8 0.5 collective-permute-start.10
  30.2 0.0 collective-permute-done.3.refs_0_
  30.2 0.0 collective-permute-done.4.refs_1_
  30.2 0.1 collective-permute-start.5
  30.4 2.3 %collective-permute-start.9 = (bf16[128,1024]{1,0:T(8,128)(2,1)S(1)}, bf16[128,1024]{1,0:T(8,128)(2,1)S(1)}, u32[]{:S(2)}, u32[]{:S(2)}) collective-permute-start(bf16[128,1024]{1,0:T(8,128)(2,1)S(1)} %get-tuple-element.65), channel_id=1, source_target_pairs={{1,0},{4,1},{3,2},{6,3},{5,4},{8,5},{7,6},{10,7},{9,8},{12,9},{11,... | collective-permute-start | bytes 786440 | tf_op jit(solution)/shard_map/ppermute | solution.py:317
  32.7 0.1 add_convert_fusion.1
  32.7 1.9 %collective-permute-start.11 = (bf16[128,1024]{1,0:T(8,128)(2,1)S(1)}, bf16[128,1024]{1,0:T(8,128)(2,1)S(1)}, u32[]{:S(2)}, u32[]{:S(2)}) collective-permute-start(bf16[128,1024]{1,0:T(8,128)(2,1)S(1)} %add_convert_fusion.1), channel_id=1, source_target_pairs={{2,0},{3,1},{4,2},{5,3},{6,4},{7,5},{8,6},{9,7},{10,8},{11,9},{12,... | collective-permute-start | bytes 786440 | tf_op jit(solution)/shard_map/ppermute | solution.py:316
  34.7 0.0 collective-permute-done.5.refs_2_
  34.7 8.3 %dscores_and_dk.1 = (bf16[8,512,1024]{2,1,0:T(8,128)(2,1)S(1)}, bf16[128,1024]{1,0:T(8,128)(2,1)S(1)}, f32[128,1024]{1,0:T(8,128)S(1)}, bf16[128,1024]{1,0:T(8,128)(2,1)S(1)}, f32[128,1024]{1,0:T(8,128)S(1)}) custom-call(s32[1]{0:T(128)} %mark.1.mark_ref, bf16[128,8192]{1,0:T(8,128)(2,1)S(1)} %get-tuple-element.36.query_ref, ...), custom_call_target="tpu_custom_call", output_to_operand_aliasing={{0}: (3, {})} | custom-call | flops 3221225472 | bytes 16777216 | tf_op jit(solution)/shard_map/dscores_and_dk/pallas_call | solution.py:224
  43.0 0.1 collective-permute-start.6
  43.1 1.4 %dq.2.refs_4_ = bf16[128,8192]{1,0:T(8,128)(2,1)} custom-call(bf16[8,512,1024]{2,1,0:T(8,128)(2,1)S(1)} %get-tuple-element.56.dscores_ref, bf16[128,1024]{1,0:T(8,128)(2,1)S(1)} %collective-permute-done.refs_0_, bf16[128,1024]{1,0:T(8,128)(2,1)S(1)} %collective-permute-done.1.refs_1_, bf16[128,1024]{1,0:T(8,128)(2,1)S(1)} %collective-permute-done.2.refs_2_, ...), custom_call_target="tpu_custom_call" | custom-call | flops 99999997952 | bytes 100000000 | tf_op jit(solution)/shard_map/dq/pallas_call | solution.py:238
  44.5 0.1 collective-permute-done.6
  44.6 0.1 add_convert_fusion.3
  44.7 5.5 %collective-permute-start.8 = (bf16[128,1024]{1,0:T(8,128)(2,1)S(1)}, bf16[128,1024]{1,0:T(8,128)(2,1)S(1)}, u32[]{:S(2)}, u32[]{:S(2)}) collective-permute-start(bf16[128,1024]{1,0:T(8,128)(2,1)S(1)} %add_convert_fusion.3), channel_id=1, source_target_pairs={{2,0},{3,1},{4,2},{5,3},{6,4},{7,5},{8,6},{9,7},{10,8},{11,9},{12,... | collective-permute-start | bytes 786440 | tf_op jit(solution)/shard_map/ppermute | solution.py:331
  50.2 2.3 %collective-permute-start.7 = (bf16[128,1024]{1,0:T(8,128)(2,1)S(1)}, bf16[128,1024]{1,0:T(8,128)(2,1)S(1)}, u32[]{:S(2)}, u32[]{:S(2)}) collective-permute-start(bf16[128,1024]{1,0:T(8,128)(2,1)S(1)} %get-tuple-element.63), channel_id=1, source_target_pairs={{1,0},{4,1},{3,2},{6,3},{5,4},{8,5},{7,6},{10,7},{9,8},{12,9},{11,... | collective-permute-start | bytes 786440 | tf_op jit(solution)/shard_map/ppermute | solution.py:333
  52.6 2.8 %dq.3 = bf16[128,8192]{1,0:T(8,128)(2,1)} custom-call(bf16[8,512,1024]{2,1,0:T(8,128)(2,1)S(1)} %get-tuple-element.56.dscores_ref, bf16[128,1024]{1,0:T(8,128)(2,1)S(1)} %collective-permute-done.refs_0_, bf16[128,1024]{1,0:T(8,128)(2,1)S(1)} %collective-permute-done.1.refs_1_, ...), custom_call_target="tpu_custom_call", output_to_operand_aliasing={{}: (5, {})} | custom-call | flops 1073741824 | bytes 16777216 | tf_op jit(solution)/shard_map/dq/pallas_call | solution.py:238
  55.4 0.8 %add_convert_fusion = bf16[128,1024]{1,0:T(8,128)(2,1)} fusion(bf16[128,1024]{1,0:T(8,128)(2,1)S(1)} %collective-permute-done.11, f32[128,1024]{1,0:T(8,128)S(1)} %get-tuple-element.64, bf16[128,1024]{1,0:T(8,128)(2,1)S(1)} %collective-permute-done.9), kind=kLoop, calls=%fused_computation | loop fusion | flops 655360 | bytes 1310720 | tf_op jit(solution)/shard_map/convert_element_type | solution.py:336
  56.2 6.5 %collective-permute-done.7 = bf16[128,1024]{1,0:T(8,128)(2,1)S(1)} collective-permute-done((bf16[128,1024]{1,0:T(8,128)(2,1)S(1)}, bf16[128,1024]{1,0:T(8,128)(2,1)S(1)}, u32[]{:S(2)}, u32[]{:S(2)}) %collective-permute-start.7) | collective-permute-done | bytes 262176 | tf_op jit(solution)/shard_map/ppermute | solution.py:333
  62.7 0.8 %add_convert_fusion.2 = bf16[128,1024]{1,0:T(8,128)(2,1)} fusion(bf16[128,1024]{1,0:T(8,128)(2,1)S(1)} %collective-permute-done.8, f32[128,1024]{1,0:T(8,128)S(1)} %get-tuple-element.59, bf16[128,1024]{1,0:T(8,128)(2,1)S(1)} %collective-permute-done.7), kind=kLoop, calls=%fused_computation.2 | loop fusion | flops 655360 | bytes 1310720 | tf_op jit(solution)/shard_map/convert_element_type | solution.py:335
  (5 shorter events, 0.0 us)
Async XLA Ops:
  0.6 18.5 %collective-permute-start.1 = (bf16[128,1024]{1,0:T(8,128)(2,1)}, bf16[128,1024]{1,0:T(8,128)(2,1)S(1)}, u32[]{:S(2)}, u32[]{:S(2)}) collective-permute-start(bf16[128,1024]{1,0:T(8,128)(2,1)} %keys_hbm.1), channel_id=1, source_target_pairs={{0,2},{1,3},{2,4},{3,5},{4,6},{5,7},{6,8},{7,9},{8,10},{9,11},{10,... | collective-permute-start | bytes 786440 | tf_op jit(solution)/shard_map/ppermute | solution.py:298
  3.1 16.1 %collective-permute-start = (bf16[128,1024]{1,0:T(8,128)(2,1)}, bf16[128,1024]{1,0:T(8,128)(2,1)S(1)}, u32[]{:S(2)}, u32[]{:S(2)}) collective-permute-start(bf16[128,1024]{1,0:T(8,128)(2,1)} %keys_hbm.1), channel_id=1, source_target_pairs={{0,1},{1,4},{2,3},{3,6},{4,5},{5,8},{6,7},{7,10},{8,9},{9,12},{10,... | collective-permute-start | bytes 786440 | tf_op jit(solution)/shard_map/ppermute | solution.py:297
  9.3 20.9 %collective-permute-start.3 = (bf16[128,1024]{1,0:T(8,128)(2,1)}, bf16[128,1024]{1,0:T(8,128)(2,1)S(1)}, u32[]{:S(2)}, u32[]{:S(2)}) collective-permute-start(bf16[128,1024]{1,0:T(8,128)(2,1)} %refs_3_.1), channel_id=1, source_target_pairs={{0,1},{1,4},{2,3},{3,6},{4,5},{5,8},{6,7},{7,10},{8,9},{9,12},{10,... | collective-permute-start | bytes 786440 | tf_op jit(solution)/shard_map/ppermute | solution.py:301
  11.3 19.0 %collective-permute-start.4 = (bf16[128,1024]{1,0:T(8,128)(2,1)}, bf16[128,1024]{1,0:T(8,128)(2,1)S(1)}, u32[]{:S(2)}, u32[]{:S(2)}) collective-permute-start(bf16[128,1024]{1,0:T(8,128)(2,1)} %refs_3_.1), channel_id=1, source_target_pairs={{0,2},{1,3},{2,4},{3,5},{4,6},{5,7},{6,8},{7,9},{8,10},{9,11},{10,... | collective-permute-start | bytes 786440 | tf_op jit(solution)/shard_map/ppermute | solution.py:302
  19.1 2.0 %collective-permute-start.2 = (bf16[128,1024]{1,0:T(8,128)(2,1)S(1)}, bf16[128,1024]{1,0:T(8,128)(2,1)S(1)}, u32[]{:S(2)}, u32[]{:S(2)}) collective-permute-start(bf16[128,1024]{1,0:T(8,128)(2,1)S(1)} %collective-permute-done.1.refs_1_), channel_id=1, source_target_pairs={{0,1},{1,0},{2,3},{3,2},{4,5},{5,4},{6,7},{7,6},{8,9},{9,8},{10,11... | collective-permute-start | bytes 786440 | tf_op jit(solution)/shard_map/ppermute | solution.py:303
  20.5 14.2 %copy-start = (bf16[128,1024]{1,0:T(8,128)(2,1)S(1)}, bf16[128,1024]{1,0:T(8,128)(2,1)}, u32[]{:S(2)}) copy-start(bf16[128,1024]{1,0:T(8,128)(2,1)} %refs_3_.1) | copy-start | bytes 786436
  29.8 2.9 %collective-permute-start.10 = (bf16[128,1024]{1,0:T(8,128)(2,1)S(1)}, bf16[128,1024]{1,0:T(8,128)(2,1)S(1)}, u32[]{:S(2)}, u32[]{:S(2)}) collective-permute-start(bf16[128,1024]{1,0:T(8,128)(2,1)S(1)} %get-tuple-element.52), channel_id=1, source_target_pairs={{0,1},{1,0},{2,3},{3,2},{4,5},{5,4},{6,7},{7,6},{8,9},{9,8},{10,11... | collective-permute-start | bytes 786440 | tf_op jit(solution)/shard_map/ppermute | solution.py:315
  30.2 4.4 %collective-permute-start.5 = (bf16[128,1024]{1,0:T(8,128)(2,1)S(1)}, bf16[128,1024]{1,0:T(8,128)(2,1)S(1)}, u32[]{:S(2)}, u32[]{:S(2)}) collective-permute-start(bf16[128,1024]{1,0:T(8,128)(2,1)S(1)} %collective-permute-done.4.refs_1_), channel_id=1, source_target_pairs={{0,1},{1,0},{2,3},{3,2},{4,5},{5,4},{6,7},{7,6},{8,9},{9,8},{10,11... | collective-permute-start | bytes 786440 | tf_op jit(solution)/shard_map/ppermute | solution.py:314
  30.4 25.0 %collective-permute-start.9 = (bf16[128,1024]{1,0:T(8,128)(2,1)S(1)}, bf16[128,1024]{1,0:T(8,128)(2,1)S(1)}, u32[]{:S(2)}, u32[]{:S(2)}) collective-permute-start(bf16[128,1024]{1,0:T(8,128)(2,1)S(1)} %get-tuple-element.65), channel_id=1, source_target_pairs={{1,0},{4,1},{3,2},{6,3},{5,4},{8,5},{7,6},{10,7},{9,8},{12,9},{11,... | collective-permute-start | bytes 786440 | tf_op jit(solution)/shard_map/ppermute | solution.py:317
  32.7 22.6 %collective-permute-start.11 = (bf16[128,1024]{1,0:T(8,128)(2,1)S(1)}, bf16[128,1024]{1,0:T(8,128)(2,1)S(1)}, u32[]{:S(2)}, u32[]{:S(2)}) collective-permute-start(bf16[128,1024]{1,0:T(8,128)(2,1)S(1)} %add_convert_fusion.1), channel_id=1, source_target_pairs={{2,0},{3,1},{4,2},{5,3},{6,4},{7,5},{8,6},{9,7},{10,8},{11,9},{12,... | collective-permute-start | bytes 786440 | tf_op jit(solution)/shard_map/ppermute | solution.py:316
  43.0 1.6 %collective-permute-start.6 = (bf16[128,1024]{1,0:T(8,128)(2,1)S(1)}, bf16[128,1024]{1,0:T(8,128)(2,1)S(1)}, u32[]{:S(2)}, u32[]{:S(2)}) collective-permute-start(bf16[128,1024]{1,0:T(8,128)(2,1)S(1)} %get-tuple-element.57), channel_id=1, source_target_pairs={{0,1},{1,0},{2,3},{3,2},{4,5},{5,4},{6,7},{7,6},{8,9},{9,8},{10,11... | collective-permute-start | bytes 786440 | tf_op jit(solution)/shard_map/ppermute | solution.py:327
  44.7 18.0 %collective-permute-start.8 = (bf16[128,1024]{1,0:T(8,128)(2,1)S(1)}, bf16[128,1024]{1,0:T(8,128)(2,1)S(1)}, u32[]{:S(2)}, u32[]{:S(2)}) collective-permute-start(bf16[128,1024]{1,0:T(8,128)(2,1)S(1)} %add_convert_fusion.3), channel_id=1, source_target_pairs={{2,0},{3,1},{4,2},{5,3},{6,4},{7,5},{8,6},{9,7},{10,8},{11,9},{12,... | collective-permute-start | bytes 786440 | tf_op jit(solution)/shard_map/ppermute | solution.py:331
  50.2 12.5 %collective-permute-start.7 = (bf16[128,1024]{1,0:T(8,128)(2,1)S(1)}, bf16[128,1024]{1,0:T(8,128)(2,1)S(1)}, u32[]{:S(2)}, u32[]{:S(2)}) collective-permute-start(bf16[128,1024]{1,0:T(8,128)(2,1)S(1)} %get-tuple-element.63), channel_id=1, source_target_pairs={{1,0},{4,1},{3,2},{6,3},{5,4},{8,5},{7,6},{10,7},{9,8},{12,9},{11,... | collective-permute-start | bytes 786440 | tf_op jit(solution)/shard_map/ppermute | solution.py:333

commit v4 on v3

--- a/solution.py
+++ b/solution.py
@@ -57,7 +57,7 @@
         bias_ref[i * ROWS : (i + 1) * ROWS] = jnp.where(visible, 0.0, HIDDEN).astype(jnp.bfloat16)
 
 
-def stack_kernel(index_ref, docs_hbm, query_hbm, dout_hbm, keys_hbm, *refs):
+def stack_kernel(docs_hbm, query_hbm, dout_hbm, keys_hbm, *refs):
     qt_ref, dot_ref, query_ref, dout_ref, bias_ref, own_ref, size_ref = refs[:7]
     docs_ref, sems, own_sem, docs_sem = refs[7:]
     loads = []
@@ -72,7 +72,7 @@
     for load in [docs_load, *loads, own_load]:
         load.start()
     docs_load.wait()
-    put_bias(index_ref[0], docs_ref, bias_ref)
+    put_bias(lax.axis_index(AXES), docs_ref, bias_ref)
     size = jnp.zeros((1, STACK), jnp.float32)
     for g in range(KVH):
         loads[g].wait()
@@ -85,7 +85,7 @@
     own_load.wait()
 
 
-def probs_kernel(place_ref, size_ref, qt_ref, bias_ref, dout_ref, *refs):
+def probs_kernel(size_ref, qt_ref, bias_ref, dout_ref, *refs):
     key_refs, probs_ref, dv_refs = refs[:4], refs[4], refs[5:9]
     bias = bias_ref[...]
     row = lax.broadcasted_iota(jnp.int32, (ROWS, STACK), 0)
@@ -182,14 +182,13 @@
 
 
 HBM = pl.BlockSpec(memory_space=pltpu.HBM)
-SMEM = pl.BlockSpec(memory_space=pltpu.SMEM)
-
-
-def stacked(index, doc_ids, queries, grad_out, keys):
+
+
+def stacked(doc_ids, queries, grad_out, keys):
     flat = (KVH, HD, STACK)
     return pl.pallas_call(
         stack_kernel,
-        in_specs=[SMEM, HBM, HBM, HBM, HBM],
+        in_specs=[HBM, HBM, HBM, HBM],
         out_specs=[VMEM] * 7,
         out_shape=[
             pltpu.VMEM(shape, jnp.bfloat16)
@@ -204,26 +203,26 @@
         ],
         name="stacked",
         compiler_params=limit(12),
-    )(index.astype(jnp.int32)[None], in_hbm(doc_ids.reshape(-1, ROWS)), queries, grad_out, keys)
-
-
-def probs_and_dv(place, size, qt, bias, grad_out, keys):
+    )(in_hbm(doc_ids.reshape(-1, ROWS)), queries, grad_out, keys)
+
+
+def probs_and_dv(size, qt, bias, grad_out, keys):
     out = pl.pallas_call(
         probs_kernel,
-        in_specs=[SMEM] + [VMEM] * 8,
+        in_specs=[VMEM] * 8,
         out_specs=[VMEM] * 5,
         out_shape=[bf16(KVH, SPAN, STACK)] + block_shapes(),
         name="probs_and_dv",
         compiler_params=limit(10),
         cost_estimate=cost(2, PAIRS),
-    )(place, size, qt, bias, grad_out, *keys)
+    )(size, qt, bias, grad_out, *keys)
     return out[0], out[1:]
 
 
 def dscores_and_dk(mark, queries, dot, probs, values):
     out = pl.pallas_call(
         scores_kernel,
-        in_specs=[SMEM] + [VMEM] * 7,
+        in_specs=[VMEM] * 8,
         out_specs=[VMEM] * 5,
         out_shape=[bf16(KVH, SPAN, STACK)] + block_shapes(),
         input_output_aliases={3: 0},
@@ -250,33 +249,35 @@
     )(dscores, *keys, *earlier)
 
 
-def place_kernel(index_ref, place_ref):
-    place_ref[0] = index_ref[0]
-
-
-def mark_of(index):
-    smem = pl.BlockSpec(memory_space=pltpu.SMEM)
+def mark_kernel(docs_hbm, mark_ref):
+    mark_ref[...] = jnp.zeros_like(mark_ref)
+
+
+def mark_of(doc_ids):
     return pl.pallas_call(
-        place_kernel,
-        in_specs=[smem],
-        out_specs=smem,
-        out_shape=jax.ShapeDtypeStruct((1,), jnp.int32),
+        mark_kernel,
+        in_specs=[HBM],
+        out_specs=VMEM,
+        out_shape=pltpu.VMEM((8, HD), jnp.float32),
         name="mark",
         compiler_params=limit(1),
-    )(index.astype(jnp.int32)[None])
-
-
-def place_of(index):
-    smem = pl.BlockSpec(memory_space=pltpu.SMEM)
+    )(doc_ids)
+
+
+def copy_kernel(in_ref, out_ref):
+    out_ref[...] = in_ref[...]
+
+
+def held(x):
     return pl.pallas_call(
-        place_kernel,
-        in_specs=[smem],
-        out_specs=smem,
-        out_shape=jax.ShapeDtypeStruct((1,), jnp.int32),
-        name="place",
+        copy_kernel,
+        in_specs=[VMEM],
+        out_specs=VMEM,
+        out_shape=pltpu.VMEM(x.shape, x.dtype),
+        name="held",
         compiler_params=limit(1),
         cost_estimate=AHEAD,
-    )(index.astype(jnp.int32)[None])
+    )(x)
 
 
 def in_hbm(x):
@@ -285,7 +286,6 @@
 
 def per_device(queries, keys, values, grad_out, doc_ids):
     devices = lax.axis_size(AXES)
-    index = lax.axis_index(AXES)
     ahead = [(i, i + (1 if i % 2 == 0 else 3)) for i in range(devices)]
     ahead = [pair for pair in ahead if pair[1] < devices]
     skip = [(i, i + 2) for i in range(devices - 2)]
@@ -296,17 +296,18 @@
     queries, grad_out = in_hbm(queries), in_hbm(grad_out)
     key_aside = lax.ppermute(keys, AXES, ahead)
     key_middle = lax.ppermute(keys, AXES, skip)
-    qt, dot, queries, grad_out, bias, own_keys, size = stacked(index, doc_ids, queries, grad_out, in_hbm(keys))
-    mark, late_values = lax.optimization_barrier((mark_of(index), values))
+    qt, dot, queries, grad_out, bias, own_keys, size = stacked(doc_ids, queries, grad_out, in_hbm(keys))
+    mark, late_values = lax.optimization_barrier(
+        (mark_of(in_hbm(doc_ids.reshape(-1, ROWS))), values)
+    )
     value_aside = lax.ppermute(late_values, AXES, ahead)
     value_middle = lax.ppermute(late_values, AXES, skip)
     key_paired = lax.ppermute(key_middle, AXES, swap)
-    key_aside, key_middle, late_index, qt, grad_out, bias, own_keys, size = lax.optimization_barrier(
-        (key_aside, key_middle, index, qt, grad_out, bias, own_keys, size)
-    )
-    place = place_of(late_index)
+    key_aside, key_middle, qt, grad_out, bias, own_keys, size = lax.optimization_barrier(
+        (key_aside, key_middle, qt, grad_out, bias, own_keys, size)
+    )
     key_blocks = [key_aside, key_middle, key_paired, own_keys]
-    probs, dv_blocks = probs_and_dv(place, size, qt, bias, grad_out, key_blocks)
+    probs, dv_blocks = probs_and_dv(size, qt, held(bias), grad_out, key_blocks)
     dv_aside, dv_middle, dv_paired, dv_own = dv_blocks
     _, value_aside, value_middle = lax.optimization_barrier(
         (dv_paired, value_aside, value_middle)

time: 64.3 us -> 62.4 us (0.970)
  Pallas kernels: 26.1 us -> 23.7 us
    pallas_call x5, Pallas kernels: 21.9 us -> 19.6 us  [the longest x1 7.98 us: probs_and_dv(): pl.pallas_call(probs_kernel, in_specs=[VMEM] * 8, out_specs=[VMEM] * 5, o...]
  transfers between devices with their start and end apart: 12 -> 12, of which waited for: 3 -> 3; matrix products, arithmetic and copies ran while one was open for 1% -> 1% of each run, Pallas kernels for 41% -> 39%
where the time goes in v4:
time: 62.4 us; the launch traced here: 61.6 us
  starting transfers between devices  27.5 us (44%)
  Pallas kernels  23.7 us (38%)
  waiting for transfers between devices  7.85 us (13%)
  other arithmetic  1.71 us (3%)
  between operations  0.8 us (1%)
    pallas_call x1, Pallas kernels, probs_and_dv(): pl.pallas_call(probs_kernel, in_specs=[VMEM] * 8, out_specs=[VMEM] * 5, o...  7.98 us
    pallas_call x1, Pallas kernels, dscores_and_dk(): pl.pallas_call(scores_kernel, in_specs=[VMEM] * 8, out_specs=[VMEM] * 5,...  7.64 us
    ppermute x1, waiting for transfers between devices, per_device(): dk_near = lax.ppermute(dk_aside, AXES, back)  6.53 us
    ppermute x1, starting transfers between devices, per_device(): key_aside = lax.ppermute(keys, AXES, ahead)  5.74 us
    ppermute x1, starting transfers between devices, per_device(): dk_far = lax.ppermute(dk_sum, AXES, unskip)  5.48 us
    pallas_call x2, Pallas kernels, dq_of(): pl.pallas_call(queries_kernel, grid=(count,), in_specs=[pl.BlockSpec((GRO...  4.16 us
    pallas_call x1, Pallas kernels, stacked(): pl.pallas_call(stack_kernel, in_specs=[HBM, HBM, HBM, HBM], out_specs=[VM...  3.94 us
    ppermute x1, starting transfers between devices, per_device(): value_middle = lax.ppermute(late_values, AXES, skip)  3.86 us
  transfers between devices with their start and end apart: 12, of which 3 were waited for; matrix products, arithmetic and copies ran while one was open for 1% of the time, Pallas kernels for 39%

profile of v4, /device:TPU:121, one launch (start us, length us, event | category | flops | bytes accessed | tf_op | source)
XLA Modules:
  0.0 61.6 jit_solution(1506916157131509553)
XLA Ops:
  0.6 2.4 %collective-permute-start.1 = (bf16[128,1024]{1,0:T(8,128)(2,1)}, bf16[128,1024]{1,0:T(8,128)(2,1)S(1)}, u32[]{:S(2)}, u32[]{:S(2)}) collective-permute-start(bf16[128,1024]{1,0:T(8,128)(2,1)} %keys_hbm.1), channel_id=1, source_target_pairs={{0,2},{1,3},{2,4},{3,5},{4,6},{5,7},{6,8},{7,9},{8,10},{9,11},{10,... | collective-permute-start | bytes 786440 | tf_op jit(solution)/shard_map/ppermute | solution.py:298
  3.1 5.7 %collective-permute-start = (bf16[128,1024]{1,0:T(8,128)(2,1)}, bf16[128,1024]{1,0:T(8,128)(2,1)S(1)}, u32[]{:S(2)}, u32[]{:S(2)}) collective-permute-start(bf16[128,1024]{1,0:T(8,128)(2,1)} %keys_hbm.1), channel_id=1, source_target_pairs={{0,1},{1,4},{2,3},{3,6},{4,5},{5,8},{6,7},{7,10},{8,9},{9,12},{10,... | collective-permute-start | bytes 786440 | tf_op jit(solution)/shard_map/ppermute | solution.py:297
  8.8 1.9 %collective-permute-start.3 = (bf16[128,1024]{1,0:T(8,128)(2,1)}, bf16[128,1024]{1,0:T(8,128)(2,1)S(1)}, u32[]{:S(2)}, u32[]{:S(2)}) collective-permute-start(bf16[128,1024]{1,0:T(8,128)(2,1)} %refs_3_.1), channel_id=1, source_target_pairs={{0,1},{1,4},{2,3},{3,6},{4,5},{5,8},{6,7},{7,10},{8,9},{9,12},{10,... | collective-permute-start | bytes 786440 | tf_op jit(solution)/shard_map/ppermute | solution.py:303
  10.8 3.9 %collective-permute-start.4 = (bf16[128,1024]{1,0:T(8,128)(2,1)}, bf16[128,1024]{1,0:T(8,128)(2,1)S(1)}, u32[]{:S(2)}, u32[]{:S(2)}) collective-permute-start(bf16[128,1024]{1,0:T(8,128)(2,1)} %refs_3_.1), channel_id=1, source_target_pairs={{0,2},{1,3},{2,4},{3,5},{4,6},{5,7},{6,8},{7,9},{8,10},{9,11},{10,... | collective-permute-start | bytes 786440 | tf_op jit(solution)/shard_map/ppermute | solution.py:304
  14.6 3.9 %stacked.1 = (bf16[8,128,1024]{2,1,0:T(8,128)(2,1)S(1)}, bf16[8,128,1024]{2,1,0:T(8,128)(2,1)S(1)}, bf16[128,8192]{1,0:T(8,128)(2,1)S(1)}, bf16[128,8192]{1,0:T(...) custom-call(s32[128,128]{1,0:T(8,128)} %bitcast.2, ...), custom_call_target="tpu_custom_call" | custom-call | tf_op jit(solution)/shard_map/stacked/pallas_call | solution.py:189
  18.6 0.0 collective-permute-done.1.refs_1_
  18.6 0.0 collective-permute-done.refs_0_
  18.6 0.9 %collective-permute-start.2 = (bf16[128,1024]{1,0:T(8,128)(2,1)S(1)}, bf16[128,1024]{1,0:T(8,128)(2,1)S(1)}, u32[]{:S(2)}, u32[]{:S(2)}) collective-permute-start(bf16[128,1024]{1,0:T(8,128)(2,1)S(1)} %collective-permute-done.1.refs_1_), channel_id=1, source_target_pairs={{0,1},{1,0},{2,3},{3,2},{4,5},{5,4},{6,7},{7,6},{8,9},{9,8},{10,11... | collective-permute-start | bytes 786440 | tf_op jit(solution)/shard_map/ppermute | solution.py:305
  19.5 0.0 copy-start
  19.5 1.1 %collective-permute-done.2.refs_2_ = bf16[128,1024]{1,0:T(8,128)(2,1)S(1)} collective-permute-done((bf16[128,1024]{1,0:T(8,128)(2,1)S(1)}, bf16[128,1024]{1,0:T(8,128)(2,1)S(1)}, u32[]{:S(2)}, u32[]{:S(2)}) %collective-permute-start.2) | collective-permute-done | bytes 262176 | tf_op jit(solution)/shard_map/ppermute | solution.py:305
  20.6 8.0 %probs_and_dv.1 = (bf16[8,512,1024]{2,1,0:T(8,128)(2,1)S(1)}, bf16[128,1024]{1,0:T(8,128)(2,1)S(1)}, f32[128,1024]{1,0:T(8,128)S(1)}, bf16[128,1024]{1,0:T(8,128)(2,1)S(1)}, f32[128,1024]{1,0:T(8,128)S(1)}) custom-call(f32[8,1024]{1,0:T(8,128)S(1)} %get-tuple-element.42.size_ref, bf16[8,128,1024]{2,1,0:T(8,128)(2,1)S(1)} %get-tuple-element.43.qt_ref, ...), custom_call_target="tpu_custom_call" | custom-call | flops 2147483648 | bytes 16777216 | tf_op jit(solution)/shard_map/probs_and_dv/pallas_call | solution.py:210
  28.6 0.4 collective-permute-start.10
  29.0 0.0 collective-permute-done.3.refs_0_
  29.1 0.0 collective-permute-done.4.refs_1_
  29.1 0.1 collective-permute-start.5
  29.2 2.3 %collective-permute-start.9 = (bf16[128,1024]{1,0:T(8,128)(2,1)S(1)}, bf16[128,1024]{1,0:T(8,128)(2,1)S(1)}, u32[]{:S(2)}, u32[]{:S(2)}) collective-permute-start(bf16[128,1024]{1,0:T(8,128)(2,1)S(1)} %get-tuple-element.63), channel_id=1, source_target_pairs={{1,0},{4,1},{3,2},{6,3},{5,4},{8,5},{7,6},{10,7},{9,8},{12,9},{11,... | collective-permute-start | bytes 786440 | tf_op jit(solution)/shard_map/ppermute | solution.py:318
  31.5 0.0 collective-permute-done.10
  31.5 0.1 add_convert_fusion.1
  31.5 1.9 %collective-permute-start.11 = (bf16[128,1024]{1,0:T(8,128)(2,1)S(1)}, bf16[128,1024]{1,0:T(8,128)(2,1)S(1)}, u32[]{:S(2)}, u32[]{:S(2)}) collective-permute-start(bf16[128,1024]{1,0:T(8,128)(2,1)S(1)} %add_convert_fusion.1), channel_id=1, source_target_pairs={{2,0},{3,1},{4,2},{5,3},{6,4},{7,5},{8,6},{9,7},{10,8},{11,9},{12,... | collective-permute-start | bytes 786440 | tf_op jit(solution)/shard_map/ppermute | solution.py:317
  33.5 0.0 collective-permute-done.5.refs_2_
  33.5 7.6 %dscores_and_dk.1 = (bf16[8,512,1024]{2,1,0:T(8,128)(2,1)S(1)}, bf16[128,1024]{1,0:T(8,128)(2,1)S(1)}, f32[128,1024]{1,0:T(8,128)S(1)}, bf16[128,1024]{1,0:T(8,128)(2,1)S(1)}, f32[128,1024]{1,0:T(8,128)S(1)}) custom-call(f32[8,128]{1,0:T(8,128)S(1)} %mark.1.mark_ref, ...), custom_call_target="tpu_custom_call", output_to_operand_aliasing={{0}: (3, {})} | custom-call | flops 3221225472 | bytes 16777216 | tf_op jit(solution)/shard_map/dscores_and_dk/pallas_call | solution.py:223
  41.1 0.1 collective-permute-start.6
  41.2 1.4 %dq.2.refs_4_ = bf16[128,8192]{1,0:T(8,128)(2,1)} custom-call(bf16[8,512,1024]{2,1,0:T(8,128)(2,1)S(1)} %get-tuple-element.54.dscores_ref, bf16[128,1024]{1,0:T(8,128)(2,1)S(1)} %collective-permute-done.refs_0_, bf16[128,1024]{1,0:T(8,128)(2,1)S(1)} %collective-permute-done.1.refs_1_, bf16[128,1024]{1,0:T(8,128)(2,1)S(1)} %collective-permute-done.2.refs_2_, ...), custom_call_target="tpu_custom_call" | custom-call | flops 99999997952 | bytes 100000000 | tf_op jit(solution)/shard_map/dq/pallas_call | solution.py:237
  42.6 0.2 collective-permute-done.6
  42.8 0.1 add_convert_fusion.3
  42.8 5.5 %collective-permute-start.8 = (bf16[128,1024]{1,0:T(8,128)(2,1)S(1)}, bf16[128,1024]{1,0:T(8,128)(2,1)S(1)}, u32[]{:S(2)}, u32[]{:S(2)}) collective-permute-start(bf16[128,1024]{1,0:T(8,128)(2,1)S(1)} %add_convert_fusion.3), channel_id=1, source_target_pairs={{2,0},{3,1},{4,2},{5,3},{6,4},{7,5},{8,6},{9,7},{10,8},{11,9},{12,... | collective-permute-start | bytes 786440 | tf_op jit(solution)/shard_map/ppermute | solution.py:332
  48.3 2.4 %collective-permute-start.7 = (bf16[128,1024]{1,0:T(8,128)(2,1)S(1)}, bf16[128,1024]{1,0:T(8,128)(2,1)S(1)}, u32[]{:S(2)}, u32[]{:S(2)}) collective-permute-start(bf16[128,1024]{1,0:T(8,128)(2,1)S(1)} %get-tuple-element.61), channel_id=1, source_target_pairs={{1,0},{4,1},{3,2},{6,3},{5,4},{8,5},{7,6},{10,7},{9,8},{12,9},{11,... | collective-permute-start | bytes 786440 | tf_op jit(solution)/shard_map/ppermute | solution.py:334
  50.7 2.8 %dq.3 = bf16[128,8192]{1,0:T(8,128)(2,1)} custom-call(bf16[8,512,1024]{2,1,0:T(8,128)(2,1)S(1)} %get-tuple-element.54.dscores_ref, bf16[128,1024]{1,0:T(8,128)(2,1)S(1)} %collective-permute-done.refs_0_, bf16[128,1024]{1,0:T(8,128)(2,1)S(1)} %collective-permute-done.1.refs_1_, ...), custom_call_target="tpu_custom_call", output_to_operand_aliasing={{}: (5, {})} | custom-call | flops 1073741824 | bytes 16777216 | tf_op jit(solution)/shard_map/dq/pallas_call | solution.py:237
  53.5 0.0 collective-permute-done.9
  53.5 0.8 %add_convert_fusion = bf16[128,1024]{1,0:T(8,128)(2,1)} fusion(bf16[128,1024]{1,0:T(8,128)(2,1)S(1)} %collective-permute-done.11, f32[128,1024]{1,0:T(8,128)S(1)} %get-tuple-element.62, bf16[128,1024]{1,0:T(8,128)(2,1)S(1)} %collective-permute-done.9), kind=kLoop, calls=%fused_computation | loop fusion | flops 655360 | bytes 1310720 | tf_op jit(solution)/shard_map/convert_element_type | solution.py:337
  54.3 6.5 %collective-permute-done.7 = bf16[128,1024]{1,0:T(8,128)(2,1)S(1)} collective-permute-done((bf16[128,1024]{1,0:T(8,128)(2,1)S(1)}, bf16[128,1024]{1,0:T(8,128)(2,1)S(1)}, u32[]{:S(2)}, u32[]{:S(2)}) %collective-permute-start.7) | collective-permute-done | bytes 262176 | tf_op jit(solution)/shard_map/ppermute | solution.py:334
  60.8 0.8 %add_convert_fusion.2 = bf16[128,1024]{1,0:T(8,128)(2,1)} fusion(bf16[128,1024]{1,0:T(8,128)(2,1)S(1)} %collective-permute-done.8, f32[128,1024]{1,0:T(8,128)S(1)} %get-tuple-element.57, bf16[128,1024]{1,0:T(8,128)(2,1)S(1)} %collective-permute-done.7), kind=kLoop, calls=%fused_computation.2 | loop fusion | flops 655360 | bytes 1310720 | tf_op jit(solution)/shard_map/convert_element_type | solution.py:336
  (5 shorter events, 0.0 us)
Async XLA Ops:
  0.6 17.9 %collective-permute-start.1 = (bf16[128,1024]{1,0:T(8,128)(2,1)}, bf16[128,1024]{1,0:T(8,128)(2,1)S(1)}, u32[]{:S(2)}, u32[]{:S(2)}) collective-permute-start(bf16[128,1024]{1,0:T(8,128)(2,1)} %keys_hbm.1), channel_id=1, source_target_pairs={{0,2},{1,3},{2,4},{3,5},{4,6},{5,7},{6,8},{7,9},{8,10},{9,11},{10,... | collective-permute-start | bytes 786440 | tf_op jit(solution)/shard_map/ppermute | solution.py:298
  3.1 15.5 %collective-permute-start = (bf16[128,1024]{1,0:T(8,128)(2,1)}, bf16[128,1024]{1,0:T(8,128)(2,1)S(1)}, u32[]{:S(2)}, u32[]{:S(2)}) collective-permute-start(bf16[128,1024]{1,0:T(8,128)(2,1)} %keys_hbm.1), channel_id=1, source_target_pairs={{0,1},{1,4},{2,3},{3,6},{4,5},{5,8},{6,7},{7,10},{8,9},{9,12},{10,... | collective-permute-start | bytes 786440 | tf_op jit(solution)/shard_map/ppermute | solution.py:297
  8.8 20.2 %collective-permute-start.3 = (bf16[128,1024]{1,0:T(8,128)(2,1)}, bf16[128,1024]{1,0:T(8,128)(2,1)S(1)}, u32[]{:S(2)}, u32[]{:S(2)}) collective-permute-start(bf16[128,1024]{1,0:T(8,128)(2,1)} %refs_3_.1), channel_id=1, source_target_pairs={{0,1},{1,4},{2,3},{3,6},{4,5},{5,8},{6,7},{7,10},{8,9},{9,12},{10,... | collective-permute-start | bytes 786440 | tf_op jit(solution)/shard_map/ppermute | solution.py:303
  10.8 18.3 %collective-permute-start.4 = (bf16[128,1024]{1,0:T(8,128)(2,1)}, bf16[128,1024]{1,0:T(8,128)(2,1)S(1)}, u32[]{:S(2)}, u32[]{:S(2)}) collective-permute-start(bf16[128,1024]{1,0:T(8,128)(2,1)} %refs_3_.1), channel_id=1, source_target_pairs={{0,2},{1,3},{2,4},{3,5},{4,6},{5,7},{6,8},{7,9},{8,10},{9,11},{10,... | collective-permute-start | bytes 786440 | tf_op jit(solution)/shard_map/ppermute | solution.py:304
  18.6 2.0 %collective-permute-start.2 = (bf16[128,1024]{1,0:T(8,128)(2,1)S(1)}, bf16[128,1024]{1,0:T(8,128)(2,1)S(1)}, u32[]{:S(2)}, u32[]{:S(2)}) collective-permute-start(bf16[128,1024]{1,0:T(8,128)(2,1)S(1)} %collective-permute-done.1.refs_1_), channel_id=1, source_target_pairs={{0,1},{1,0},{2,3},{3,2},{4,5},{5,4},{6,7},{7,6},{8,9},{9,8},{10,11... | collective-permute-start | bytes 786440 | tf_op jit(solution)/shard_map/ppermute | solution.py:305
  19.5 14.0 %copy-start = (bf16[128,1024]{1,0:T(8,128)(2,1)S(1)}, bf16[128,1024]{1,0:T(8,128)(2,1)}, u32[]{:S(2)}) copy-start(bf16[128,1024]{1,0:T(8,128)(2,1)} %refs_3_.1) | copy-start | bytes 786436
  28.6 2.9 %collective-permute-start.10 = (bf16[128,1024]{1,0:T(8,128)(2,1)S(1)}, bf16[128,1024]{1,0:T(8,128)(2,1)S(1)}, u32[]{:S(2)}, u32[]{:S(2)}) collective-permute-start(bf16[128,1024]{1,0:T(8,128)(2,1)S(1)} %get-tuple-element.50), channel_id=1, source_target_pairs={{0,1},{1,0},{2,3},{3,2},{4,5},{5,4},{6,7},{7,6},{8,9},{9,8},{10,11... | collective-permute-start | bytes 786440 | tf_op jit(solution)/shard_map/ppermute | solution.py:316
  29.1 4.4 %collective-permute-start.5 = (bf16[128,1024]{1,0:T(8,128)(2,1)S(1)}, bf16[128,1024]{1,0:T(8,128)(2,1)S(1)}, u32[]{:S(2)}, u32[]{:S(2)}) collective-permute-start(bf16[128,1024]{1,0:T(8,128)(2,1)S(1)} %collective-permute-done.4.refs_1_), channel_id=1, source_target_pairs={{0,1},{1,0},{2,3},{3,2},{4,5},{5,4},{6,7},{7,6},{8,9},{9,8},{10,11... | collective-permute-start | bytes 786440 | tf_op jit(solution)/shard_map/ppermute | solution.py:315
  29.2 24.3 %collective-permute-start.9 = (bf16[128,1024]{1,0:T(8,128)(2,1)S(1)}, bf16[128,1024]{1,0:T(8,128)(2,1)S(1)}, u32[]{:S(2)}, u32[]{:S(2)}) collective-permute-start(bf16[128,1024]{1,0:T(8,128)(2,1)S(1)} %get-tuple-element.63), channel_id=1, source_target_pairs={{1,0},{4,1},{3,2},{6,3},{5,4},{8,5},{7,6},{10,7},{9,8},{12,9},{11,... | collective-permute-start | bytes 786440 | tf_op jit(solution)/shard_map/ppermute | solution.py:318
  31.5 21.9 %collective-permute-start.11 = (bf16[128,1024]{1,0:T(8,128)(2,1)S(1)}, bf16[128,1024]{1,0:T(8,128)(2,1)S(1)}, u32[]{:S(2)}, u32[]{:S(2)}) collective-permute-start(bf16[128,1024]{1,0:T(8,128)(2,1)S(1)} %add_convert_fusion.1), channel_id=1, source_target_pairs={{2,0},{3,1},{4,2},{5,3},{6,4},{7,5},{8,6},{9,7},{10,8},{11,9},{12,... | collective-permute-start | bytes 786440 | tf_op jit(solution)/shard_map/ppermute | solution.py:317
  41.1 1.6 %collective-permute-start.6 = (bf16[128,1024]{1,0:T(8,128)(2,1)S(1)}, bf16[128,1024]{1,0:T(8,128)(2,1)S(1)}, u32[]{:S(2)}, u32[]{:S(2)}) collective-permute-start(bf16[128,1024]{1,0:T(8,128)(2,1)S(1)} %get-tuple-element.55), channel_id=1, source_target_pairs={{0,1},{1,0},{2,3},{3,2},{4,5},{5,4},{6,7},{7,6},{8,9},{9,8},{10,11... | collective-permute-start | bytes 786440 | tf_op jit(solution)/shard_map/ppermute | solution.py:328
  42.8 18.0 %collective-permute-start.8 = (bf16[128,1024]{1,0:T(8,128)(2,1)S(1)}, bf16[128,1024]{1,0:T(8,128)(2,1)S(1)}, u32[]{:S(2)}, u32[]{:S(2)}) collective-permute-start(bf16[128,1024]{1,0:T(8,128)(2,1)S(1)} %add_convert_fusion.3), channel_id=1, source_target_pairs={{2,0},{3,1},{4,2},{5,3},{6,4},{7,5},{8,6},{9,7},{10,8},{11,9},{12,... | collective-permute-start | bytes 786440 | tf_op jit(solution)/shard_map/ppermute | solution.py:332
  48.3 12.5 %collective-permute-start.7 = (bf16[128,1024]{1,0:T(8,128)(2,1)S(1)}, bf16[128,1024]{1,0:T(8,128)(2,1)S(1)}, u32[]{:S(2)}, u32[]{:S(2)}) collective-permute-start(bf16[128,1024]{1,0:T(8,128)(2,1)S(1)} %get-tuple-element.61), channel_id=1, source_target_pairs={{1,0},{4,1},{3,2},{6,3},{5,4},{8,5},{7,6},{10,7},{9,8},{12,9},{11,... | collective-permute-start | bytes 786440 | tf_op jit(solution)/shard_map/ppermute | solution.py:334

commit v5 on v4

--- a/solution.py
+++ b/solution.py
@@ -19,6 +19,7 @@
 KEY_MOST = 6.0
 NT = (((1,), (1,)), ((), ()))
 GROUPS = 2
+PROBS_GROUPS = 4
 MIB = 2**20
 VMEM = pl.BlockSpec(memory_space=pltpu.VMEM)
 
@@ -93,7 +94,7 @@
     identity = jnp.where((column & (ROWS - 1)) == row, 1.0, 0.0).astype(jnp.bfloat16)
 
     def step(i, shift):
-        groups = [i * GROUPS + j for j in range(GROUPS)]
+        groups = [i * PROBS_GROUPS + j for j in range(PROBS_GROUPS)]
         scores = [
             jnp.dot(
                 jnp.concatenate([stacked_blocks(key_refs, g), bias], axis=1),
@@ -117,7 +118,7 @@
             step(i, shift)
             return carry
 
-        lax.fori_loop(0, KVH // GROUPS, body, 0)
+        lax.fori_loop(0, KVH // PROBS_GROUPS, body, 0)
 
     small = jnp.max(size_ref[0:1]) * (KEY_MOST * SCALE_LOG2) <= 115.0
     pl.when(small)(lambda: run(False))
@@ -213,7 +214,7 @@
         out_specs=[VMEM] * 5,
         out_shape=[bf16(KVH, SPAN, STACK)] + block_shapes(),
         name="probs_and_dv",
-        compiler_params=limit(10),
+        compiler_params=limit(16),
         cost_estimate=cost(2, PAIRS),
     )(size, qt, bias, grad_out, *keys)
     return out[0], out[1:]
@@ -233,20 +234,18 @@
     return out[0], out[1:]
 
 
-def dq_of(dscores, keys, shape, first, count, earlier=()):
+def dq_of(dscores, keys, shape):
     return pl.pallas_call(
         queries_kernel,
-        grid=(count,),
-        in_specs=[pl.BlockSpec((GROUPS, SPAN, STACK), lambda s: (s + first, 0, 0))]
-        + [pl.BlockSpec((ROWS, GROUPS * HD), lambda s: (0, s + first))] * 4
-        + [pl.BlockSpec(memory_space=pl.ANY)] * len(earlier),
-        out_specs=pl.BlockSpec((ROWS, GROUPS * G * HD), lambda s: (0, s + first)),
+        grid=(KVH // GROUPS,),
+        in_specs=[pl.BlockSpec((GROUPS, SPAN, STACK), lambda s: (s, 0, 0))]
+        + [pl.BlockSpec((ROWS, GROUPS * HD), lambda s: (0, s))] * 4,
+        out_specs=pl.BlockSpec((ROWS, GROUPS * G * HD), lambda s: (0, s)),
         out_shape=bf16(*shape),
-        input_output_aliases={5: 0} if earlier else {},
         name="dq",
         compiler_params=limit(24),
-        cost_estimate=cost(1) if earlier else AHEAD,
-    )(dscores, *keys, *earlier)
+        cost_estimate=cost(1),
+    )(dscores, *keys)
 
 
 def mark_kernel(docs_hbm, mark_ref):
@@ -275,7 +274,7 @@
         out_specs=VMEM,
         out_shape=pltpu.VMEM(x.shape, x.dtype),
         name="held",
-        compiler_params=limit(1),
+        compiler_params=limit(2),
         cost_estimate=AHEAD,
     )(x)
 
@@ -326,13 +325,12 @@
     dk_aside, dk_middle, dk_paired, dk_own = dk_blocks
 
     dk_other = lax.ppermute(dk_paired, AXES, swap)
-    first_dq = dq_of(dscores, key_blocks, queries.shape, 0, 1)
-    dk_other, first_dq = lax.optimization_barrier((dk_other, first_dq))
+    dk_other, dk_own = lax.optimization_barrier((dk_other, held(dk_own)))
     dk_sum = (dk_middle + dk_other).astype(jnp.bfloat16)
     dk_far = lax.ppermute(dk_sum, AXES, unskip)
     dk_sum, dk_aside = lax.optimization_barrier((dk_sum, dk_aside))
     dk_near = lax.ppermute(dk_aside, AXES, back)
-    grad_queries = dq_of(dscores, key_blocks, queries.shape, 1, KVH // GROUPS - 1, [first_dq])
+    grad_queries = dq_of(dscores, key_blocks, queries.shape)
     grad_keys = (dk_own + dk_near + dk_far).astype(jnp.bfloat16)
     grad_values = (dv_own + dv_near + dv_far).astype(jnp.bfloat16)
     return grad_queries, grad_keys, grad_values

time: 62.4 us -> 62.1 us (level)
  Pallas kernels: 23.7 us -> 22.9 us
    ppermute x1, waiting for transfers between devices: 0.15 us -> 1.48 us  [per_device(): dk_other = lax.ppermute(dk_paired, AXES, swap)]
    ppermute x1, waiting for transfers between devices: 6.53 us -> 5.72 us  [per_device(): dk_near = lax.ppermute(dk_aside, AXES, back)]
    pallas_call x2 -> x1, Pallas kernels: 4.16 us -> 3.39 us  [dq_of(): pl.pallas_call(queries_kernel, grid=(KVH // GROUPS,), in_specs=[pl.BlockS...]
  transfers between devices with their start and end apart: 12 -> 12, of which waited for: 3 -> 3; matrix products, arithmetic and copies ran while one was open for 1% -> 2% of each run, Pallas kernels for 39% -> 37%
where the time goes in v5:
time: 62.1 us; the launch traced here: 61.3 us
  starting transfers between devices  27.5 us (44%)
  Pallas kernels  22.9 us (37%)
  waiting for transfers between devices  8.36 us (13%)
  other arithmetic  1.73 us (3%)
  between operations  0.8 us (1%)
    pallas_call x1, Pallas kernels, probs_and_dv(): pl.pallas_call(probs_kernel, in_specs=[VMEM] * 8, out_specs=[VMEM] * 5, o...  7.86 us
    pallas_call x1, Pallas kernels, dscores_and_dk(): pl.pallas_call(scores_kernel, in_specs=[VMEM] * 8, out_specs=[VMEM] * 5,...  7.64 us
    ppermute x1, starting transfers between devices, per_device(): key_aside = lax.ppermute(keys, AXES, ahead)  5.74 us
    ppermute x1, waiting for transfers between devices, per_device(): dk_near = lax.ppermute(dk_aside, AXES, back)  5.72 us
    ppermute x1, starting transfers between devices, per_device(): dk_far = lax.ppermute(dk_sum, AXES, unskip)  5.3 us
    pallas_call x1, Pallas kernels, stacked(): pl.pallas_call(stack_kernel, in_specs=[HBM, HBM, HBM, HBM], out_specs=[VM...  3.95 us
    ppermute x1, starting transfers between devices, per_device(): value_middle = lax.ppermute(late_values, AXES, skip)  3.86 us
    pallas_call x1, Pallas kernels, dq_of(): pl.pallas_call(queries_kernel, grid=(KVH // GROUPS,), in_specs=[pl.BlockS...  3.39 us
  transfers between devices with their start and end apart: 12, of which 3 were waited for; matrix products, arithmetic and copies ran while one was open for 2% of the time, Pallas kernels for 37%

profile of v5, /device:TPU:121, one launch (start us, length us, event | category | flops | bytes accessed | tf_op | source)
XLA Modules:
  0.0 61.3 jit_solution(15585833269556840363)
XLA Ops:
  0.6 2.4 %collective-permute-start.1 = (bf16[128,1024]{1,0:T(8,128)(2,1)}, bf16[128,1024]{1,0:T(8,128)(2,1)S(1)}, u32[]{:S(2)}, u32[]{:S(2)}) collective-permute-start(bf16[128,1024]{1,0:T(8,128)(2,1)} %keys_hbm.1), channel_id=1, source_target_pairs={{0,2},{1,3},{2,4},{3,5},{4,6},{5,7},{6,8},{7,9},{8,10},{9,11},{10,... | collective-permute-start | bytes 786440 | tf_op jit(solution)/shard_map/ppermute | solution.py:297
  3.1 5.7 %collective-permute-start = (bf16[128,1024]{1,0:T(8,128)(2,1)}, bf16[128,1024]{1,0:T(8,128)(2,1)S(1)}, u32[]{:S(2)}, u32[]{:S(2)}) collective-permute-start(bf16[128,1024]{1,0:T(8,128)(2,1)} %keys_hbm.1), channel_id=1, source_target_pairs={{0,1},{1,4},{2,3},{3,6},{4,5},{5,8},{6,7},{7,10},{8,9},{9,12},{10,... | collective-permute-start | bytes 786440 | tf_op jit(solution)/shard_map/ppermute | solution.py:296
  8.8 1.9 %collective-permute-start.3 = (bf16[128,1024]{1,0:T(8,128)(2,1)}, bf16[128,1024]{1,0:T(8,128)(2,1)S(1)}, u32[]{:S(2)}, u32[]{:S(2)}) collective-permute-start(bf16[128,1024]{1,0:T(8,128)(2,1)} %refs_3_.1), channel_id=1, source_target_pairs={{0,1},{1,4},{2,3},{3,6},{4,5},{5,8},{6,7},{7,10},{8,9},{9,12},{10,... | collective-permute-start | bytes 786440 | tf_op jit(solution)/shard_map/ppermute | solution.py:302
  10.8 3.9 %collective-permute-start.4 = (bf16[128,1024]{1,0:T(8,128)(2,1)}, bf16[128,1024]{1,0:T(8,128)(2,1)S(1)}, u32[]{:S(2)}, u32[]{:S(2)}) collective-permute-start(bf16[128,1024]{1,0:T(8,128)(2,1)} %refs_3_.1), channel_id=1, source_target_pairs={{0,2},{1,3},{2,4},{3,5},{4,6},{5,7},{6,8},{7,9},{8,10},{9,11},{10,... | collective-permute-start | bytes 786440 | tf_op jit(solution)/shard_map/ppermute | solution.py:303
  14.6 3.9 %stacked.1 = (bf16[8,128,1024]{2,1,0:T(8,128)(2,1)S(1)}, bf16[8,128,1024]{2,1,0:T(8,128)(2,1)S(1)}, bf16[128,8192]{1,0:T(8,128)(2,1)S(1)}, bf16[128,8192]{1,0:T(...) custom-call(s32[128,128]{1,0:T(8,128)} %bitcast.2, ...), custom_call_target="tpu_custom_call" | custom-call | tf_op jit(solution)/shard_map/stacked/pallas_call | solution.py:190
  18.6 0.0 collective-permute-done.1.refs_1_
  18.6 0.0 collective-permute-done.refs_0_
  18.6 0.9 %collective-permute-start.2 = (bf16[128,1024]{1,0:T(8,128)(2,1)S(1)}, bf16[128,1024]{1,0:T(8,128)(2,1)S(1)}, u32[]{:S(2)}, u32[]{:S(2)}) collective-permute-start(bf16[128,1024]{1,0:T(8,128)(2,1)S(1)} %collective-permute-done.1.refs_1_), channel_id=1, source_target_pairs={{0,1},{1,0},{2,3},{3,2},{4,5},{5,4},{6,7},{7,6},{8,9},{9,8},{10,11... | collective-permute-start | bytes 786440 | tf_op jit(solution)/shard_map/ppermute | solution.py:304
  19.5 0.0 copy-start
  19.5 1.1 %collective-permute-done.2.refs_2_ = bf16[128,1024]{1,0:T(8,128)(2,1)S(1)} collective-permute-done((bf16[128,1024]{1,0:T(8,128)(2,1)S(1)}, bf16[128,1024]{1,0:T(8,128)(2,1)S(1)}, u32[]{:S(2)}, u32[]{:S(2)}) %collective-permute-start.2) | collective-permute-done | bytes 262176 | tf_op jit(solution)/shard_map/ppermute | solution.py:304
  20.6 7.9 %probs_and_dv.1 = (bf16[8,512,1024]{2,1,0:T(8,128)(2,1)S(1)}, bf16[128,1024]{1,0:T(8,128)(2,1)S(1)}, f32[128,1024]{1,0:T(8,128)S(1)}, bf16[128,1024]{1,0:T(8,128)(2,1)S(1)}, f32[128,1024]{1,0:T(8,128)S(1)}) custom-call(f32[8,1024]{1,0:T(8,128)S(1)} %get-tuple-element.42.size_ref, bf16[8,128,1024]{2,1,0:T(8,128)(2,1)S(1)} %get-tuple-element.43.qt_ref, ...), custom_call_target="tpu_custom_call" | custom-call | flops 2147483648 | bytes 16777216 | tf_op jit(solution)/shard_map/probs_and_dv/pallas_call | solution.py:211
  28.5 0.4 collective-permute-start.10
  28.9 0.0 collective-permute-done.3.refs_0_
  28.9 0.0 collective-permute-done.4.refs_1_
  28.9 0.2 collective-permute-start.5
  29.1 2.2 %collective-permute-start.9 = (bf16[128,1024]{1,0:T(8,128)(2,1)S(1)}, bf16[128,1024]{1,0:T(8,128)(2,1)S(1)}, u32[]{:S(2)}, u32[]{:S(2)}) collective-permute-start(bf16[128,1024]{1,0:T(8,128)(2,1)S(1)} %get-tuple-element.63), channel_id=1, source_target_pairs={{1,0},{4,1},{3,2},{6,3},{5,4},{8,5},{7,6},{10,7},{9,8},{12,9},{11,... | collective-permute-start | bytes 786440 | tf_op jit(solution)/shard_map/ppermute | solution.py:317
  31.3 0.1 add_convert_fusion.1
  31.4 1.9 %collective-permute-start.11 = (bf16[128,1024]{1,0:T(8,128)(2,1)S(1)}, bf16[128,1024]{1,0:T(8,128)(2,1)S(1)}, u32[]{:S(2)}, u32[]{:S(2)}) collective-permute-start(bf16[128,1024]{1,0:T(8,128)(2,1)S(1)} %add_convert_fusion.1), channel_id=1, source_target_pairs={{2,0},{3,1},{4,2},{5,3},{6,4},{7,5},{8,6},{9,7},{10,8},{11,9},{12,... | collective-permute-start | bytes 786440 | tf_op jit(solution)/shard_map/ppermute | solution.py:316
  33.4 0.0 collective-permute-done.5.refs_2_
  33.4 7.6 %dscores_and_dk.1 = (bf16[8,512,1024]{2,1,0:T(8,128)(2,1)S(1)}, bf16[128,1024]{1,0:T(8,128)(2,1)S(1)}, f32[128,1024]{1,0:T(8,128)S(1)}, bf16[128,1024]{1,0:T(8,128)(2,1)S(1)}, f32[128,1024]{1,0:T(8,128)S(1)}) custom-call(f32[8,128]{1,0:T(8,128)S(1)} %mark.1.mark_ref, ...), custom_call_target="tpu_custom_call", output_to_operand_aliasing={{0}: (3, {})} | custom-call | flops 3221225472 | bytes 16777216 | tf_op jit(solution)/shard_map/dscores_and_dk/pallas_call | solution.py:224
  41.0 0.1 collective-permute-start.6
  41.2 1.5 %collective-permute-done.6 = bf16[128,1024]{1,0:T(8,128)(2,1)S(1)} collective-permute-done((bf16[128,1024]{1,0:T(8,128)(2,1)S(1)}, bf16[128,1024]{1,0:T(8,128)(2,1)S(1)}, u32[]{:S(2)}, u32[]{:S(2)}) %collective-permute-start.6) | collective-permute-done | bytes 262176 | tf_op jit(solution)/shard_map/ppermute | solution.py:327
  42.6 0.1 add_convert_fusion.3
  42.7 5.3 %collective-permute-start.8 = (bf16[128,1024]{1,0:T(8,128)(2,1)S(1)}, bf16[128,1024]{1,0:T(8,128)(2,1)S(1)}, u32[]{:S(2)}, u32[]{:S(2)}) collective-permute-start(bf16[128,1024]{1,0:T(8,128)(2,1)S(1)} %add_convert_fusion.3), channel_id=1, source_target_pairs={{2,0},{3,1},{4,2},{5,3},{6,4},{7,5},{8,6},{9,7},{10,8},{11,9},{12,... | collective-permute-start | bytes 786440 | tf_op jit(solution)/shard_map/ppermute | solution.py:330
  48.0 2.6 %collective-permute-start.7 = (bf16[128,1024]{1,0:T(8,128)(2,1)S(1)}, bf16[128,1024]{1,0:T(8,128)(2,1)S(1)}, u32[]{:S(2)}, u32[]{:S(2)}) collective-permute-start(bf16[128,1024]{1,0:T(8,128)(2,1)S(1)} %get-tuple-element.61), channel_id=1, source_target_pairs={{1,0},{4,1},{3,2},{6,3},{5,4},{8,5},{7,6},{10,7},{9,8},{12,9},{11,... | collective-permute-start | bytes 786440 | tf_op jit(solution)/shard_map/ppermute | solution.py:332
  50.6 3.4 %dq.1 = bf16[128,8192]{1,0:T(8,128)(2,1)} custom-call(bf16[8,512,1024]{2,1,0:T(8,128)(2,1)S(1)} %get-tuple-element.54.dscores_ref, bf16[128,1024]{1,0:T(8,128)(2,1)S(1)} %collective-permute-done.refs_0_, bf16[128,1024]{1,0:T(8,128)(2,1)S(1)} %collective-permute-done.1.refs_1_, bf16[128,1024]{1,0:T(8,128)(2,1)S(1)} %collective-permute-done.2.refs_2_, ...), custom_call_target="tpu_custom_call" | custom-call | flops 1073741824 | bytes 16777216 | tf_op jit(solution)/shard_map/dq/pallas_call | solution.py:238
  54.0 0.0 collective-permute-done.9
  54.0 0.0 collective-permute-done.11
  54.0 0.8 %add_convert_fusion = bf16[128,1024]{1,0:T(8,128)(2,1)} fusion(bf16[128,1024]{1,0:T(8,128)(2,1)S(1)} %collective-permute-done.11, f32[128,1024]{1,0:T(8,128)S(1)} %get-tuple-element.62, bf16[128,1024]{1,0:T(8,128)(2,1)S(1)} %collective-permute-done.9), kind=kLoop, calls=%fused_computation | loop fusion | flops 655360 | bytes 1310720 | tf_op jit(solution)/shard_map/convert_element_type | solution.py:335
  54.8 5.7 %collective-permute-done.7 = bf16[128,1024]{1,0:T(8,128)(2,1)S(1)} collective-permute-done((bf16[128,1024]{1,0:T(8,128)(2,1)S(1)}, bf16[128,1024]{1,0:T(8,128)(2,1)S(1)}, u32[]{:S(2)}, u32[]{:S(2)}) %collective-permute-start.7) | collective-permute-done | bytes 262176 | tf_op jit(solution)/shard_map/ppermute | solution.py:332
  60.5 0.0 collective-permute-done.8
  60.5 0.8 %add_convert_fusion.2 = bf16[128,1024]{1,0:T(8,128)(2,1)} fusion(bf16[128,1024]{1,0:T(8,128)(2,1)S(1)} %collective-permute-done.8, f32[128,1024]{1,0:T(8,128)S(1)} %held.3, bf16[128,1024]{1,0:T(8,128)(2,1)S(1)} %collective-permute-done.7), kind=kLoop, calls=%fused_computation.2 | loop fusion | flops 655360 | bytes 1310720 | tf_op jit(solution)/shard_map/convert_element_type | solution.py:334
  (5 shorter events, 0.1 us)
Async XLA Ops:
  0.6 18.0 %collective-permute-start.1 = (bf16[128,1024]{1,0:T(8,128)(2,1)}, bf16[128,1024]{1,0:T(8,128)(2,1)S(1)}, u32[]{:S(2)}, u32[]{:S(2)}) collective-permute-start(bf16[128,1024]{1,0:T(8,128)(2,1)} %keys_hbm.1), channel_id=1, source_target_pairs={{0,2},{1,3},{2,4},{3,5},{4,6},{5,7},{6,8},{7,9},{8,10},{9,11},{10,... | collective-permute-start | bytes 786440 | tf_op jit(solution)/shard_map/ppermute | solution.py:297
  3.1 15.5 %collective-permute-start = (bf16[128,1024]{1,0:T(8,128)(2,1)}, bf16[128,1024]{1,0:T(8,128)(2,1)S(1)}, u32[]{:S(2)}, u32[]{:S(2)}) collective-permute-start(bf16[128,1024]{1,0:T(8,128)(2,1)} %keys_hbm.1), channel_id=1, source_target_pairs={{0,1},{1,4},{2,3},{3,6},{4,5},{5,8},{6,7},{7,10},{8,9},{9,12},{10,... | collective-permute-start | bytes 786440 | tf_op jit(solution)/shard_map/ppermute | solution.py:296
  8.8 20.1 %collective-permute-start.3 = (bf16[128,1024]{1,0:T(8,128)(2,1)}, bf16[128,1024]{1,0:T(8,128)(2,1)S(1)}, u32[]{:S(2)}, u32[]{:S(2)}) collective-permute-start(bf16[128,1024]{1,0:T(8,128)(2,1)} %refs_3_.1), channel_id=1, source_target_pairs={{0,1},{1,4},{2,3},{3,6},{4,5},{5,8},{6,7},{7,10},{8,9},{9,12},{10,... | collective-permute-start | bytes 786440 | tf_op jit(solution)/shard_map/ppermute | solution.py:302
  10.8 18.2 %collective-permute-start.4 = (bf16[128,1024]{1,0:T(8,128)(2,1)}, bf16[128,1024]{1,0:T(8,128)(2,1)S(1)}, u32[]{:S(2)}, u32[]{:S(2)}) collective-permute-start(bf16[128,1024]{1,0:T(8,128)(2,1)} %refs_3_.1), channel_id=1, source_target_pairs={{0,2},{1,3},{2,4},{3,5},{4,6},{5,7},{6,8},{7,9},{8,10},{9,11},{10,... | collective-permute-start | bytes 786440 | tf_op jit(solution)/shard_map/ppermute | solution.py:303
  18.6 2.0 %collective-permute-start.2 = (bf16[128,1024]{1,0:T(8,128)(2,1)S(1)}, bf16[128,1024]{1,0:T(8,128)(2,1)S(1)}, u32[]{:S(2)}, u32[]{:S(2)}) collective-permute-start(bf16[128,1024]{1,0:T(8,128)(2,1)S(1)} %collective-permute-done.1.refs_1_), channel_id=1, source_target_pairs={{0,1},{1,0},{2,3},{3,2},{4,5},{5,4},{6,7},{7,6},{8,9},{9,8},{10,11... | collective-permute-start | bytes 786440 | tf_op jit(solution)/shard_map/ppermute | solution.py:304
  19.5 13.9 %copy-start = (bf16[128,1024]{1,0:T(8,128)(2,1)S(1)}, bf16[128,1024]{1,0:T(8,128)(2,1)}, u32[]{:S(2)}) copy-start(bf16[128,1024]{1,0:T(8,128)(2,1)} %refs_3_.1) | copy-start | bytes 786436
  28.5 2.9 %collective-permute-start.10 = (bf16[128,1024]{1,0:T(8,128)(2,1)S(1)}, bf16[128,1024]{1,0:T(8,128)(2,1)S(1)}, u32[]{:S(2)}, u32[]{:S(2)}) collective-permute-start(bf16[128,1024]{1,0:T(8,128)(2,1)S(1)} %get-tuple-element.50), channel_id=1, source_target_pairs={{0,1},{1,0},{2,3},{3,2},{4,5},{5,4},{6,7},{7,6},{8,9},{9,8},{10,11... | collective-permute-start | bytes 786440 | tf_op jit(solution)/shard_map/ppermute | solution.py:315
  28.9 4.4 %collective-permute-start.5 = (bf16[128,1024]{1,0:T(8,128)(2,1)S(1)}, bf16[128,1024]{1,0:T(8,128)(2,1)S(1)}, u32[]{:S(2)}, u32[]{:S(2)}) collective-permute-start(bf16[128,1024]{1,0:T(8,128)(2,1)S(1)} %collective-permute-done.4.refs_1_), channel_id=1, source_target_pairs={{0,1},{1,0},{2,3},{3,2},{4,5},{5,4},{6,7},{7,6},{8,9},{9,8},{10,11... | collective-permute-start | bytes 786440 | tf_op jit(solution)/shard_map/ppermute | solution.py:314
  29.1 24.9 %collective-permute-start.9 = (bf16[128,1024]{1,0:T(8,128)(2,1)S(1)}, bf16[128,1024]{1,0:T(8,128)(2,1)S(1)}, u32[]{:S(2)}, u32[]{:S(2)}) collective-permute-start(bf16[128,1024]{1,0:T(8,128)(2,1)S(1)} %get-tuple-element.63), channel_id=1, source_target_pairs={{1,0},{4,1},{3,2},{6,3},{5,4},{8,5},{7,6},{10,7},{9,8},{12,9},{11,... | collective-permute-start | bytes 786440 | tf_op jit(solution)/shard_map/ppermute | solution.py:317
  31.4 22.5 %collective-permute-start.11 = (bf16[128,1024]{1,0:T(8,128)(2,1)S(1)}, bf16[128,1024]{1,0:T(8,128)(2,1)S(1)}, u32[]{:S(2)}, u32[]{:S(2)}) collective-permute-start(bf16[128,1024]{1,0:T(8,128)(2,1)S(1)} %add_convert_fusion.1), channel_id=1, source_target_pairs={{2,0},{3,1},{4,2},{5,3},{6,4},{7,5},{8,6},{9,7},{10,8},{11,9},{12,... | collective-permute-start | bytes 786440 | tf_op jit(solution)/shard_map/ppermute | solution.py:316
  41.0 1.6 %collective-permute-start.6 = (bf16[128,1024]{1,0:T(8,128)(2,1)S(1)}, bf16[128,1024]{1,0:T(8,128)(2,1)S(1)}, u32[]{:S(2)}, u32[]{:S(2)}) collective-permute-start(bf16[128,1024]{1,0:T(8,128)(2,1)S(1)} %get-tuple-element.55), channel_id=1, source_target_pairs={{0,1},{1,0},{2,3},{3,2},{4,5},{5,4},{6,7},{7,6},{8,9},{9,8},{10,11... | collective-permute-start | bytes 786440 | tf_op jit(solution)/shard_map/ppermute | solution.py:327
  42.7 17.8 %collective-permute-start.8 = (bf16[128,1024]{1,0:T(8,128)(2,1)S(1)}, bf16[128,1024]{1,0:T(8,128)(2,1)S(1)}, u32[]{:S(2)}, u32[]{:S(2)}) collective-permute-start(bf16[128,1024]{1,0:T(8,128)(2,1)S(1)} %add_convert_fusion.3), channel_id=1, source_target_pairs={{2,0},{3,1},{4,2},{5,3},{6,4},{7,5},{8,6},{9,7},{10,8},{11,9},{12,... | collective-permute-start | bytes 786440 | tf_op jit(solution)/shard_map/ppermute | solution.py:330
  48.0 12.5 %collective-permute-start.7 = (bf16[128,1024]{1,0:T(8,128)(2,1)S(1)}, bf16[128,1024]{1,0:T(8,128)(2,1)S(1)}, u32[]{:S(2)}, u32[]{:S(2)}) collective-permute-start(bf16[128,1024]{1,0:T(8,128)(2,1)S(1)} %get-tuple-element.61), channel_id=1, source_target_pairs={{1,0},{4,1},{3,2},{6,3},{5,4},{8,5},{7,6},{10,7},{9,8},{12,9},{11,... | collective-permute-start | bytes 786440 | tf_op jit(solution)/shard_map/ppermute | solution.py:332

commit v6 on v5

--- a/solution.py
+++ b/solution.py
@@ -135,6 +135,8 @@
             out = jnp.dot(values.T, probs_ref[g], preferred_element_type=jnp.float32)
             out = out.astype(jnp.bfloat16).astype(jnp.float32)
             deltas.append(jnp.sum(out * dot_ref[g].astype(jnp.float32), axis=0, keepdims=True))
+        for g in groups:
+            values = stacked_blocks(value_refs, g)
             dprobs.append(jnp.dot(values, dot_ref[g], preferred_element_type=jnp.float32))
         for g, delta, dprob in zip(groups, deltas, dprobs):
             dscores = (probs_ref[g].astype(jnp.float32) * (dprob - delta)).astype(jnp.bfloat16)

time: 62.1 us -> 61.6 us (level)
  no operation moved by 1% of the time
where the time goes in v6:
time: 61.6 us; the launch traced here: 60.8 us
  starting transfers between devices  27.5 us (45%)
  Pallas kernels  22.4 us (36%)
  waiting for transfers between devices  8.36 us (14%)
  other arithmetic  1.73 us (3%)
  between operations  0.8 us (1%)
    pallas_call x1, Pallas kernels, probs_and_dv(): pl.pallas_call(probs_kernel, in_specs=[VMEM] * 8, out_specs=[VMEM] * 5, o...  7.86 us
    pallas_call x1, Pallas kernels, dscores_and_dk(): pl.pallas_call(scores_kernel, in_specs=[VMEM] * 8, out_specs=[VMEM] * 5,...  7.18 us
    ppermute x1, starting transfers between devices, per_device(): key_aside = lax.ppermute(keys, AXES, ahead)  5.74 us
    ppermute x1, waiting for transfers between devices, per_device(): dk_near = lax.ppermute(dk_aside, AXES, back)  5.72 us
    ppermute x1, starting transfers between devices, per_device(): dk_far = lax.ppermute(dk_sum, AXES, unskip)  5.3 us
    pallas_call x1, Pallas kernels, stacked(): pl.pallas_call(stack_kernel, in_specs=[HBM, HBM, HBM, HBM], out_specs=[VM...  3.95 us
    ppermute x1, starting transfers between devices, per_device(): value_middle = lax.ppermute(late_values, AXES, skip)  3.86 us
    pallas_call x1, Pallas kernels, dq_of(): pl.pallas_call(queries_kernel, grid=(KVH // GROUPS,), in_specs=[pl.BlockS...  3.39 us
  transfers between devices with their start and end apart: 12, of which 3 were waited for; matrix products, arithmetic and copies ran while one was open for 2% of the time, Pallas kernels for 37%

profile of v6, /device:TPU:121, one launch (start us, length us, event | category | flops | bytes accessed | tf_op | source)
XLA Modules:
  0.0 60.8 jit_solution(2231990901995719671)
XLA Ops:
  0.6 2.4 %collective-permute-start.1 = (bf16[128,1024]{1,0:T(8,128)(2,1)}, bf16[128,1024]{1,0:T(8,128)(2,1)S(1)}, u32[]{:S(2)}, u32[]{:S(2)}) collective-permute-start(bf16[128,1024]{1,0:T(8,128)(2,1)} %keys_hbm.1), channel_id=1, source_target_pairs={{0,2},{1,3},{2,4},{3,5},{4,6},{5,7},{6,8},{7,9},{8,10},{9,11},{10,... | collective-permute-start | bytes 786440 | tf_op jit(solution)/shard_map/ppermute | solution.py:299
  3.1 5.7 %collective-permute-start = (bf16[128,1024]{1,0:T(8,128)(2,1)}, bf16[128,1024]{1,0:T(8,128)(2,1)S(1)}, u32[]{:S(2)}, u32[]{:S(2)}) collective-permute-start(bf16[128,1024]{1,0:T(8,128)(2,1)} %keys_hbm.1), channel_id=1, source_target_pairs={{0,1},{1,4},{2,3},{3,6},{4,5},{5,8},{6,7},{7,10},{8,9},{9,12},{10,... | collective-permute-start | bytes 786440 | tf_op jit(solution)/shard_map/ppermute | solution.py:298
  8.8 1.9 %collective-permute-start.3 = (bf16[128,1024]{1,0:T(8,128)(2,1)}, bf16[128,1024]{1,0:T(8,128)(2,1)S(1)}, u32[]{:S(2)}, u32[]{:S(2)}) collective-permute-start(bf16[128,1024]{1,0:T(8,128)(2,1)} %refs_3_.1), channel_id=1, source_target_pairs={{0,1},{1,4},{2,3},{3,6},{4,5},{5,8},{6,7},{7,10},{8,9},{9,12},{10,... | collective-permute-start | bytes 786440 | tf_op jit(solution)/shard_map/ppermute | solution.py:304
  10.8 3.9 %collective-permute-start.4 = (bf16[128,1024]{1,0:T(8,128)(2,1)}, bf16[128,1024]{1,0:T(8,128)(2,1)S(1)}, u32[]{:S(2)}, u32[]{:S(2)}) collective-permute-start(bf16[128,1024]{1,0:T(8,128)(2,1)} %refs_3_.1), channel_id=1, source_target_pairs={{0,2},{1,3},{2,4},{3,5},{4,6},{5,7},{6,8},{7,9},{8,10},{9,11},{10,... | collective-permute-start | bytes 786440 | tf_op jit(solution)/shard_map/ppermute | solution.py:305
  14.6 3.9 %stacked.1 = (bf16[8,128,1024]{2,1,0:T(8,128)(2,1)S(1)}, bf16[8,128,1024]{2,1,0:T(8,128)(2,1)S(1)}, bf16[128,8192]{1,0:T(8,128)(2,1)S(1)}, bf16[128,8192]{1,0:T(...) custom-call(s32[128,128]{1,0:T(8,128)} %bitcast.2, ...), custom_call_target="tpu_custom_call" | custom-call | tf_op jit(solution)/shard_map/stacked/pallas_call | solution.py:192
  18.6 0.0 collective-permute-done.1.refs_1_
  18.6 0.0 collective-permute-done.refs_0_
  18.6 0.9 %collective-permute-start.2 = (bf16[128,1024]{1,0:T(8,128)(2,1)S(1)}, bf16[128,1024]{1,0:T(8,128)(2,1)S(1)}, u32[]{:S(2)}, u32[]{:S(2)}) collective-permute-start(bf16[128,1024]{1,0:T(8,128)(2,1)S(1)} %collective-permute-done.1.refs_1_), channel_id=1, source_target_pairs={{0,1},{1,0},{2,3},{3,2},{4,5},{5,4},{6,7},{7,6},{8,9},{9,8},{10,11... | collective-permute-start | bytes 786440 | tf_op jit(solution)/shard_map/ppermute | solution.py:306
  19.5 0.0 copy-start
  19.5 1.1 %collective-permute-done.2.refs_2_ = bf16[128,1024]{1,0:T(8,128)(2,1)S(1)} collective-permute-done((bf16[128,1024]{1,0:T(8,128)(2,1)S(1)}, bf16[128,1024]{1,0:T(8,128)(2,1)S(1)}, u32[]{:S(2)}, u32[]{:S(2)}) %collective-permute-start.2) | collective-permute-done | bytes 262176 | tf_op jit(solution)/shard_map/ppermute | solution.py:306
  20.6 7.9 %probs_and_dv.1 = (bf16[8,512,1024]{2,1,0:T(8,128)(2,1)S(1)}, bf16[128,1024]{1,0:T(8,128)(2,1)S(1)}, f32[128,1024]{1,0:T(8,128)S(1)}, bf16[128,1024]{1,0:T(8,128)(2,1)S(1)}, f32[128,1024]{1,0:T(8,128)S(1)}) custom-call(f32[8,1024]{1,0:T(8,128)S(1)} %get-tuple-element.42.size_ref, bf16[8,128,1024]{2,1,0:T(8,128)(2,1)S(1)} %get-tuple-element.43.qt_ref, ...), custom_call_target="tpu_custom_call" | custom-call | flops 2147483648 | bytes 16777216 | tf_op jit(solution)/shard_map/probs_and_dv/pallas_call | solution.py:213
  28.5 0.4 collective-permute-start.10
  28.9 0.0 collective-permute-done.3.refs_0_
  28.9 0.0 collective-permute-done.4.refs_1_
  28.9 0.2 collective-permute-start.5
  29.1 2.2 %collective-permute-start.9 = (bf16[128,1024]{1,0:T(8,128)(2,1)S(1)}, bf16[128,1024]{1,0:T(8,128)(2,1)S(1)}, u32[]{:S(2)}, u32[]{:S(2)}) collective-permute-start(bf16[128,1024]{1,0:T(8,128)(2,1)S(1)} %get-tuple-element.63), channel_id=1, source_target_pairs={{1,0},{4,1},{3,2},{6,3},{5,4},{8,5},{7,6},{10,7},{9,8},{12,9},{11,... | collective-permute-start | bytes 786440 | tf_op jit(solution)/shard_map/ppermute | solution.py:319
  31.3 0.0 collective-permute-done.10
  31.3 0.1 add_convert_fusion.1
  31.4 1.9 %collective-permute-start.11 = (bf16[128,1024]{1,0:T(8,128)(2,1)S(1)}, bf16[128,1024]{1,0:T(8,128)(2,1)S(1)}, u32[]{:S(2)}, u32[]{:S(2)}) collective-permute-start(bf16[128,1024]{1,0:T(8,128)(2,1)S(1)} %add_convert_fusion.1), channel_id=1, source_target_pairs={{2,0},{3,1},{4,2},{5,3},{6,4},{7,5},{8,6},{9,7},{10,8},{11,9},{12,... | collective-permute-start | bytes 786440 | tf_op jit(solution)/shard_map/ppermute | solution.py:318
  33.4 0.0 collective-permute-done.5.refs_2_
  33.4 7.2 %dscores_and_dk.1 = (bf16[8,512,1024]{2,1,0:T(8,128)(2,1)S(1)}, bf16[128,1024]{1,0:T(8,128)(2,1)S(1)}, f32[128,1024]{1,0:T(8,128)S(1)}, bf16[128,1024]{1,0:T(8,128)(2,1)S(1)}, f32[128,1024]{1,0:T(8,128)S(1)}) custom-call(f32[8,128]{1,0:T(8,128)S(1)} %mark.1.mark_ref, ...), custom_call_target="tpu_custom_call", output_to_operand_aliasing={{0}: (3, {})} | custom-call | flops 3221225472 | bytes 16777216 | tf_op jit(solution)/shard_map/dscores_and_dk/pallas_call | solution.py:226
  40.6 0.1 collective-permute-start.6
  40.7 1.5 %collective-permute-done.6 = bf16[128,1024]{1,0:T(8,128)(2,1)S(1)} collective-permute-done((bf16[128,1024]{1,0:T(8,128)(2,1)S(1)}, bf16[128,1024]{1,0:T(8,128)(2,1)S(1)}, u32[]{:S(2)}, u32[]{:S(2)}) %collective-permute-start.6) | collective-permute-done | bytes 262176 | tf_op jit(solution)/shard_map/ppermute | solution.py:329
  42.2 0.1 add_convert_fusion.3
  42.2 5.3 %collective-permute-start.8 = (bf16[128,1024]{1,0:T(8,128)(2,1)S(1)}, bf16[128,1024]{1,0:T(8,128)(2,1)S(1)}, u32[]{:S(2)}, u32[]{:S(2)}) collective-permute-start(bf16[128,1024]{1,0:T(8,128)(2,1)S(1)} %add_convert_fusion.3), channel_id=1, source_target_pairs={{2,0},{3,1},{4,2},{5,3},{6,4},{7,5},{8,6},{9,7},{10,8},{11,9},{12,... | collective-permute-start | bytes 786440 | tf_op jit(solution)/shard_map/ppermute | solution.py:332
  47.5 2.6 %collective-permute-start.7 = (bf16[128,1024]{1,0:T(8,128)(2,1)S(1)}, bf16[128,1024]{1,0:T(8,128)(2,1)S(1)}, u32[]{:S(2)}, u32[]{:S(2)}) collective-permute-start(bf16[128,1024]{1,0:T(8,128)(2,1)S(1)} %get-tuple-element.61), channel_id=1, source_target_pairs={{1,0},{4,1},{3,2},{6,3},{5,4},{8,5},{7,6},{10,7},{9,8},{12,9},{11,... | collective-permute-start | bytes 786440 | tf_op jit(solution)/shard_map/ppermute | solution.py:334
  50.1 3.4 %dq.1 = bf16[128,8192]{1,0:T(8,128)(2,1)} custom-call(bf16[8,512,1024]{2,1,0:T(8,128)(2,1)S(1)} %get-tuple-element.54.dscores_ref, bf16[128,1024]{1,0:T(8,128)(2,1)S(1)} %collective-permute-done.refs_0_, bf16[128,1024]{1,0:T(8,128)(2,1)S(1)} %collective-permute-done.1.refs_1_, bf16[128,1024]{1,0:T(8,128)(2,1)S(1)} %collective-permute-done.2.refs_2_, ...), custom_call_target="tpu_custom_call" | custom-call | flops 1073741824 | bytes 16777216 | tf_op jit(solution)/shard_map/dq/pallas_call | solution.py:240
  53.5 0.0 collective-permute-done.9
  53.5 0.0 collective-permute-done.11
  53.5 0.8 %add_convert_fusion = bf16[128,1024]{1,0:T(8,128)(2,1)} fusion(bf16[128,1024]{1,0:T(8,128)(2,1)S(1)} %collective-permute-done.11, f32[128,1024]{1,0:T(8,128)S(1)} %get-tuple-element.62, bf16[128,1024]{1,0:T(8,128)(2,1)S(1)} %collective-permute-done.9), kind=kLoop, calls=%fused_computation | loop fusion | flops 655360 | bytes 1310720 | tf_op jit(solution)/shard_map/convert_element_type | solution.py:337
  54.3 5.7 %collective-permute-done.7 = bf16[128,1024]{1,0:T(8,128)(2,1)S(1)} collective-permute-done((bf16[128,1024]{1,0:T(8,128)(2,1)S(1)}, bf16[128,1024]{1,0:T(8,128)(2,1)S(1)}, u32[]{:S(2)}, u32[]{:S(2)}) %collective-permute-start.7) | collective-permute-done | bytes 262176 | tf_op jit(solution)/shard_map/ppermute | solution.py:334
  60.0 0.8 %add_convert_fusion.2 = bf16[128,1024]{1,0:T(8,128)(2,1)} fusion(bf16[128,1024]{1,0:T(8,128)(2,1)S(1)} %collective-permute-done.8, f32[128,1024]{1,0:T(8,128)S(1)} %held.3, bf16[128,1024]{1,0:T(8,128)(2,1)S(1)} %collective-permute-done.7), kind=kLoop, calls=%fused_computation.2 | loop fusion | flops 655360 | bytes 1310720 | tf_op jit(solution)/shard_map/convert_element_type | solution.py:336
  (5 shorter events, 0.1 us)
Async XLA Ops:
  0.6 18.0 %collective-permute-start.1 = (bf16[128,1024]{1,0:T(8,128)(2,1)}, bf16[128,1024]{1,0:T(8,128)(2,1)S(1)}, u32[]{:S(2)}, u32[]{:S(2)}) collective-permute-start(bf16[128,1024]{1,0:T(8,128)(2,1)} %keys_hbm.1), channel_id=1, source_target_pairs={{0,2},{1,3},{2,4},{3,5},{4,6},{5,7},{6,8},{7,9},{8,10},{9,11},{10,... | collective-permute-start | bytes 786440 | tf_op jit(solution)/shard_map/ppermute | solution.py:299
  3.1 15.5 %collective-permute-start = (bf16[128,1024]{1,0:T(8,128)(2,1)}, bf16[128,1024]{1,0:T(8,128)(2,1)S(1)}, u32[]{:S(2)}, u32[]{:S(2)}) collective-permute-start(bf16[128,1024]{1,0:T(8,128)(2,1)} %keys_hbm.1), channel_id=1, source_target_pairs={{0,1},{1,4},{2,3},{3,6},{4,5},{5,8},{6,7},{7,10},{8,9},{9,12},{10,... | collective-permute-start | bytes 786440 | tf_op jit(solution)/shard_map/ppermute | solution.py:298
  8.8 20.1 %collective-permute-start.3 = (bf16[128,1024]{1,0:T(8,128)(2,1)}, bf16[128,1024]{1,0:T(8,128)(2,1)S(1)}, u32[]{:S(2)}, u32[]{:S(2)}) collective-permute-start(bf16[128,1024]{1,0:T(8,128)(2,1)} %refs_3_.1), channel_id=1, source_target_pairs={{0,1},{1,4},{2,3},{3,6},{4,5},{5,8},{6,7},{7,10},{8,9},{9,12},{10,... | collective-permute-start | bytes 786440 | tf_op jit(solution)/shard_map/ppermute | solution.py:304
  10.8 18.2 %collective-permute-start.4 = (bf16[128,1024]{1,0:T(8,128)(2,1)}, bf16[128,1024]{1,0:T(8,128)(2,1)S(1)}, u32[]{:S(2)}, u32[]{:S(2)}) collective-permute-start(bf16[128,1024]{1,0:T(8,128)(2,1)} %refs_3_.1), channel_id=1, source_target_pairs={{0,2},{1,3},{2,4},{3,5},{4,6},{5,7},{6,8},{7,9},{8,10},{9,11},{10,... | collective-permute-start | bytes 786440 | tf_op jit(solution)/shard_map/ppermute | solution.py:305
  18.6 2.0 %collective-permute-start.2 = (bf16[128,1024]{1,0:T(8,128)(2,1)S(1)}, bf16[128,1024]{1,0:T(8,128)(2,1)S(1)}, u32[]{:S(2)}, u32[]{:S(2)}) collective-permute-start(bf16[128,1024]{1,0:T(8,128)(2,1)S(1)} %collective-permute-done.1.refs_1_), channel_id=1, source_target_pairs={{0,1},{1,0},{2,3},{3,2},{4,5},{5,4},{6,7},{7,6},{8,9},{9,8},{10,11... | collective-permute-start | bytes 786440 | tf_op jit(solution)/shard_map/ppermute | solution.py:306
  19.5 13.9 %copy-start = (bf16[128,1024]{1,0:T(8,128)(2,1)S(1)}, bf16[128,1024]{1,0:T(8,128)(2,1)}, u32[]{:S(2)}) copy-start(bf16[128,1024]{1,0:T(8,128)(2,1)} %refs_3_.1) | copy-start | bytes 786436
  28.5 2.9 %collective-permute-start.10 = (bf16[128,1024]{1,0:T(8,128)(2,1)S(1)}, bf16[128,1024]{1,0:T(8,128)(2,1)S(1)}, u32[]{:S(2)}, u32[]{:S(2)}) collective-permute-start(bf16[128,1024]{1,0:T(8,128)(2,1)S(1)} %get-tuple-element.50), channel_id=1, source_target_pairs={{0,1},{1,0},{2,3},{3,2},{4,5},{5,4},{6,7},{7,6},{8,9},{9,8},{10,11... | collective-permute-start | bytes 786440 | tf_op jit(solution)/shard_map/ppermute | solution.py:317
  28.9 4.4 %collective-permute-start.5 = (bf16[128,1024]{1,0:T(8,128)(2,1)S(1)}, bf16[128,1024]{1,0:T(8,128)(2,1)S(1)}, u32[]{:S(2)}, u32[]{:S(2)}) collective-permute-start(bf16[128,1024]{1,0:T(8,128)(2,1)S(1)} %collective-permute-done.4.refs_1_), channel_id=1, source_target_pairs={{0,1},{1,0},{2,3},{3,2},{4,5},{5,4},{6,7},{7,6},{8,9},{9,8},{10,11... | collective-permute-start | bytes 786440 | tf_op jit(solution)/shard_map/ppermute | solution.py:316
  29.1 24.4 %collective-permute-start.9 = (bf16[128,1024]{1,0:T(8,128)(2,1)S(1)}, bf16[128,1024]{1,0:T(8,128)(2,1)S(1)}, u32[]{:S(2)}, u32[]{:S(2)}) collective-permute-start(bf16[128,1024]{1,0:T(8,128)(2,1)S(1)} %get-tuple-element.63), channel_id=1, source_target_pairs={{1,0},{4,1},{3,2},{6,3},{5,4},{8,5},{7,6},{10,7},{9,8},{12,9},{11,... | collective-permute-start | bytes 786440 | tf_op jit(solution)/shard_map/ppermute | solution.py:319
  31.4 22.1 %collective-permute-start.11 = (bf16[128,1024]{1,0:T(8,128)(2,1)S(1)}, bf16[128,1024]{1,0:T(8,128)(2,1)S(1)}, u32[]{:S(2)}, u32[]{:S(2)}) collective-permute-start(bf16[128,1024]{1,0:T(8,128)(2,1)S(1)} %add_convert_fusion.1), channel_id=1, source_target_pairs={{2,0},{3,1},{4,2},{5,3},{6,4},{7,5},{8,6},{9,7},{10,8},{11,9},{12,... | collective-permute-start | bytes 786440 | tf_op jit(solution)/shard_map/ppermute | solution.py:318
  40.6 1.6 %collective-permute-start.6 = (bf16[128,1024]{1,0:T(8,128)(2,1)S(1)}, bf16[128,1024]{1,0:T(8,128)(2,1)S(1)}, u32[]{:S(2)}, u32[]{:S(2)}) collective-permute-start(bf16[128,1024]{1,0:T(8,128)(2,1)S(1)} %get-tuple-element.55), channel_id=1, source_target_pairs={{0,1},{1,0},{2,3},{3,2},{4,5},{5,4},{6,7},{7,6},{8,9},{9,8},{10,11... | collective-permute-start | bytes 786440 | tf_op jit(solution)/shard_map/ppermute | solution.py:329
  42.2 17.8 %collective-permute-start.8 = (bf16[128,1024]{1,0:T(8,128)(2,1)S(1)}, bf16[128,1024]{1,0:T(8,128)(2,1)S(1)}, u32[]{:S(2)}, u32[]{:S(2)}) collective-permute-start(bf16[128,1024]{1,0:T(8,128)(2,1)S(1)} %add_convert_fusion.3), channel_id=1, source_target_pairs={{2,0},{3,1},{4,2},{5,3},{6,4},{7,5},{8,6},{9,7},{10,8},{11,9},{12,... | collective-permute-start | bytes 786440 | tf_op jit(solution)/shard_map/ppermute | solution.py:332
  47.5 12.5 %collective-permute-start.7 = (bf16[128,1024]{1,0:T(8,128)(2,1)S(1)}, bf16[128,1024]{1,0:T(8,128)(2,1)S(1)}, u32[]{:S(2)}, u32[]{:S(2)}) collective-permute-start(bf16[128,1024]{1,0:T(8,128)(2,1)S(1)} %get-tuple-element.61), channel_id=1, source_target_pairs={{1,0},{4,1},{3,2},{6,3},{5,4},{8,5},{7,6},{10,7},{9,8},{12,9},{11,... | collective-permute-start | bytes 786440 | tf_op jit(solution)/shard_map/ppermute | solution.py:334
